TPU v7x, 32 devices: a whole 2x2x4 slice. The times are simulated.
32 devices in a mesh: replica: 4 (over y, x), shard: 8 (over z, core).
Axes of the slice: x: 2, y: 2, z: 4, core: 2. Of those that a mesh axis runs over, the one named last changes fastest.
Arguments:
- tokens: bfloat16 [4096, 1600], P(('replica', 'shard')), may hold values from -6 to 6
- offsets: int32 [4, 8, 1], replicated, may hold values from 0 to 896, as said below
- qkv_weight: bfloat16 [1600, 4800], P('shard'), may hold values from -0.15625 to 0.15625
- out_weight: bfloat16 [1600, 1600], P('shard'), may hold values from -0.625 to 0.625
- fc_weight: bfloat16 [1600, 6400], P('shard'), may hold values from -0.15625 to 0.15625
- proj_weight: bfloat16 [6400, 1600], P('shard'), may hold values from -0.078125 to 0.078125
- query_bias: bfloat16 [1600], P('shard'), may hold values from -3 to 3
- value_bias: bfloat16 [1600], P('shard'), may hold values from -3 to 3
- out_bias: bfloat16 [1600], P('shard'), may hold values from -3 to 3
- fc_bias: bfloat16 [6400], P('shard'), may hold values from -3 to 3
- proj_bias: bfloat16 [1600], P('shard'), may hold values from -3 to 3
- gain_first: bfloat16 [1600], P('shard'), may hold values from 0.25 to 1.75
- shift_first: bfloat16 [1600], P('shard'), may hold values from -2 to 2
- gain_second: bfloat16 [1600], P('shard'), may hold values from 0.25 to 1.75
- shift_second: bfloat16 [1600], P('shard'), may hold values from -2 to 2
- cotangent: bfloat16 [4096, 1600], P(('replica', 'shard')), may hold values from -6 to 6
Outputs:
- output: bfloat16 [4096, 1600], P(('replica', 'shard'))
- tokens_grad: bfloat16 [4096, 1600], P(('replica', 'shard'))
- qkv_grad: float32 [1600, 4800], P('shard')
- outw_grad: float32 [1600, 1600], P('shard')
- fc_grad: float32 [1600, 6400], P('shard')
- proj_grad: float32 [6400, 1600], P('shard')
- qbias_grad: float32 [1600], P('shard')
- vbias_grad: float32 [1600], P('shard')
- obias_grad: float32 [1600], P('shard')
- fbias_grad: float32 [6400], P('shard')
- pbias_grad: float32 [1600], P('shard')
- gfirst_grad: float32 [1600], P('shard')
- sfirst_grad: float32 [1600], P('shard')
- gsecond_grad: float32 [1600], P('shard')
- ssecond_grad: float32 [1600], P('shard')
Inputs may be any that keep to these rules, and one draw needn't show every extreme that they name: For every group and every sequence s, offsets[g, 0:8, s] are 0, 128, ..., 896 in some order, so the group's blocks cover the sequence once.
All inputs are finite; a program needn't handle non-finite values.
Results may differ from a plain program's by a relative error of at most 0.018.
Values may be sent and summed in bfloat16 or wider, within the bound.
No kernel may reach another device: no remote copies, remote signals or barrier semaphores. Data moves between devices by JAX's collectives and lax.ppermute only.
A program may use at most 320 MiB of HBM per device.

v0:
```python
import jax
import jax.numpy as jnp
from jax import lax
from jax.sharding import PartitionSpec as P

D = 1600
H = 25
HD = 64
CP = 8
STRETCH = 128
SEQ_GRP = 1


norm_eps = 1e-05
masked_score = -1e30
gelu_coeff = 0.7978845608028654


def swapped(block, axis, apart):
    count = lax.axis_size(axis)
    route = []
    for low in range(count):
        high = low | 1 << apart
        if high != low and high < count:
            route += [(low, high), (high, low)]
    return lax.ppermute(block, axis, route)


def layer_norm(values, gain_vec, shift_vec):
    average = jnp.mean(values, axis=-1, keepdims=True)
    centred = values - average
    variance = jnp.mean(centred * centred, axis=-1, keepdims=True)
    return centred * lax.rsqrt(variance + norm_eps) * gain_vec + shift_vec


def gelu_tanh(values):
    return (
        0.5 * values * (1.0 + jnp.tanh(gelu_coeff * (values + 0.044715 * values * values * values)))
    )


def matmul_rows(left_side, right_side):
    return lax.dot_general(
        left_side, right_side, (((0,), (0,)), ((), ())), preferred_element_type=jnp.float32
    )


def matmul_back(left_side, right_side):
    return lax.dot_general(
        left_side, right_side, (((1,), (1,)), ((), ())), preferred_element_type=jnp.float32
    )


def score_block(queries, keys_all, q_places, k_places):
    scores = jnp.einsum(
        "qhd,khd->hqk", queries, keys_all, preferred_element_type=jnp.float32
    ) * HD ** (-0.5)
    allowed = k_places[None, :] <= q_places[:, None]
    return jnp.where(allowed[None], scores, masked_score)


def attend_forward(inputs):
    queries, keys_all, values_all, q_places, k_places = inputs
    scores = score_block(queries, keys_all, q_places, k_places)
    highest = jnp.max(scores, axis=-1, keepdims=True)
    weights = jnp.exp(scores - highest)
    totals = jnp.sum(weights, axis=-1, keepdims=True)
    probabilities = (weights / totals).astype(jnp.bfloat16)
    attended = jnp.einsum(
        "hqk,khd->qhd", probabilities, values_all, preferred_element_type=jnp.float32
    )
    return (attended, highest + jnp.log(totals))


def attend_backward(inputs):
    queries, keys_all, values_all, q_places, k_places, log_total, attended_grad = inputs
    scores = score_block(queries, keys_all, q_places, k_places)
    probabilities = jnp.exp(scores - log_total)
    value_grads = jnp.einsum(
        "hqk,qhd->khd",
        probabilities.astype(jnp.bfloat16),
        attended_grad,
        preferred_element_type=jnp.float32,
    )
    prob_grads = jnp.einsum(
        "qhd,khd->hqk", attended_grad, values_all, preferred_element_type=jnp.float32
    )
    row_dot = jnp.sum(probabilities * prob_grads, axis=-1, keepdims=True)
    score_grads = (probabilities * (prob_grads - row_dot)).astype(jnp.bfloat16)
    score_scale = HD ** (-0.5)
    query_grads = (
        jnp.einsum("hqk,khd->qhd", score_grads, keys_all, preferred_element_type=jnp.float32)
        * score_scale
    )
    key_grads = (
        jnp.einsum("hqk,qhd->khd", score_grads, queries, preferred_element_type=jnp.float32)
        * score_scale
    )
    return (query_grads, key_grads, value_grads)


def on_device(
    tokens,
    offsets,
    qkv_weight,
    out_weight,
    fc_weight,
    proj_weight,
    query_bias,
    value_bias,
    out_bias,
    fc_bias,
    proj_bias,
    gain_first,
    shift_first,
    gain_second,
    shift_second,
    cotangent,
):
    gathered = (
        lax.all_gather(qkv_weight, "shard", axis=0, tiled=True),
        lax.all_gather(out_weight, "shard", axis=0, tiled=True),
        lax.all_gather(fc_weight, "shard", axis=0, tiled=True),
        lax.all_gather(proj_weight, "shard", axis=0, tiled=True),
        lax.all_gather(query_bias, "shard", axis=0, tiled=True),
        lax.all_gather(value_bias, "shard", axis=0, tiled=True),
        lax.all_gather(out_bias, "shard", axis=0, tiled=True),
        lax.all_gather(fc_bias, "shard", axis=0, tiled=True),
        lax.all_gather(proj_bias, "shard", axis=0, tiled=True),
        lax.all_gather(gain_first, "shard", axis=0, tiled=True),
        lax.all_gather(shift_first, "shard", axis=0, tiled=True),
        lax.all_gather(gain_second, "shard", axis=0, tiled=True),
        lax.all_gather(shift_second, "shard", axis=0, tiled=True),
    )
    (
        w_qkv,
        w_out,
        w_fc,
        w_proj,
        b_query,
        b_value,
        b_out,
        b_fc,
        b_proj,
        g_first,
        s_first,
        g_second,
        s_second,
    ) = gathered
    tok_rows = tokens.shape[0]
    shard_place = lax.axis_index("shard")
    group_place = shard_place % CP
    group_index = lax.axis_index("replica") * (lax.axis_size("shard") // CP) + shard_place // CP
    group_offsets = lax.dynamic_index_in_dim(offsets, group_index, 0, keepdims=False)
    step_range = jnp.arange(STRETCH, dtype=jnp.int32)
    k_places = (group_offsets.T[:, :, None] + step_range[None, None, :]).reshape(
        SEQ_GRP, CP * STRETCH
    )
    q_places = (
        lax.dynamic_index_in_dim(group_offsets, group_place, 0, keepdims=False)[:, None]
        + step_range[None, :]
    )
    in_rows = tokens.astype(jnp.float32)
    normed_one, pull_first = jax.vjp(
        layer_norm, in_rows, g_first.astype(jnp.float32), s_first.astype(jnp.float32)
    )
    normed_low = normed_one.astype(jnp.bfloat16)
    projected = jnp.dot(normed_low, w_qkv, preferred_element_type=jnp.float32)
    queries = (projected[:, :D] + b_query.astype(jnp.float32)).astype(jnp.bfloat16)
    keys_own = projected[:, D : 2 * D].astype(jnp.bfloat16)
    values_own = (projected[:, 2 * D :] + b_value.astype(jnp.float32)).astype(jnp.bfloat16)
    levels = CP.bit_length() - 1
    gathered_kv = jnp.stack([keys_own, values_own])[:, None]
    for level_bit in range(levels):
        partner = swapped(gathered_kv, "shard", level_bit)
        upper_half = shard_place >> level_bit & 1
        gathered_kv = jnp.where(
            upper_half == 1,
            jnp.concatenate([partner, gathered_kv], 1),
            jnp.concatenate([gathered_kv, partner], 1),
        )

    def by_sequence(stacked):
        return (
            stacked.reshape(CP, SEQ_GRP, STRETCH, H, HD)
            .transpose(1, 0, 2, 3, 4)
            .reshape(SEQ_GRP, CP * STRETCH, H, HD)
        )

    def by_place(stacked):
        return (
            stacked.reshape(SEQ_GRP, CP, STRETCH, D).transpose(1, 0, 2, 3).reshape(CP, tok_rows, D)
        )

    keys_seq = by_sequence(gathered_kv[0])
    values_seq = by_sequence(gathered_kv[1])
    queries_seq = queries.reshape(SEQ_GRP, STRETCH, H, HD)
    attended, log_total = lax.map(
        attend_forward, (queries_seq, keys_seq, values_seq, q_places, k_places)
    )
    attended_low = attended.reshape(tok_rows, D).astype(jnp.bfloat16)
    branch = jnp.dot(attended_low, w_out, preferred_element_type=jnp.float32) + b_out.astype(
        jnp.float32
    )
    middle = in_rows + branch
    normed_two, pull_second = jax.vjp(
        layer_norm, middle, g_second.astype(jnp.float32), s_second.astype(jnp.float32)
    )
    second_low = normed_two.astype(jnp.bfloat16)
    hidden = jnp.dot(second_low, w_fc, preferred_element_type=jnp.float32) + b_fc.astype(
        jnp.float32
    )
    active, pull_gelu = jax.vjp(gelu_tanh, hidden)
    active_low = active.astype(jnp.bfloat16)
    output = (
        middle
        + jnp.dot(active_low, w_proj, preferred_element_type=jnp.float32)
        + b_proj.astype(jnp.float32)
    )
    back_weights = (
        lax.all_gather(qkv_weight, "shard", axis=0, tiled=True),
        lax.all_gather(out_weight, "shard", axis=0, tiled=True),
        lax.all_gather(fc_weight, "shard", axis=0, tiled=True),
        lax.all_gather(proj_weight, "shard", axis=0, tiled=True),
    )
    back_qkv, back_out, back_fc, back_proj = back_weights
    grad_rows = cotangent.astype(jnp.float32)
    proj_grad = matmul_rows(active_low, cotangent)
    pbias_grad = jnp.sum(grad_rows, axis=0)
    active_grad = matmul_back(cotangent, back_proj)
    (hidden_grad,) = pull_gelu(active_grad)
    hidden_low = hidden_grad.astype(jnp.bfloat16)
    fc_grad = matmul_rows(second_low, hidden_low)
    fbias_grad = jnp.sum(hidden_low.astype(jnp.float32), axis=0)
    second_grad = matmul_back(hidden_low, back_fc)
    middle_part, gsecond_grad, ssecond_grad = pull_second(second_grad)
    middle_grad = grad_rows + middle_part
    branch_low = middle_grad.astype(jnp.bfloat16)
    outw_grad = matmul_rows(attended_low, branch_low)
    obias_grad = jnp.sum(branch_low.astype(jnp.float32), axis=0)
    attended_grad = (
        matmul_back(branch_low, back_out).astype(jnp.bfloat16).reshape(SEQ_GRP, STRETCH, H, HD)
    )
    query_grads, key_grads, value_grads = lax.map(
        attend_backward,
        (queries_seq, keys_seq, values_seq, q_places, k_places, log_total, attended_grad),
    )
    pending = jnp.stack([by_place(key_grads), by_place(value_grads)])
    for level_bit in reversed(range(levels)):
        half_size = pending.shape[1] // 2
        upper_half = shard_place >> level_bit & 1 == 1
        lower_part = pending[:, :half_size]
        upper_part = pending[:, half_size:]
        outgoing = jnp.where(upper_half, lower_part, upper_part)
        retained = jnp.where(upper_half, upper_part, lower_part)
        pending = retained + swapped(outgoing.astype(jnp.bfloat16), "shard", level_bit).astype(
            outgoing.dtype
        )
    qgrad_low = query_grads.reshape(tok_rows, D).astype(jnp.bfloat16)
    kgrad_low = pending[0, 0].astype(jnp.bfloat16)
    vgrad_low = pending[1, 0].astype(jnp.bfloat16)
    projected_grad = jnp.concatenate([qgrad_low, kgrad_low, vgrad_low], axis=1)
    qkv_grad = matmul_rows(normed_low, projected_grad)
    qbias_grad = jnp.sum(qgrad_low.astype(jnp.float32), axis=0)
    vbias_grad = jnp.sum(vgrad_low.astype(jnp.float32), axis=0)
    first_grad = matmul_back(projected_grad, back_qkv)
    input_part, gfirst_grad, sfirst_grad = pull_first(first_grad)
    tokens_grad = (middle_grad + input_part).astype(jnp.bfloat16)
    shared = (
        lax.psum_scatter(
            qkv_grad.astype(jnp.bfloat16), "shard", scatter_dimension=0, tiled=True
        ).astype(jnp.float32),
        lax.psum_scatter(
            outw_grad.astype(jnp.bfloat16), "shard", scatter_dimension=0, tiled=True
        ).astype(jnp.float32),
        lax.psum_scatter(
            fc_grad.astype(jnp.bfloat16), "shard", scatter_dimension=0, tiled=True
        ).astype(jnp.float32),
        lax.psum_scatter(
            proj_grad.astype(jnp.bfloat16), "shard", scatter_dimension=0, tiled=True
        ).astype(jnp.float32),
        lax.psum_scatter(
            qbias_grad.astype(jnp.bfloat16), "shard", scatter_dimension=0, tiled=True
        ).astype(jnp.float32),
        lax.psum_scatter(
            vbias_grad.astype(jnp.bfloat16), "shard", scatter_dimension=0, tiled=True
        ).astype(jnp.float32),
        lax.psum_scatter(
            obias_grad.astype(jnp.bfloat16), "shard", scatter_dimension=0, tiled=True
        ).astype(jnp.float32),
        lax.psum_scatter(
            fbias_grad.astype(jnp.bfloat16), "shard", scatter_dimension=0, tiled=True
        ).astype(jnp.float32),
        lax.psum_scatter(
            pbias_grad.astype(jnp.bfloat16), "shard", scatter_dimension=0, tiled=True
        ).astype(jnp.float32),
        lax.psum_scatter(
            gfirst_grad.astype(jnp.bfloat16), "shard", scatter_dimension=0, tiled=True
        ).astype(jnp.float32),
        lax.psum_scatter(
            sfirst_grad.astype(jnp.bfloat16), "shard", scatter_dimension=0, tiled=True
        ).astype(jnp.float32),
        lax.psum_scatter(
            gsecond_grad.astype(jnp.bfloat16), "shard", scatter_dimension=0, tiled=True
        ).astype(jnp.float32),
        lax.psum_scatter(
            ssecond_grad.astype(jnp.bfloat16), "shard", scatter_dimension=0, tiled=True
        ).astype(jnp.float32),
    )
    owned = (
        lax.psum_scatter(
            shared[0].astype(jnp.bfloat16), "replica", scatter_dimension=1, tiled=True
        ).astype(jnp.float32),
        lax.psum_scatter(
            shared[1].astype(jnp.bfloat16), "replica", scatter_dimension=1, tiled=True
        ).astype(jnp.float32),
        lax.psum_scatter(
            shared[2].astype(jnp.bfloat16), "replica", scatter_dimension=1, tiled=True
        ).astype(jnp.float32),
        lax.psum_scatter(
            shared[3].astype(jnp.bfloat16), "replica", scatter_dimension=1, tiled=True
        ).astype(jnp.float32),
    )
    matrices = (
        lax.all_gather(owned[0].astype(jnp.bfloat16), "replica", axis=1, tiled=True).astype(
            jnp.float32
        ),
        lax.all_gather(owned[1].astype(jnp.bfloat16), "replica", axis=1, tiled=True).astype(
            jnp.float32
        ),
        lax.all_gather(owned[2].astype(jnp.bfloat16), "replica", axis=1, tiled=True).astype(
            jnp.float32
        ),
        lax.all_gather(owned[3].astype(jnp.bfloat16), "replica", axis=1, tiled=True).astype(
            jnp.float32
        ),
    )
    vectors = lax.psum(
        (
            shared[4],
            shared[5],
            shared[6],
            shared[7],
            shared[8],
            shared[9],
            shared[10],
            shared[11],
            shared[12],
        ),
        "replica",
    )
    return (output.astype(jnp.bfloat16), tokens_grad) + tuple(matrices) + tuple(vectors)


def solution(mesh):
    placed = (
        P(("replica", "shard"), None),
        P(),
        P("shard", None),
        P("shard", None),
        P("shard", None),
        P("shard", None),
        P("shard"),
        P("shard"),
        P("shard"),
        P("shard"),
        P("shard"),
        P("shard"),
        P("shard"),
        P("shard"),
        P("shard"),
        P(("replica", "shard"), None),
    )
    return jax.shard_map(
        on_device,
        mesh=mesh,
        in_specs=placed,
        out_specs=(
            P(("replica", "shard"), None),
            P(("replica", "shard"), None),
            P("shard", None),
            P("shard", None),
            P("shard", None),
            P("shard", None),
            P("shard"),
            P("shard"),
            P("shard"),
            P("shard"),
            P("shard"),
            P("shard"),
            P("shard"),
            P("shard"),
            P("shard"),
        ),
        check_vma=False,
    )
```

profile of v0, /device:TPU:0, one launch (start us, length us, event | category | flops | bytes accessed | tf_op | source)
XLA Modules:
  0.0 2006.0 jit_solution(11616875526531276761)
XLA Ops:
  14.1 32.0 %all-reduce.23 = (bf16[1600]{0:T(1024)(128)(2,1)S(1)}, bf16[1600]{0:T(1024)(128)(2,1)S(1)}, bf16[1600]{0:T(1024)(128)(2,1)S(1)}, bf16[1600]{0:T(1024)(128)(2,1)S...) all-reduce(bf16[1600]{0:T(1024)(128)(2,1)S(1)} %dynamic-update-slic, ...), channel_id=1, replica_groups=mesh['replica'=4,'shard'=8] {'shard'}, use_global_device_ids=true, to_apply=%add.1 | all-reduce | flops 17600 | bytes 70400
  46.7 107.7 %all-gather.10.cloned.1.call-done = bf16[1600,4800]{1,0:T(8,128)(2,1)} async-done(((bf16[200,4800]{1,0:T(8,128)(2,1)}), bf16[1600,4800]{1,0:T(8,128)(2,1)}) %all-gather.10.cloned.1.call-update) | async-done | bytes 15360016 | tf_op jit(solution)/shard_map/all_gather | solution.py:121
  170.5 72.4 %collective-permute-done.1 = bf16[2,2,128,1600]{2,3,0,1:T(8,128)(2,1)} collective-permute-done((bf16[2,2,128,1600]{2,3,0,1:T(8,128)(2,1)S(1)}, bf16[2,2,128,1600]{2,3,0,1:T(8,128)(2,1)}, u32[]{:S(2)}, u32[]{:S(2)}) %collective-permute-start.1) | collective-permute-done | bytes 1638432 | tf_op jit(solution)/shard_map/ppermute | solution.py:26
  249.7 293.3 %collective-permute-done.2 = bf16[2,4,128,1600]{2,3,0,1:T(8,128)(2,1)} collective-permute-done((bf16[2,4,128,1600]{2,3,0,1:T(8,128)(2,1)}, bf16[2,4,128,1600]{2,3,0,1:T(8,128)(2,1)}, u32[]{:S(2)}, u32[]{:S(2)}) %collective-permute-start.2) | collective-permute-done | bytes 3276832 | tf_op jit(solution)/shard_map/ppermute | solution.py:26
  592.8 13.4 fusion.16
  611.6 12.1 convolution_add_fusion
  623.6 122.9 %all-gather.16.cloned.1.call-done = bf16[6400,1600]{1,0:T(8,128)(2,1)} async-done(((bf16[800,1600]{1,0:T(8,128)(2,1)}), bf16[6400,1600]{1,0:T(8,128)(2,1)}) %all-gather.16.cloned.1.call-update) | async-done | bytes 20480016 | tf_op jit(solution)/shard_map/all_gather | solution.py:124
  746.6 12.8 fusion.43
  759.3 12.5 multiply_reduce_fusion.1
  822.6 141.7 %collective-permute-done.3 = bf16[2,4,128,1600]{2,3,1,0:T(8,128)(2,1)S(1)} collective-permute-done((bf16[2,4,128,1600]{2,3,1,0:T(8,128)(2,1)}, bf16[2,4,128,1600]{2,3,1,0:T(8,128)(2,1)S(1)}, u32[]{:S(2)}, u32[]{:S(2)}) %collective-permute-start.3) | collective-permute-done | bytes 3276832 | tf_op jit(solution)/shard_map/ppermute | solution.py:26
  970.4 37.7 %collective-permute-done.4 = bf16[2,2,128,1600]{2,3,1,0:T(8,128)(2,1)S(1)} collective-permute-done((bf16[2,2,128,1600]{2,3,1,0:T(8,128)(2,1)S(1)}, bf16[2,2,128,1600]{2,3,1,0:T(8,128)(2,1)S(1)}, u32[]{:S(2)}, u32[]{:S(2)}) %collective-permute-start.4) | collective-permute-done | bytes 1638432 | tf_op jit(solution)/shard_map/ppermute | solution.py:26
  1024.3 11.9 convolution_convert_fusion
  1053.1 127.6 %reduce-scatter.19.cloned.1.call-done = bf16[200,4800]{1,0:T(8,128)(2,1)} async-done(((bf16[1600,4800]{1,0:T(8,128)(2,1)}), bf16[200,4800]{1,0:T(8,128)(2,1)}) %reduce-scatter.19.cloned.1.call-update) | async-done | bytes 1920016 | tf_op jit(solution)/shard_map/reduce_scatter | solution.py:270
  1184.9 207.8 %reduce-scatter.21.cloned.1.call-done = bf16[800,1600]{1,0:T(8,128)(2,1)} async-done(((bf16[6400,1600]{1,0:T(8,128)(2,1)}), bf16[800,1600]{1,0:T(8,128)(2,1)}) %reduce-scatter.21.cloned.1.call-update) | async-done | bytes 2560016 | tf_op jit(solution)/shard_map/reduce_scatter | solution.py:279
  1392.8 204.8 %reduce-scatter.31.cloned.1.call-done = bf16[200,6400]{1,0:T(8,128)(2,1)} async-done(((bf16[1600,6400]{1,0:T(8,128)(2,1)}), bf16[200,6400]{1,0:T(8,128)(2,1)}) %reduce-scatter.31.cloned.1.call-update) | async-done | bytes 2560016
  1602.3 57.9 %reduce-scatter.29.cloned.1.call-done = bf16[200,1600]{1,0:T(8,128)(2,1)} async-done(((bf16[1600,1600]{1,0:T(8,128)(2,1)}), bf16[200,1600]{1,0:T(8,128)(2,1)}) %reduce-scatter.29.cloned.1.call-update) | async-done | bytes 640016
  1662.7 38.0 %reduce-scatter.23.cloned.1.call-done = bf16[1200,200]{1,0:T(8,128)(2,1)} async-done(((bf16[4800,200]{1,0:T(8,128)(2,1)}), bf16[1200,200]{1,0:T(8,128)(2,1)}) %reduce-scatter.23.cloned.1.call-update) | async-done | bytes 480016
  1704.2 79.1 %all-reduce.26.cloned.1.call-done = bf16[800,1600]{1,0:T(8,128)(2,1)} async-done(((bf16[800,1600]{1,0:T(8,128)(2,1)}), bf16[800,1600]{1,0:T(8,128)(2,1)}) %all-reduce.26.cloned.1.call-update) | async-done | bytes 2560016
  1787.8 44.7 %reduce-scatter.27.cloned.1.call-done = bf16[1600,200]{1,0:T(8,128)(2,1)} async-done(((bf16[6400,200]{1,0:T(8,128)(2,1)}), bf16[1600,200]{1,0:T(8,128)(2,1)}) %reduce-scatter.27.cloned.1.call-update) | async-done | bytes 640016
  1845.6 29.2 %all-reduce.22 = (bf16[1600]{0:T(1024)(128)(2,1)S(1)}, bf16[1600]{0:T(1024)(128)(2,1)S(1)}, bf16[1600]{0:T(1024)(128)(2,1)S(1)}, bf16[1600]{0:T(1024)(128)(2,1)S...) all-reduce(bf16[1600]{0:T(1024)(128)(2,1)S(1)} %dynamic-update-slic, ...), channel_id=1, replica_groups=mesh['replica'=4,'shard'=8] {'shard'}, use_global_device_ids=true, to_apply=%add.8 | all-reduce | flops 20800 | bytes 83200
  1875.2 15.7 all-reduce.21
  1893.2 14.7 fusion.14
  1907.9 15.1 all_gather.69
  1950.7 36.6 %all-gather.22.cloned.1.call-done = bf16[4,1600,200]{1,2,0:T(8,128)(2,1)} async-done(((bf16[1,1600,200]{1,2,0:T(8,128)(2,1)}), bf16[4,1600,200]{1,2,0:T(8,128)(2,1)}) %all-gather.22.cloned.1.call-update) | async-done | bytes 2560016 | tf_op jit(solution)/shard_map/all_gather | solution.py:331
  (242 shorter events, 246.0 us)
Async XLA Ops:
  7.2 241.0 %copy-start = (s32[4,8,1]{1,2,0:T(1,128)S(1)}, s32[4,8,1]{1,2,0:T(1,128)}, u32[]{:S(2)}) copy-start(s32[4,8,1]{1,2,0:T(1,128)} %param.17) | copy-start | bytes 388
  7.2 147.1 %all-gather.10.cloned.1.call-start = ((), (), s32[]{:S(2)}) async-start(), calls=%async_computation.7 | async-start | bytes 17510400 | tf_op jit(solution)/shard_map/all_gather | solution.py:121
  8.0 598.2 %all-gather.12.cloned.1.call-start = ((), (), s32[]{:S(2)}) async-start(), calls=%async_computation.8 | async-start | bytes 5990400 | tf_op jit(solution)/shard_map/all_gather | solution.py:122
  8.8 602.8 %all-gather.14.cloned.1.call-start = ((), (), s32[]{:S(2)}) async-start(), calls=%async_computation.9 | async-start | bytes 23040000 | tf_op jit(solution)/shard_map/all_gather | solution.py:123
  9.5 737.0 %all-gather.16.cloned.1.call-start = ((), (), s32[]{:S(2)}) async-start(), calls=%async_computation.10 | async-start | bytes 23961600 | tf_op jit(solution)/shard_map/all_gather | solution.py:124
  10.1 1170.6 %reduce-scatter.19.cloned.1.call-start = ((), (), s32[]{:S(2)}) async-start(), calls=%async_computation.11 | async-start | bytes 17510400 | tf_op jit(solution)/shard_map/reduce_scatter | solution.py:270
  165.5 418.2 %copy-start.11 = (bf16[128,1600]{0,1:T(8,128)(2,1)}, bf16[128,1600]{0,1:T(8,128)(2,1)S(1)}, u32[]{:S(2)}) copy-start(bf16[128,1600]{0,1:T(8,128)(2,1)S(1)} %get-tuple-element.129) | copy-start | bytes 1228804
  165.6 2.5 collective-permute-start
  170.4 72.5 %collective-permute-start.1 = (bf16[2,2,128,1600]{2,3,0,1:T(8,128)(2,1)S(1)}, bf16[2,2,128,1600]{2,3,0,1:T(8,128)(2,1)}, u32[]{:S(2)}, u32[]{:S(2)}) collective-permute-start(bf16[2,2,128,1600]{2,3,0,1:T(8,128)(2,1)S(1)} %maximum_select_fusion.2), channel_id=1, source_target_pairs={{0,2},{2,0},{1,3},{3,1},{4,6},{6,4},{5,7},{7,5},{8,10},{10,8},{9,1... | collective-permute-start | bytes 4915208 | tf_op jit(solution)/shard_map/ppermute | solution.py:26
  246.2 296.7 %collective-permute-start.2 = (bf16[2,4,128,1600]{2,3,0,1:T(8,128)(2,1)}, bf16[2,4,128,1600]{2,3,0,1:T(8,128)(2,1)}, u32[]{:S(2)}, u32[]{:S(2)}) collective-permute-start(bf16[2,4,128,1600]{2,3,0,1:T(8,128)(2,1)} %maximum_select_fusion.1), channel_id=1, source_target_pairs={{0,4},{4,0},{1,5},{5,1},{2,6},{6,2},{3,7},{7,3},{8,12},{12,8},{9,1... | collective-permute-start | bytes 9830408 | tf_op jit(solution)/shard_map/ppermute | solution.py:26
  611.5 135.0 %copy-start.13 = (bf16[128,1600]{0,1:T(8,128)(2,1)S(1)}, bf16[128,1600]{0,1:T(8,128)(2,1)}, u32[]{:S(2)}) copy-start(bf16[128,1600]{0,1:T(8,128)(2,1)} %param.31) | copy-start | bytes 1228804
  822.0 142.3 %collective-permute-start.3 = (bf16[2,4,128,1600]{2,3,1,0:T(8,128)(2,1)}, bf16[2,4,128,1600]{2,3,1,0:T(8,128)(2,1)S(1)}, u32[]{:S(2)}, u32[]{:S(2)}) collective-permute-start(bf16[2,4,128,1600]{2,3,1,0:T(8,128)(2,1)} %select_convert_fusion), channel_id=1, source_target_pairs={{0,4},{4,0},{1,5},{5,1},{2,6},{6,2},{3,7},{7,3},{8,12},{12,8},{9,1... | collective-permute-start | bytes 9830408 | tf_op jit(solution)/shard_map/ppermute | solution.py:26
  970.3 37.8 %collective-permute-start.4 = (bf16[2,2,128,1600]{2,3,1,0:T(8,128)(2,1)S(1)}, bf16[2,2,128,1600]{2,3,1,0:T(8,128)(2,1)S(1)}, u32[]{:S(2)}, u32[]{:S(2)}) collective-permute-start(bf16[2,2,128,1600]{2,3,1,0:T(8,128)(2,1)S(1)} %select_convert_fusion.1), channel_id=1, source_target_pairs={{0,2},{2,0},{1,3},{3,1},{4,6},{6,4},{5,7},{7,5},{8,10},{10,8},{9,1... | collective-permute-start | bytes 4915208 | tf_op jit(solution)/shard_map/ppermute | solution.py:26
  1008.8 4.4 collective-permute-start.5
  1023.3 369.4 %reduce-scatter.21.cloned.1.call-start = ((), (), s32[]{:S(2)}) async-start(), calls=%async_computation.12 | async-start | bytes 23961600 | tf_op jit(solution)/shard_map/reduce_scatter | solution.py:279
  1036.3 561.4 %reduce-scatter.31.cloned.1.call-start = ((), (), s32[]{:S(2)}) async-start(), calls=%async_computation.21 | async-start | bytes 23040000
  1048.0 612.2 %reduce-scatter.29.cloned.1.call-start = ((), (), s32[]{:S(2)}) async-start(), calls=%async_computation.20 | async-start | bytes 5990400
  1053.0 647.7 %reduce-scatter.23.cloned.1.call-start = ((), (), s32[]{:S(2)}) async-start(), calls=%async_computation.16 | async-start | bytes 3072000
  1184.8 598.4 %all-reduce.26.cloned.1.call-start = ((), (), s32[]{:S(2)}) async-start(), calls=%async_computation.19 | async-start | bytes 5324800
  1392.8 439.7 %reduce-scatter.27.cloned.1.call-start = ((), (), s32[]{:S(2)}) async-start(), calls=%async_computation.18 | async-start | bytes 4096000
  1602.2 305.7 %reduce-scatter.25.cloned.1.call-start = ((), (), s32[]{:S(2)}) async-start(), calls=%async_computation.17 | async-start | bytes 1024000
  1662.5 261.9 %all-gather.20.cloned.1.call-start = ((), (), s32[]{:S(2)}) async-start(), calls=%async_computation.14 | async-start | bytes 2560000 | tf_op jit(solution)/shard_map/all_gather | solution.py:325
  1702.9 242.6 %all-gather.18.cloned.1.call-start = ((), (), s32[]{:S(2)}) async-start(), calls=%async_computation.13 | async-start | bytes 3584000 | tf_op jit(solution)/shard_map/all_gather | solution.py:334
  1786.1 201.2 %all-gather.22.cloned.1.call-start = ((), (), s32[]{:S(2)}) async-start(), calls=%async_computation.15 | async-start | bytes 3328000 | tf_op jit(solution)/shard_map/all_gather | solution.py:331
  (42 other events, 933.2 us)
Sparse Core Ops, SparseCore 0:
  9.7 144.6 all-gather.9
  156.0 84.0 all-gather.11
  241.8 315.0 all-gather.13
  558.3 188.1 all-gather.15
  1023.4 157.1 reduce-scatter.18
  1183.0 209.6 reduce-scatter.20
  1395.2 202.3 reduce-scatter.30
  1600.6 59.4 reduce-scatter.28
  1663.6 37.1 reduce-scatter.22
  1704.1 79.1 all-reduce.25
  1787.2 45.3 reduce-scatter.26
  1836.1 26.2 reduce-scatter.24
  1864.4 35.0 all-gather.19
  1901.3 44.0 all-gather.17
  1947.3 39.9 all-gather.21
where the time goes:
time: 2010 us
  waiting for transfers between devices  1590 us (79%)
  matrix products  150 us (7%)
  local copies, waits for them, and re-layouts  118 us (6%)
  blocking collectives  92 us (5%)
  other arithmetic  36 us (2%)
    ppermute x6, waiting for transfers between devices, swapped(): return lax.ppermute(block, axis, route)  547 us
    unnamed x21, waiting for transfers between devices  427 us
    reduce_scatter x1, waiting for transfers between devices, on_device(): lax.psum_scatter(proj_grad.astype(jnp.bfloat16), 'shard', scatter_dimensi...  208 us
    reduce_scatter x1, waiting for transfers between devices, on_device(): lax.psum_scatter(qkv_grad.astype(jnp.bfloat16), 'shard', scatter_dimensio...  128 us
    all_gather x1, waiting for transfers between devices, on_device(): lax.all_gather(proj_weight, 'shard', axis=0, tiled=True)  123 us
    all_gather x1, waiting for transfers between devices, on_device(): lax.all_gather(qkv_weight, 'shard', axis=0, tiled=True)  108 us
    unnamed x2, blocking collectives  61.2 us
    unnamed x121, local copies, waits for them, and re-layouts  55.1 us
  transfers between devices with their start and end apart: 21, of which 16 were waited for; matrix products, arithmetic and copies ran while one was open for 10% of the time, Pallas kernels for 0%

commit v1 on v0

v1 whole, which is shorter than its diff:
```python
import functools

import jax
import jax.numpy as jnp
from jax import lax
from jax.experimental import pallas as pl
from jax.experimental.pallas import tpu as pltpu
from jax.experimental.layout import Layout, with_layout_constraint
from jax.sharding import PartitionSpec as P

D = 1600
H = 25
HD = 64
CP = 8
STRETCH = 128
SEQ = CP * STRETCH
TILE = 256

norm_eps = 1e-05
masked_score = -1e30
gelu_coeff = 0.7978845608028654
low = jnp.bfloat16
full = jnp.float32


def xor_send(block, axis, bits):
    count = lax.axis_size(axis)
    return lax.ppermute(block, axis, [(i, i ^ bits) for i in range(count)])


def normed(values):
    average = jnp.mean(values, axis=-1, keepdims=True)
    centred = values - average
    variance = jnp.mean(centred * centred, axis=-1, keepdims=True)
    return centred * lax.rsqrt(variance + norm_eps)


def layer_norm(values, gain_vec, shift_vec):
    return normed(values) * gain_vec + shift_vec


def gelu_tanh(values):
    return (
        0.5 * values * (1.0 + jnp.tanh(gelu_coeff * (values + 0.044715 * values * values * values)))
    )


def mm(left_side, right_side, left_dim, right_dim):
    return lax.dot_general(
        left_side,
        right_side,
        (((left_dim,), (right_dim,)), ((), ())),
        preferred_element_type=full,
    )


def sort_blocks(order_ref, seq, source, target):
    for place in range(CP):
        start = pl.multiple_of(order_ref[seq, place] * STRETCH, STRETCH)
        target[place * STRETCH : (place + 1) * STRETCH, :] = source[pl.ds(start, STRETCH), :]


def unsort_tile(order_ref, seq, tile, value, target):
    for part in range(TILE // STRETCH):
        place = tile * (TILE // STRETCH) + part
        start = pl.multiple_of(order_ref[seq, place] * STRETCH, STRETCH)
        target[pl.ds(start, STRETCH), :] = value[part * STRETCH : (part + 1) * STRETCH, :]


def causal(scores):
    key_row = lax.broadcasted_iota(jnp.int32, scores.shape, 0)
    query_col = lax.broadcasted_iota(jnp.int32, scores.shape, 1)
    return jnp.where(key_row <= query_col, scores, masked_score)


def forward_kernel(heads, seqs, order_ref, q_ref, k_ref, v_ref, a_ref, lse_ref, qs, ks, vs, qt, vt):
    width = heads * HD
    for seq in range(seqs):
        sort_blocks(order_ref, seq, q_ref, qs)
        sort_blocks(order_ref, seq, k_ref, ks)
        sort_blocks(order_ref, seq, v_ref, vs)
        qt[...] = (qs[...].astype(full).T * HD ** (-0.5)).astype(low)
        vt[...] = vs[...].astype(full).T.astype(low)
        for tile in range(SEQ // TILE):
            cols = slice(tile * TILE, (tile + 1) * TILE)
            before = tile * TILE
            pieces = []
            for head in range(heads):
                row = lax.broadcasted_iota(jnp.int32, (width, TILE), 0)
                mine = (row >= head * HD) & (row < (head + 1) * HD)
                query = jnp.where(mine, qt[:, cols], jnp.zeros((), low))
                diag = causal(mm(ks[cols, :], query, 1, 0))
                high = jnp.max(diag, axis=0, keepdims=True)
                if tile:
                    past = mm(ks[:before, :], query, 1, 0)
                    high = jnp.maximum(high, jnp.max(past, axis=0, keepdims=True))
                    past = jnp.exp(past - high)
                diag = jnp.exp(diag - high)
                total = jnp.sum(diag, axis=0, keepdims=True)
                if tile:
                    total = total + jnp.sum(past, axis=0, keepdims=True)
                share = 1.0 / total
                own = slice(head * HD, (head + 1) * HD)
                mixed = mm(vt[own, cols], (diag * share).astype(low), 1, 0)
                if tile:
                    mixed = mixed + mm(vt[own, :before], (past * share).astype(low), 1, 0)
                pieces.append(mixed)
                lse_ref[seq, head : head + 1, cols] = high + jnp.log(total)
            mixed = jnp.concatenate(pieces, 0).T.astype(low)
            unsort_tile(order_ref, seqs + seq, tile, mixed, a_ref)


def backward_kernel(
    heads, seqs, order_ref, q_ref, k_ref, v_ref, da_ref, lse_ref,
    dq_ref, dk_ref, dv_ref, qs, ks, vs, das, qt, kt, dat, dks, dvs,
):
    width = heads * HD
    scale = HD ** (-0.5)
    for seq in range(seqs):
        sort_blocks(order_ref, seq, q_ref, qs)
        sort_blocks(order_ref, seq, k_ref, ks)
        sort_blocks(order_ref, seq, v_ref, vs)
        sort_blocks(order_ref, 2 * seqs + seq, da_ref, das)
        qt[...] = (qs[...].astype(full).T * scale).astype(low)
        kt[...] = (ks[...].astype(full).T * scale).astype(low)
        dat[...] = das[...].astype(full).T.astype(low)
        dks[...] = jnp.zeros_like(dks)
        dvs[...] = jnp.zeros_like(dvs)
        for tile in range(SEQ // TILE):
            cols = slice(tile * TILE, (tile + 1) * TILE)
            before = tile * TILE
            pieces = []
            for head in range(heads):
                own = slice(head * HD, (head + 1) * HD)
                row = lax.broadcasted_iota(jnp.int32, (width, TILE), 0)
                mine = (row >= head * HD) & (row < (head + 1) * HD)
                lane = lax.broadcasted_iota(jnp.int32, (TILE, width), 1)
                mine_lane = (lane >= head * HD) & (lane < (head + 1) * HD)
                none = jnp.zeros((), low)
                query_t = jnp.where(mine, qt[:, cols], none)
                grad_t = jnp.where(mine, dat[:, cols], none)
                query = jnp.where(mine_lane, qs[cols, :], none)
                grad = jnp.where(mine_lane, das[cols, :], none)
                log_total = lse_ref[seq, head : head + 1, cols]

                spans = [(cols, True)] + ([(slice(0, before), False)] if tile else [])
                kept = []
                dot = None
                for span, edge in spans:
                    scores = mm(ks[span, :], query_t, 1, 0)
                    if edge:
                        scores = causal(scores)
                    weights = jnp.exp(scores - log_total)
                    weight_grads = mm(vs[span, :], grad_t, 1, 0)
                    part = jnp.sum(weights * weight_grads, axis=0, keepdims=True)
                    dot = part if dot is None else dot + part
                    dvs[span, :] += mm(weights.astype(low), grad, 1, 0)
                    kept.append((span, weights, weight_grads))
                total = None
                for span, weights, weight_grads in kept:
                    score_grads = (weights * (weight_grads - dot)).astype(low)
                    dks[span, :] += mm(score_grads, query, 1, 0)
                    part = mm(kt[own, span], score_grads, 1, 0)
                    total = part if total is None else total + part
                pieces.append(total)
            unsort_tile(order_ref, seq, tile, jnp.concatenate(pieces, 0).T.astype(low), dq_ref)
        for tile in range(SEQ // TILE):
            cols = slice(tile * TILE, (tile + 1) * TILE)
            unsort_tile(order_ref, seq, tile, (dks[cols, :] * scale).astype(low), dk_ref)
            unsort_tile(order_ref, seq, tile, dvs[cols, :].astype(low), dv_ref)


vmem = pl.BlockSpec(memory_space=pltpu.VMEM)
smem = pl.BlockSpec(memory_space=pltpu.SMEM)


def attend_forward(order, queries, keys, values, heads):
    rows, width = queries.shape
    seqs = rows // SEQ
    return pl.pallas_call(
        functools.partial(forward_kernel, heads, seqs),
        out_shape=(
            jax.ShapeDtypeStruct((rows, width), low),
            jax.ShapeDtypeStruct((seqs, heads, SEQ), full),
        ),
        in_specs=[smem, vmem, vmem, vmem],
        out_specs=(vmem, vmem),
        scratch_shapes=[pltpu.VMEM((SEQ, width), low)] * 3 + [pltpu.VMEM((width, SEQ), low)] * 2,
        compiler_params=pltpu.CompilerParams(vmem_limit_bytes=40 * 2**20),
        cost_estimate=pl.CostEstimate(
            flops=seqs * heads * 2 * 2 * SEQ * SEQ * 256,
            bytes_accessed=8 * rows * width,
            transcendentals=seqs * heads * SEQ * SEQ,
        ),
        name="attend_forward",
    )(order, queries, keys, values)


def attend_backward(order, queries, keys, values, grads, log_total, heads):
    rows, width = queries.shape
    seqs = rows // SEQ
    shape = jax.ShapeDtypeStruct((rows, width), low)
    return pl.pallas_call(
        functools.partial(backward_kernel, heads, seqs),
        out_shape=(shape, shape, shape),
        in_specs=[smem, vmem, vmem, vmem, vmem, vmem],
        out_specs=(vmem, vmem, vmem),
        scratch_shapes=[pltpu.VMEM((SEQ, width), low)] * 4
        + [pltpu.VMEM((width, SEQ), low)] * 3
        + [pltpu.VMEM((SEQ, width), full)] * 2,
        compiler_params=pltpu.CompilerParams(vmem_limit_bytes=48 * 2**20),
        cost_estimate=pl.CostEstimate(
            flops=seqs * heads * 2 * 5 * SEQ * SEQ * 256,
            bytes_accessed=14 * rows * width,
            transcendentals=seqs * heads * SEQ * SEQ,
        ),
        name="attend_backward",
    )(order, queries, keys, values, grads, log_total)


def ranks(count):
    return list(range(0, count, 2)) + list(range(1, count, 2))


def rank_of(bits, count):
    return (bits & 1) * (count // 2) + (bits >> 1)


def windows(rows, copies, unit):
    step = rows // copies // unit * unit
    return step, rows - step * (copies - 1)


def local_call(kernel, shapes, scratch, name, where, *operands, after=()):
    operands = operands + tuple(after)
    many = isinstance(shapes, (list, tuple))
    size = sum(x.size * x.dtype.itemsize for x in operands)
    free = pl.BlockSpec(memory_space=pl.ANY)
    used = len(operands) - len(after)
    return pl.pallas_call(
        kernel,
        out_shape=tuple(shapes) if many else shapes,
        in_specs=[smem] + [vmem] * used + [free] * len(after),
        out_specs=tuple(vmem for _ in shapes) if many else vmem,
        scratch_shapes=scratch,
        compiler_params=pltpu.CompilerParams(vmem_limit_bytes=56 * 2**20),
        cost_estimate=pl.CostEstimate(flops=0, bytes_accessed=3 * size, transcendentals=0),
        name=name,
    )(where, *operands)


def pack_heads(where, weight, copies, count, width):
    step, span = windows(weight.shape[0], copies, 16)

    def kernel(where_ref, weight_ref, *refs):
        outs, pieces = refs[: count // 2], refs[count // 2]
        start = pl.multiple_of(where_ref[1] * step, 16)
        for other in range(count):
            low_col, high_col = other * width, min(D, (other + 1) * width)
            for third in range(3):
                have = max(0, high_col - low_col)
                at = third * width
                if have:
                    pieces[other, :, at : at + have] = weight_ref[
                        pl.ds(start, span), third * D + low_col : third * D + high_col
                    ]
                if have < width:
                    pieces[other, :, at + have : at + width] = jnp.zeros((span, width - have), low)
        for bits in range(count):
            outs[bits // 2][bits % 2] = pieces[where_ref[0] ^ bits]

    shape = jax.ShapeDtypeStruct((2, span, 3 * width), low)
    scratch = [pltpu.VMEM((count, span, 3 * width), low)]
    return local_call(kernel, [shape] * (count // 2), scratch, "pack_heads", where, weight)


def slot_rows(span):
    return -(-span // 16) * 16


def pack_columns(where, weight, out_weight, vectors, copies, count):
    step, span = windows(weight.shape[0], copies, 16)
    cols = weight.shape[1] // count
    slot = slot_rows(span)

    def kernel(where_ref, weight_ref, out_ref, vectors_ref, *refs):
        outs, pieces = refs[: count // 2], refs[count // 2]
        start = pl.multiple_of(where_ref[1] * step, 16)
        for other in range(count):
            pieces[other] = weight_ref[pl.ds(start, span), other * cols : (other + 1) * cols]
        for pair, out in enumerate(outs):
            for side in range(2):
                out[:span, side * cols : (side + 1) * cols] = pieces[
                    where_ref[0] ^ (2 * pair + side)
                ]
            out[slot : slot + span, :] = out_ref[pl.ds(start, span), :]
            out[2 * slot :, :] = vectors_ref[...]

    shape = jax.ShapeDtypeStruct((2 * slot + 16, D), low)
    scratch = [pltpu.VMEM((count, span, cols), low)]
    return local_call(
        kernel, [shape] * (count // 2), scratch, "pack_columns", where, weight, out_weight, vectors
    )


def split_columns(where, got, span, cols):
    half = len(got)
    slot = slot_rows(span)

    def kernel(where_ref, *refs):
        odd, rows = refs[half:]
        for pair in range(half):
            odd[pair] = refs[pair][:span, cols : 2 * cols]
            rows[pair] = refs[pair][slot : slot + span, :]

    shapes = [
        jax.ShapeDtypeStruct((half, span, cols), low),
        jax.ShapeDtypeStruct((half, span, D), low),
    ]
    return local_call(kernel, shapes, [], "split_columns", where, *got)


def assemble_rows(where, stacks, own_rows):
    each = len(stacks[0])
    count = sum(array.shape[0] for array in stacks[0])
    span, cols = stacks[0][0].shape[1:]
    step, _ = windows(own_rows, len(stacks), 16)
    stacks = stacks if step else stacks[:1]
    copies = len(stacks)
    arrays = [array for stack in stacks for array in stack]

    def kernel(where_ref, *refs):
        out = refs[-1]
        for bits_copy in range(copies):
            start = pl.multiple_of((where_ref[1] ^ bits_copy) * step, 16)
            blocks = [
                ref.at[row]
                for ref in refs[bits_copy * each : (bits_copy + 1) * each]
                for row in range(ref.shape[0])
            ]
            for block, bits in zip(blocks, ranks(count)):
                out[where_ref[0] ^ bits, pl.ds(start, span), :] = block[...]

    shape = jax.ShapeDtypeStruct((count, own_rows, cols), low)
    return local_call(kernel, shape, [], "assemble_rows", where, *arrays)


def split_heads(where, block, count, width):
    rows, cols = block.shape

    def kernel(where_ref, block_ref, *refs):
        outs, pieces = refs[: count // 2], refs[count // 2]
        for other in range(count):
            start, stop = min(cols, other * width), min(cols, (other + 1) * width)
            if start < stop:
                pieces[other, :, : stop - start] = block_ref[:, start:stop]
            if stop - start < width:
                pieces[other, :, stop - start :] = jnp.zeros((rows, width - stop + start), low)
        for bits in range(count):
            outs[bits // 2][bits % 2] = pieces[where_ref[0] ^ bits]

    shape = jax.ShapeDtypeStruct((2, rows, width), low)
    scratch = [pltpu.VMEM((count, rows, width), low)]
    return local_call(kernel, [shape] * (count // 2), scratch, "split_heads", where, block)


def order_heads(where, pairs, far):
    half = len(pairs)
    count = 2 * half
    _, rows, width = far.shape

    def kernel(where_ref, *refs):
        out, pieces = refs[-2], refs[-1]
        for pair in range(half):
            pieces[2 * pair] = refs[pair][0]
            pieces[2 * pair + 1] = refs[half][pair]
        for other in range(count):
            out[:, other * width : (other + 1) * width] = pieces[where_ref[0] ^ other]

    shape = jax.ShapeDtypeStruct((rows, count * width), low)
    scratch = [pltpu.VMEM((count, rows, width), low)]
    return local_call(kernel, shape, scratch, "order_heads", where, *pairs, far)


SLOTS = 4


def lane_of(bits, cols):
    return bits // SLOTS * cols


def own_block(ref, bits, cols, groups):
    slot, group = lax.rem(bits, SLOTS), lax.div(bits, SLOTS)
    value = ref[slot, :, :cols].astype(full)
    for index in range(1, groups):
        other = ref[slot, :, index * cols : (index + 1) * cols].astype(full)
        value = jnp.where(group == index, other, value)
    return value


def pack_hidden(where, fc_full, proj_full, sums, copies):
    count, rows, cols = fc_full.shape
    step, span = windows(rows, copies, 16)
    proj_step, proj_span = windows(proj_full.shape[0], copies, 8)
    extra = -(-(proj_span + 16) // span)
    after = slot_rows(proj_span) - (extra - 1) * span

    def kernel(where_ref, fc_ref, proj_ref, sums_ref, *outs):
        for index, out in enumerate(outs):
            copy = where_ref[1] ^ index
            start = pl.multiple_of(copy * step, 16)
            for bits in range(count):
                lane = lane_of(bits, cols)
                out[bits % SLOTS, :, lane : lane + cols] = fc_ref[
                    where_ref[0] ^ bits, pl.ds(start, span), :
                ].astype(low)
            first = copy * proj_step
            for slot in range(extra):
                length = min(span, proj_span - slot * span)
                if length > 0:
                    at = pl.multiple_of(first + slot * span, 8) if span % 8 == 0 else first
                    out[SLOTS + slot, :length, :] = proj_ref[pl.ds(at, length), :].astype(low)
            out[SLOTS + extra - 1, after : after + 16, : sums.shape[2]] = sums_ref[copy].astype(low)

    shape = jax.ShapeDtypeStruct((SLOTS + extra, span, D), low)
    return local_call(
        kernel, [shape] * copies, [], "pack_hidden", where, fc_full, proj_full, sums
    )


def sum_hidden(where, pieces, count, cols):
    number = len(pieces)
    slots, span, _ = pieces[0].shape

    def kernel(where_ref, *refs):
        outs, rest = refs[number:-1], refs[-1]
        for slot in range(slots):
            total = refs[0][slot].astype(full)
            for piece in refs[1:number]:
                total = total + piece[slot].astype(full)
            total = total.astype(low)
            if slot >= SLOTS:
                rest[slot - SLOTS] = total
                continue
            for bits in range(slot, count, SLOTS):
                lane = lane_of(bits, cols)
                outs[bits // 2][bits % 2] = total[:, lane : lane + cols]

    shapes = [jax.ShapeDtypeStruct((2, span, cols), low)] * (count // 2)
    shapes.append(jax.ShapeDtypeStruct((slots - SLOTS, span, D), low))
    outs = local_call(kernel, shapes, [], "sum_hidden", where, *pieces)
    return outs[:-1], outs[-1]


def join_hidden(where, got, far, rest):
    half = len(got)
    _, span, cols = far.shape

    def kernel(where_ref, *refs):
        out = refs[-1]
        for bits in range(2 * half):
            block = refs[half][bits // 2] if bits % 2 else refs[bits // 2][0]
            lane = lane_of(bits, cols)
            out[bits % SLOTS, :, lane : lane + cols] = block
        for slot in range(rest.shape[0]):
            out[SLOTS + slot] = refs[half + 1][slot]

    shape = jax.ShapeDtypeStruct((SLOTS + rest.shape[0], span, D), low)
    return local_call(kernel, shape, [], "join_hidden", where, *got, far, rest)


def finish_hidden(where, stacks, count, rows, cols, proj_rows, lanes):
    copies = len(stacks)
    slots, span, _ = stacks[0].shape
    step, _ = windows(rows, copies, 16)
    proj_step, proj_span = windows(proj_rows, copies, 8)
    extra = slots - SLOTS
    after = slot_rows(proj_span) - (extra - 1) * span

    def kernel(where_ref, *refs):
        fc_out, proj_out, sums_out = refs[copies:]
        for index in range(copies):
            piece, copy = refs[index], where_ref[1] ^ index
            start = pl.multiple_of(copy * step, 16)
            if step or index == 0:
                for other in range(count):
                    fc_out[pl.ds(start, span), other * cols : (other + 1) * cols] = own_block(
                        piece, where_ref[0] ^ other, cols, count // SLOTS
                    )
            for slot in range(extra):
                length = min(span, proj_span - slot * span)
                if length > 0:
                    at = copy * proj_step
                    at = pl.multiple_of(at + slot * span, 8) if span % 8 == 0 else at
                    proj_out[pl.ds(at, length), :] = piece[SLOTS + slot, :length, :].astype(full)
            sums_out[copy] = piece[SLOTS + extra - 1, after : after + 16, :lanes].astype(full)

    shapes = [
        jax.ShapeDtypeStruct((rows, count * cols), full),
        jax.ShapeDtypeStruct((proj_rows, D), full),
        jax.ShapeDtypeStruct((copies, 16, lanes), full),
    ]
    return local_call(kernel, shapes, [], "finish_hidden", where, *stacks)


def split_outw(where, grad, copies):
    count, rows, cols = grad.shape
    half = count // 2
    step, span = windows(rows, copies, 16)
    parts = copies if step else 1

    def kernel(where_ref, grad_ref, *refs):
        far = refs[parts]
        for index in range(parts):
            start = pl.multiple_of((where_ref[1] ^ index) * step, 16)
            for pair in range(half):
                for side, out in enumerate((refs[index], far.at[index])):
                    out[pair] = grad_ref[
                        where_ref[0] ^ (2 * pair + side), pl.ds(start, span), :
                    ].astype(low)

    shapes = [jax.ShapeDtypeStruct((half, span, cols), low)] * parts
    shapes.append(jax.ShapeDtypeStruct((parts, half, span, cols), low))
    outs = local_call(kernel, shapes, [], "split_outw", where, grad)
    return outs[:-1], outs[-1]


def pack_last(where, qkv_full, near, far, sums):
    copies, parts = sums.shape[0], len(near)
    count, rows, cols = qkv_full.shape
    half = count // 2
    step, span = windows(rows, copies, 16)
    spare = count // SLOTS * cols

    def kernel(where_ref, qkv_ref, *refs):
        far_ref, sums_ref = refs[parts], refs[parts + 1]
        for index, out in enumerate(refs[parts + 2 :]):
            copy = where_ref[1] ^ index
            start = pl.multiple_of(copy * step, 16)
            for bits in range(count):
                lane = lane_of(bits, cols)
                out[bits % SLOTS, :, lane : lane + cols] = qkv_ref[
                    where_ref[0] ^ bits, pl.ds(start, span), :
                ].astype(low)
                row = bits // SLOTS * 16
                out[bits % SLOTS, row : row + 16, spare : spare + 64] = sums_ref[copy, bits].astype(
                    low
                )
            for pair in range(half):
                total = refs[index % parts][pair].astype(full)
                total = total + far_ref[index % parts, pair].astype(full)
                out[SLOTS + pair] = total.astype(low)

    shape = jax.ShapeDtypeStruct((SLOTS + half, span, D), low)
    return local_call(kernel, [shape] * copies, [], "pack_last", where, qkv_full, *near, far, sums)


def sum_last(where, pieces, count, cols):
    number = len(pieces)
    half = count // 2
    span = pieces[0].shape[1]
    spare = count // SLOTS * cols

    def kernel(where_ref, *refs):
        outs = refs[number:]
        for slot in range(SLOTS + half):
            total = refs[0][slot].astype(full)
            for piece in refs[1:number]:
                total = total + piece[slot].astype(full)
            total = total.astype(low)
            if slot >= SLOTS:
                outs[slot - SLOTS][1] = total
                continue
            for bits in range(slot, count, SLOTS):
                lane, row, side = lane_of(bits, cols), bits // SLOTS * 16, bits % 2
                out = outs[bits // 2]
                out[0, :, side * cols : (side + 1) * cols] = total[:, lane : lane + cols]
                out[0, side * 16 : side * 16 + 16, 2 * cols : 2 * cols + 64] = total[
                    row : row + 16, spare : spare + 64
                ]

    shape = jax.ShapeDtypeStruct((2, span, D), low)
    return local_call(kernel, [shape] * half, [], "sum_last", where, *pieces)


def odd_last(where, got, cols):
    half = len(got)
    span = got[0].shape[1]

    def kernel(where_ref, *refs):
        out = refs[half]
        for pair in range(half):
            out[pair, :, :cols] = refs[pair][0, :, cols : 2 * cols]
            out[pair, :16, cols : cols + 64] = refs[pair][0, 16:32, 2 * cols : 2 * cols + 64]

    shape = jax.ShapeDtypeStruct((half, span, cols + 64), low)
    return local_call(kernel, shape, [], "odd_last", where, *got)


def join_last(where, got, far):
    half = len(got)
    _, span, wide = far.shape
    cols = wide - 64
    spare = 2 * half // SLOTS * cols

    def kernel(where_ref, *refs):
        far_ref, out = refs[half], refs[half + 1]
        sums = jnp.zeros((16, 64), full)
        total = jnp.zeros((span, D), full)
        for pair in range(half):
            for side in range(2):
                lane = lane_of(2 * pair + side, cols)
                block = far_ref[pair, :, :cols] if side else refs[pair][0, :, :cols]
                out[(2 * pair + side) % SLOTS, :, lane : lane + cols] = block
            sums = sums + refs[pair][0, :16, 2 * cols : 2 * cols + 64].astype(full)
            sums = sums + far_ref[pair, :16, cols : cols + 64].astype(full)
            total = total + refs[pair][1].astype(full)
        out[SLOTS] = total.astype(low)
        out[0, :16, spare : spare + 64] = sums.astype(low)

    shape = jax.ShapeDtypeStruct((SLOTS + 1, span, D), low)
    return local_call(kernel, shape, [], "join_last", where, *got, far)


def finish_last(where, stacks, count, rows, width):
    copies = len(stacks)
    span = stacks[0].shape[1]
    step, _ = windows(rows, copies, 16)
    cols = 3 * width
    spare = count // SLOTS * cols

    def kernel(where_ref, *refs):
        qkv_out, outw_out, sums_out = refs[copies:]
        for index in range(copies):
            piece, copy = refs[index], where_ref[1] ^ index
            start = pl.multiple_of(copy * step, 16)
            sums_out[copy] = piece[0, :16, spare : spare + 64].astype(full)
            if index and not step:
                continue
            outw_out[pl.ds(start, span), :] = piece[SLOTS].astype(full)
            for other in range(count):
                have = min(width, D - other * width)
                if have <= 0:
                    continue
                block = own_block(piece, where_ref[0] ^ other, cols, count // SLOTS)
                for third in range(3):
                    target = third * D + other * width
                    qkv_out[pl.ds(start, span), target : target + have] = block[
                        :, third * width : third * width + have
                    ]

    shapes = [
        jax.ShapeDtypeStruct((rows, 3 * D), full),
        jax.ShapeDtypeStruct((rows, D), full),
        jax.ShapeDtypeStruct((copies, 16, 64), full),
    ]
    return local_call(kernel, shapes, [], "finish_last", where, *stacks)


def on_device(
    tokens,
    offsets,
    qkv_weight,
    out_weight,
    fc_weight,
    proj_weight,
    query_bias,
    value_bias,
    out_bias,
    fc_bias,
    proj_bias,
    gain_first,
    shift_first,
    gain_second,
    shift_second,
    cotangent,
):
    count = lax.axis_size("shard")
    copies = lax.axis_size("replica")
    place = lax.axis_index("shard")
    copy = lax.axis_index("replica")
    where = jnp.stack([place, copy]).astype(jnp.int32)
    evens = list(range(0, count, 2))
    bits_of = ranks(count)
    half = count // 2
    heads = -(-H // count)
    span = windows(D // count, copies, 16)[1]
    width = heads * HD
    own_rows = D // count
    ff_cols = fc_weight.shape[1] // count

    def gather_rows(block):
        return lax.all_gather(block, "shard", axis=0, tiled=True)

    def scatter_rows(blocks):
        blocks = with_layout_constraint(blocks, Layout((0, 1)))
        return lax.psum_scatter(blocks, "shard", scatter_dimension=0, tiled=True)

    def exchange(pairs):
        got = [pairs[0]] + [xor_send(pairs[j], "shard", evens[j]) for j in range(1, half)]
        return got, xor_send(jnp.concatenate([pair[1:] for pair in got], 0), "shard", 1)

    def by_rank(got, far):
        return jnp.concatenate([pair[:1] for pair in got] + [far], 0)

    def from_copies(block):
        return [block] + [xor_send(block, "replica", bits) for bits in range(1, copies)]

    def to_copies(pieces):
        return [pieces[0]] + [xor_send(pieces[bits], "replica", bits) for bits in range(1, copies)]

    def tie(value, *others):
        return lax.optimization_barrier((value,) + others)[0]

    vectors = (
        query_bias,
        value_bias,
        out_bias,
        proj_bias,
        gain_first,
        shift_first,
        gain_second,
        shift_second,
    )
    token_all = gather_rows(tokens)
    qkv_got, qkv_far = exchange(pack_heads(where, qkv_weight, copies, count, width))
    qkv_stack = by_rank(qkv_got, qkv_far)
    vectors = tie(jnp.concatenate(vectors), qkv_stack)
    vectors = jnp.pad(vectors[None], ((0, 15), (0, D - 8 * own_rows)))
    fc_pairs = pack_columns(where, fc_weight, out_weight, vectors, copies, count)
    fc_got = [fc_pairs[0]] + [xor_send(fc_pairs[j], "shard", evens[j]) for j in range(1, half)]
    fc_odd, out_near = split_columns(where, fc_got, span, ff_cols)
    fc_far = xor_send(fc_odd, "shard", 1)
    vectors = jnp.concatenate([got[2 * slot_rows(span) :][:1] for got in fc_got], 0)
    vectors = jnp.concatenate([vectors, xor_send(vectors, "shard", 1)], 0)
    vectors = vectors[:, : 8 * own_rows].astype(full)
    chosen = (jnp.arange(count)[:, None] ^ place == jnp.array(bits_of)[None, :]).astype(full)
    vectors = lax.dot(chosen, vectors, precision=lax.Precision.HIGHEST)
    vectors = vectors.reshape(count, 8, own_rows).transpose(1, 0, 2).reshape(8, D)
    b_query, b_value, b_out, b_proj, g_first, s_first, g_second, s_second = vectors
    qkv_stacks = from_copies(qkv_stack)
    w_qkv = assemble_rows(where, [[stack] for stack in qkv_stacks], own_rows)
    w_qkv = w_qkv.reshape(D, 3 * width)

    out_near = from_copies(tie(out_near, *qkv_stacks))
    out_far = [xor_send(block, "shard", 1) for block in out_near]
    w_out = assemble_rows(where, list(zip(out_near, out_far)), own_rows).reshape(D, D)
    fc_stack = jnp.concatenate(
        [got[:span, :ff_cols][None] for got in fc_got] + [fc_far], 0
    )
    fc_stacks = from_copies(fc_stack)
    w_fc = assemble_rows(where, [[stack] for stack in fc_stacks], own_rows).reshape(D, ff_cols)

    def own_heads(vector):
        vector = jnp.pad(vector, (0, count * width - D))
        return lax.dynamic_slice_in_dim(vector, place * width, width, 0)

    seqs = count // CP
    starts = lax.dynamic_slice_in_dim(offsets, copy * seqs, seqs, 0)[:, :, 0] // STRETCH
    is_at = starts[:, None, :] == jnp.arange(CP)[None, :, None]
    order = jnp.sum(jnp.where(is_at, jnp.arange(CP)[None, None, :], 0), axis=2)
    order = order + CP * jnp.arange(seqs)[:, None]
    bits = order ^ place
    order = jnp.concatenate([order, bits, rank_of(bits, count)], 0).astype(jnp.int32)

    normed_low = layer_norm(token_all.astype(full), g_first, s_first).astype(low)
    projected = mm(normed_low, w_qkv, 1, 0)
    queries = (projected[:, :width] + own_heads(b_query)).astype(low)
    keys = tie(projected, fc_stack)[:, width : 2 * width].astype(low)
    values = (projected[:, 2 * width :] + own_heads(b_value)).astype(low)
    cot_all = gather_rows(tie(cotangent, queries))
    attended, log_total = attend_forward(order, queries, keys, values, heads)

    attended_own = order_heads(where, *exchange(list(attended.reshape(half, 2, STRETCH, width))))
    attended_own = attended_own[:, :D]
    in_rows = tokens.astype(full)
    middle = in_rows + mm(attended_own, w_out, 1, 0) + b_out
    second_own = layer_norm(middle, g_second, s_second).astype(low)
    second_all = gather_rows(tie(second_own, cot_all, *fc_stacks))
    hidden = mm(second_all, w_fc, 1, 0) + fc_bias.astype(full)
    active, pull_gelu = jax.vjp(gelu_tanh, hidden)
    active_low = active.astype(low)

    (hidden_grad,) = pull_gelu(mm(cot_all, proj_weight, 1, 1))
    hidden_low = hidden_grad.astype(low)
    second_part = mm(hidden_low, w_fc, 1, 1).astype(low)
    second_grad = scatter_rows(second_part).astype(full)

    proj_full = mm(tie(active_low, second_part), cot_all, 0, 0)
    fc_full = mm(tie(second_all, second_part), hidden_low, 0, 0)
    hidden_sums = jnp.sum(hidden_low.astype(full), axis=0).reshape(copies, 1, ff_cols // copies)
    hidden_sums = jnp.pad(hidden_sums, ((0, 0), (0, 15), (0, -ff_cols // copies % 128)))
    hidden_pieces = pack_hidden(
        where, fc_full.reshape(count, own_rows, ff_cols), proj_full, hidden_sums, copies
    )
    second_grad = tie(second_grad, hidden_pieces[0])
    hidden_pieces = to_copies(hidden_pieces)
    grad_rows = cotangent.astype(full)
    _, pull_second = jax.vjp(layer_norm, middle, g_second, s_second)
    middle_part, gsecond_part, ssecond_part = pull_second(second_grad)
    middle_grad = grad_rows + middle_part
    branch_low = middle_grad.astype(low)
    attended_grad = mm(branch_low, w_out, 1, 1).astype(low)
    attended_pairs = split_heads(where, attended_grad, count, width)
    outw_full = mm(attended_own, tie(branch_low, attended_pairs[0]), 0, 0)
    outw_near, outw_far = split_outw(where, outw_full.reshape(count, own_rows, D), copies)
    attended_grad = by_rank(*exchange(attended_pairs)).reshape(count * STRETCH, width)
    outw_far = xor_send(outw_far, "shard", 1)
    output_low = tie(active_low, attended_grad)
    attended_grad = tie(attended_grad, *hidden_pieces)
    early = jnp.stack(
        [jnp.sum(branch_low.astype(full), axis=0), jnp.sum(grad_rows, axis=0), gsecond_part, ssecond_part]
    )

    query_grads, key_grads, value_grads = attend_backward(
        order, queries, keys, values, attended_grad, log_total, heads
    )
    projected_grad = jnp.concatenate([query_grads, key_grads, value_grads], 1)
    first_part = mm(projected_grad, w_qkv, 1, 1)

    def head_sums(block):
        sums = jnp.sum(block.astype(full), axis=0)
        placed = lax.dynamic_update_slice_in_dim(
            jnp.zeros((count * width,), full), sums, place * width, 0
        )
        return placed[:D]

    norms = normed(token_all.astype(full))
    sums = jnp.stack(
        [
            head_sums(query_grads),
            head_sums(value_grads),
            early[0],
            early[1],
            jnp.sum(first_part * norms, axis=0),
            jnp.sum(first_part, axis=0),
            early[2],
            early[3],
        ]
    )
    sums = sums.reshape(8, count, own_rows).transpose(1, 0, 2).reshape(count, 8 * own_rows)
    by_bits = (jnp.arange(count)[:, None] ^ place == jnp.arange(count)[None, :]).astype(full)
    sums = lax.dot(by_bits, sums, precision=lax.Precision.HIGHEST)
    share = 8 * own_rows // copies
    sums = sums.reshape(count, copies, share).transpose(1, 0, 2)
    sums = jnp.pad(sums, ((0, 0), (0, 0), (0, 16 * 64 - share))).reshape(copies, count, 16, 64)
    first_grad = scatter_rows(first_part.astype(low)).astype(full)
    qkv_full = mm(normed_low, projected_grad, 0, 0).reshape(count, own_rows, 3 * width)
    last = pack_last(where, qkv_full, outw_near, outw_far, sums)
    first_grad = tie(first_grad, last[0])
    hidden_pieces[0] = tie(hidden_pieces[0], last[0])
    last = to_copies(last)

    fc_sums, rest = sum_hidden(where, hidden_pieces, count, ff_cols)
    hidden_stacks = from_copies(join_hidden(where, *exchange(fc_sums), rest))
    fc_grad, proj_grad, fbias = finish_hidden(
        where, hidden_stacks, count, own_rows, ff_cols, ff_cols, hidden_sums.shape[2]
    )
    fbias = fbias[:, 0, : ff_cols // copies].reshape(ff_cols)

    last = sum_last(where, last, count, 3 * width)
    last = [last[0]] + [xor_send(last[j], "shard", evens[j]) for j in range(1, half)]
    far = xor_send(odd_last(where, last, 3 * width), "shard", 1)
    last = from_copies(join_last(where, last, tie(far, hidden_stacks[1])))
    qkv_grad, outw_grad, sums = finish_last(where, last, count, own_rows, width)
    sums = sums.reshape(copies, 16 * 64)[:, :share].reshape(8, own_rows)

    output_part = mm(output_low, proj_weight, 1, 0).astype(low)
    output = middle + b_proj + scatter_rows(output_part).astype(full)

    _, pull_first = jax.vjp(lambda rows: layer_norm(rows, g_first, s_first), in_rows)
    (input_part,) = pull_first(first_grad)
    tokens_grad = (middle_grad + input_part).astype(low)
    qbias, vbias, obias, pbias, gfirst, sfirst, gsecond, ssecond = sums
    return (
        output.astype(low),
        tokens_grad,
        qkv_grad,
        outw_grad,
        fc_grad,
        proj_grad,
        qbias,
        vbias,
        obias,
        fbias,
        pbias,
        gfirst,
        sfirst,
        gsecond,
        ssecond,
    )


def solution(mesh):
    rows = P(("replica", "shard"), None)
    matrix = P("shard", None)
    vector = P("shard")
    return jax.shard_map(
        on_device,
        mesh=mesh,
        in_specs=(rows, P()) + (matrix,) * 4 + (vector,) * 9 + (rows,),
        out_specs=(rows, rows) + (matrix,) * 4 + (vector,) * 9,
        check_vma=False,
    )
```

time: 2010 us -> 665 us (0.33)
  waiting for transfers between devices: 1590 us -> 331 us
  Pallas kernels: 0 us -> 98 us
  blocking collectives: 92 us -> 0 us
  matrix products: 150 us -> 73.8 us
  local copies, waits for them, and re-layouts: 118 us -> 45.5 us
  starting transfers between devices: 3.93 us -> 76.3 us
    unnamed x21 -> x6, waiting for transfers between devices: 427 us -> 0.76 us
    reduce_scatter x2 -> x3, waiting for transfers between devices: 335 us -> 17.2 us  [scatter_rows(): return lax.psum_scatter(blocks, 'shard', scatter_dimension=0, tiled=True)]
    ppermute x6 -> x51, waiting for transfers between devices: 547 us -> 282 us  [xor_send(): return lax.ppermute(block, axis, [(i, i ^ bits) for i in range(count)])]
    all_gather x7 -> x3, waiting for transfers between devices: 278 us -> 30.4 us  [gather_rows(): return lax.all_gather(block, 'shard', axis=0, tiled=True)]
    pallas_call x0 -> x20, Pallas kernels: none -> 98 us  [the longest x18 79 us: local_call(): pl.pallas_call(kernel, out_shape=tuple(shapes) if many else shapes, in_sp...]
    dot_general x18 -> x14, matrix products: 150 us -> 73.8 us  [the longest x12 73.3 us: mm(): lax.dot_general(left_side, right_side, (((left_dim,), (right_dim,)), ((),...]
    ppermute x6 -> x51, starting transfers between devices: 3.11 us -> 74.8 us  [xor_send(): return lax.ppermute(block, axis, [(i, i ^ bits) for i in range(count)])]
    unnamed x2 -> x0, blocking collectives: 61.2 us -> none
  transfers between devices with their start and end apart: 21 -> 57, of which waited for: 16 -> 30; matrix products, arithmetic and copies ran while one was open for 10% -> 12% of each run, Pallas kernels for 0% -> 15%
where the time goes in v1:
time: 665 us; the launch traced here: 658 us
  waiting for transfers between devices  331 us (50%)
  Pallas kernels  98 us (15%)
  starting transfers between devices  76.3 us (11%)
  matrix products  73.8 us (11%)
  local copies, waits for them, and re-layouts  45.5 us (7%)
  other arithmetic  18.4 us (3%)
  between operations  15.2 us (2%)
    ppermute x51, waiting for transfers between devices, xor_send(): return lax.ppermute(block, axis, [(i, i ^ bits) for i in range(count)])  282 us
    pallas_call x18, Pallas kernels, local_call(): pl.pallas_call(kernel, out_shape=tuple(shapes) if many else shapes, in_sp...  79 us
    ppermute x51, starting transfers between devices, xor_send(): return lax.ppermute(block, axis, [(i, i ^ bits) for i in range(count)])  74.8 us
    dot_general x12, matrix products, mm(): lax.dot_general(left_side, right_side, (((left_dim,), (right_dim,)), ((),...  73.3 us
    all_gather x3, waiting for transfers between devices, gather_rows(): return lax.all_gather(block, 'shard', axis=0, tiled=True)  30.4 us
    unnamed x136, local copies, waits for them, and re-layouts  22.8 us
    reduce_scatter x3, waiting for transfers between devices, scatter_rows(): return lax.psum_scatter(blocks, 'shard', scatter_dimension=0, tiled=True)  17.2 us
  transfers between devices with their start and end apart: 57, of which 30 were waited for; matrix products, arithmetic and copies ran while one was open for 12% of the time, Pallas kernels for 15%

profile of v1, /device:TPU:0, one launch (start us, length us, event | category | flops | bytes accessed | tf_op | source)
XLA Modules:
  0.0 657.9 jit_solution(16646596673390536997)
XLA Ops:
  17.8 17.8 %collective-permute-done = bf16[2,56,768]{2,1,0:T(8,128)(2,1)S(1)} collective-permute-done((bf16[2,56,768]{2,1,0:T(8,128)(2,1)}, bf16[2,56,768]{2,1,0:T(8,128)(2,1)S(1)}, u32[]{:S(2)}, u32[]{:S(2)}) %collective-permute-start) | collective-permute-done | bytes 172064 | tf_op jit(solution)/shard_map/ppermute | solution.py:28
  35.7 11.6 %collective-permute-done.1 = bf16[2,56,768]{2,1,0:T(8,128)(2,1)S(1)} collective-permute-done((bf16[2,56,768]{2,1,0:T(8,128)(2,1)}, bf16[2,56,768]{2,1,0:T(8,128)(2,1)S(1)}, u32[]{:S(2)}, u32[]{:S(2)}) %collective-permute-start.1) | collective-permute-done | bytes 172064 | tf_op jit(solution)/shard_map/ppermute | solution.py:28
  63.6 17.1 %collective-permute-done.4.refs_1_ = bf16[144,1600]{1,0:T(8,128)(2,1)S(1)} collective-permute-done((bf16[144,1600]{1,0:T(8,128)(2,1)}, bf16[144,1600]{1,0:T(8,128)(2,1)S(1)}, u32[]{:S(2)}, u32[]{:S(2)}) %collective-permute-start.4) | collective-permute-done | bytes 460832 | tf_op jit(solution)/shard_map/ppermute | solution.py:28
  83.2 8.2 %collective-permute-done.5.refs_2_ = bf16[144,1600]{1,0:T(8,128)(2,1)S(1)} collective-permute-done((bf16[144,1600]{1,0:T(8,128)(2,1)}, bf16[144,1600]{1,0:T(8,128)(2,1)S(1)}, u32[]{:S(2)}, u32[]{:S(2)}) %collective-permute-start.5) | collective-permute-done | bytes 460832 | tf_op jit(solution)/shard_map/ppermute | solution.py:28
  126.0 8.2 %attend_forward.1 = (bf16[1024,256]{1,0:T(8,128)(2,1)S(1)}, f32[1,4,1024]{2,1,0:T(4,128)S(1)}) custom-call(s32[3,8]{1,0:T(4,128)S(1)} %pad_add_fusion.order_ref, bf16[1024,256]{1,0:T(8,128)(2,1)S(1)} %copy-done.4, bf16[1024,256]{1,0:T(8,128)(2,1)S(1)} %slice.248.k_ref, bf16[1024,256]{1,0:T(8,128)(2,1)S(1)} %copy-done.2), custom_call_target="tpu_custom_call" | custom-call | flops 4294967296 | bytes 2097152 | tf_op jit(solution)/shard_map/attend_forward/pallas_call | solution.py:180
  143.4 14.0 %collective-permute-done.19.refs_4_ = bf16[4,56,1600]{2,1,0:T(8,128)(2,1)} collective-permute-done((bf16[4,56,1600]{2,1,0:T(8,128)(2,1)}, bf16[4,56,1600]{2,1,0:T(8,128)(2,1)}, u32[]{:S(2)}, u32[]{:S(2)}) %collective-permute-start.19) | collective-permute-done | bytes 716832 | tf_op jit(solution)/shard_map/ppermute | solution.py:28
  194.2 18.0 %collective-permute-done.24.refs_2_ = bf16[8,56,800]{2,1,0:T(8,128)(2,1)} collective-permute-done((bf16[8,56,800]{2,1,0:T(8,128)(2,1)}, bf16[8,56,800]{2,1,0:T(8,128)(2,1)}, u32[]{:S(2)}, u32[]{:S(2)}) %collective-permute-start.24) | collective-permute-done | bytes 716832 | tf_op jit(solution)/shard_map/ppermute | solution.py:28
  221.2 30.4 %all-gather.8.cloned.1.call-done = bf16[1024,1600]{1,0:T(8,128)(2,1)} async-done(((bf16[128,1600]{1,0:T(8,128)(2,1)}), bf16[1024,1600]{1,0:T(8,128)(2,1)}) %all-gather.8.cloned.1.call-update) | async-done | bytes 3276816 | tf_op jit(solution)/shard_map/all_gather | solution.py:693
  251.6 11.3 %convert_reduce_fusion.1 = (f32[800]{0:T(1024)S(1)}, bf16[1024,800]{0,1:T(8,128)(2,1)S(1)}, bf16[1024,800]{0,1:T(8,128)(2,1)}) fusion(f32[1024,800]{0,1:T(8,128)} %fusion.61, f32[800]{0:T(1024)S(1)} %convert_element_type.92, bf16[1024,1600]{1,0:T(8,128)(2,1)} %all-gather.8.cloned.1.call-done, bf16[1600,800]{1,0:T(8,128)(2,1)} %bitcast.87), kind=kOutput, calls=%fused_computation.22 | convolution fusion | flops 2645196032 | bytes 12396800 | tf_op jit(solution)/shard_map/dot_general | solution.py:49
  272.6 8.4 %fusion.60.proj_ref = f32[800,1600]{1,0:T(8,128)} fusion(bf16[1024,800]{0,1:T(8,128)(2,1)} %get-tuple-element.100, bf16[1024,1600]{0,1:T(8,128)(2,1)} %all-gather.6.cloned.1.call-done), kind=kOutput, calls=%fused_computation.144 | convolution fusion | flops 2621440000 | bytes 10035200 | tf_op jit(solution)/shard_map/dot_general | solution.py:49
  286.4 7.5 %pack_hidden.1 = (bf16[8,56,1600]{2,1,0:T(8,128)(2,1)}, bf16[8,56,1600]{2,1,0:T(8,128)(2,1)}, bf16[8,56,1600]{2,1,0:T(8,128)(2,1)}, bf16[8,56,1600]{2,1,0:T(8,128)(2,1)}) custom-call(s32[2]{0:T(128)} %pad_add_fusion.1.where_ref, f32[8,200,800]{2,1,0:T(8,128)} %bitcast.85, f32[800,1600]{1,0:T(8,128)} %fusion.60.proj_ref, f32[4,16,256]{2,1,0:T(8,128)} %pad.22.sums_ref), custom_call_target="tpu_custom_call" | custom-call | bytes 30916608 | tf_op jit(solution)/shard_map/pack_hidden/pallas_call | solution.py:240
  293.9 17.2 %reduce-scatter.4.cloned.1.call-done = bf16[128,1600]{1,0:T(8,128)(2,1)} async-done(((bf16[1024,1600]{1,0:T(8,128)(2,1)}), bf16[128,1600]{1,0:T(8,128)(2,1)}) %reduce-scatter.4.cloned.1.call-update) | async-done | bytes 409616 | tf_op jit(solution)/shard_map/reduce_scatter | solution.py:697
  338.7 7.4 %convolution_convert_fusion = bf16[1024,1600]{1,0:T(8,128)(2,1)} fusion(bf16[1024,800]{0,1:T(8,128)(2,1)} %get-tuple-element.100, bf16[800,1600]{1,0:T(8,128)(2,1)S(1)} %copy-done), kind=kOutput, calls=%fused_computation.14 | convolution fusion | flops 2623078400 | bytes 7475200 | tf_op jit(solution)/shard_map/dot_general | solution.py:49
  363.7 19.0 %collective-permute-done.30.refs_1_ = bf16[8,56,1600]{2,1,0:T(8,128)(2,1)S(1)} collective-permute-done((bf16[8,56,1600]{2,1,0:T(8,128)(2,1)}, bf16[8,56,1600]{2,1,0:T(8,128)(2,1)S(1)}, u32[]{:S(2)}, u32[]{:S(2)}) %collective-permute-start.30) | collective-permute-done | bytes 1433632 | tf_op jit(solution)/shard_map/ppermute | solution.py:28
  382.7 33.1 %collective-permute-done.31.refs_2_ = bf16[8,56,1600]{2,1,0:T(8,128)(2,1)S(1)} collective-permute-done((bf16[8,56,1600]{2,1,0:T(8,128)(2,1)}, bf16[8,56,1600]{2,1,0:T(8,128)(2,1)S(1)}, u32[]{:S(2)}, u32[]{:S(2)}) %collective-permute-start.31) | collective-permute-done | bytes 1433632 | tf_op jit(solution)/shard_map/ppermute | solution.py:28
  415.9 10.8 %attend_backward.1 = (bf16[1024,256]{1,0:T(8,128)(2,1)S(1)}, bf16[1024,256]{1,0:T(8,128)(2,1)S(1)}, bf16[1024,256]{1,0:T(8,128)(2,1)S(1)}) custom-call(s32[3,8]{1,0:T(4,128)S(1)} %pad_add_fusion.order_ref, bf16[1024,256]{1,0:T(8,128)(2,1)S(1)} %copy-done.5, bf16[1024,256]{1,0:T(8,128)(2,1)S(1)} %slice.248.k_ref, bf16[1024,256]{1,0:T(8,128)(2,1)S(1)} %copy-done.3, ...), custom_call_target="tpu_custom_call" | custom-call | flops 10737418240 | bytes 3670016 | tf_op jit(solution)/shard_map/attend_backward/pallas_call | solution.py:203
  466.5 11.3 %collective-permute-done.43.refs_3_ = bf16[2,56,800]{2,1,0:T(8,128)(2,1)S(1)} collective-permute-done((bf16[2,56,800]{2,1,0:T(8,128)(2,1)}, bf16[2,56,800]{2,1,0:T(8,128)(2,1)S(1)}, u32[]{:S(2)}, u32[]{:S(2)}) %collective-permute-start.43) | collective-permute-done | bytes 179232 | tf_op jit(solution)/shard_map/ppermute | solution.py:28
  477.8 10.6 %collective-permute-start.41 = (bf16[2,56,800]{2,1,0:T(8,128)(2,1)}, bf16[2,56,800]{2,1,0:T(8,128)(2,1)S(1)}, u32[]{:S(2)}, u32[]{:S(2)}) collective-permute-start(bf16[2,56,800]{2,1,0:T(8,128)(2,1)} %get-tuple-element.126), channel_id=1, source_target_pairs={{0,2},{1,3},{2,0},{3,1},{4,6},{5,7},{6,4},{7,5},{8,10},{9,11},{10,... | collective-permute-start | bytes 537608 | tf_op jit(solution)/shard_map/ppermute | solution.py:28
  502.7 18.0 %collective-permute-done.35.refs_2_ = bf16[8,56,1600]{2,1,0:T(8,128)(2,1)S(1)} collective-permute-done((bf16[8,56,1600]{2,1,0:T(8,128)(2,1)}, bf16[8,56,1600]{2,1,0:T(8,128)(2,1)S(1)}, u32[]{:S(2)}, u32[]{:S(2)}) %collective-permute-start.35) | collective-permute-done | bytes 1433632 | tf_op jit(solution)/shard_map/ppermute | solution.py:28
  534.4 9.9 %collective-permute-done.37.refs_1_ = bf16[2,56,1600]{2,1,0:T(8,128)(2,1)S(1)} collective-permute-done((bf16[2,56,1600]{2,1,0:T(8,128)(2,1)}, bf16[2,56,1600]{2,1,0:T(8,128)(2,1)S(1)}, u32[]{:S(2)}, u32[]{:S(2)}) %collective-permute-start.37) | collective-permute-done | bytes 358432 | tf_op jit(solution)/shard_map/ppermute | solution.py:28
  545.2 12.6 %collective-permute-done.38.refs_2_ = bf16[2,56,1600]{2,1,0:T(8,128)(2,1)S(1)} collective-permute-done((bf16[2,56,1600]{2,1,0:T(8,128)(2,1)}, bf16[2,56,1600]{2,1,0:T(8,128)(2,1)S(1)}, u32[]{:S(2)}, u32[]{:S(2)}) %collective-permute-start.38) | collective-permute-done | bytes 358432 | tf_op jit(solution)/shard_map/ppermute | solution.py:28
  569.7 31.8 %collective-permute-done.49.refs_2_ = bf16[8,56,1600]{2,1,0:T(8,128)(2,1)} collective-permute-done((bf16[8,56,1600]{2,1,0:T(8,128)(2,1)S(1)}, bf16[8,56,1600]{2,1,0:T(8,128)(2,1)}, u32[]{:S(2)}, u32[]{:S(2)}) %collective-permute-start.49) | collective-permute-done | bytes 1433632 | tf_op jit(solution)/shard_map/ppermute | solution.py:28
  601.5 9.7 %finish_hidden.1 = (f32[200,6400]{1,0:T(8,128)}, f32[800,1600]{1,0:T(8,128)}, f32[4,16,256]{2,1,0:T(8,128)}) custom-call(s32[2]{0:T(128)} %pad_add_fusion.1.where_ref, bf16[8,56,1600]{2,1,0:T(8,128)(2,1)} %join_hidden.1.refs_0_, bf16[8,56,1600]{2,1,0:T(8,128)(2,1)} %collective-permute-done.45.refs_1_, bf16[8,56,1600]{2,1,0:T(8,128)(2,1)} %collective-permute-done.49.refs_2_, ...), custom_call_target="tpu_custom_call" | custom-call | bytes 17203200 | tf_op jit(solution)/shard_map/finish_hidden/pallas_call | solution.py:240
  612.7 23.2 %collective-permute-done.47.refs_2_ = bf16[5,56,1600]{2,1,0:T(8,128)(2,1)} collective-permute-done((bf16[5,56,1600]{2,1,0:T(8,128)(2,1)}, bf16[5,56,1600]{2,1,0:T(8,128)(2,1)}, u32[]{:S(2)}, u32[]{:S(2)}) %collective-permute-start.47) | collective-permute-done | bytes 896032 | tf_op jit(solution)/shard_map/ppermute | solution.py:28
  (372 shorter events, 275.6 us)
Async XLA Ops:
  7.3 95.2 %all-gather.4.cloned.1.call-start = ((), (), s32[]{:S(2)}) async-start(), calls=%async_computation.3 | async-start | bytes 3686400 | tf_op jit(solution)/shard_map/all_gather | solution.py:693
  8.0 204.2 %all-gather.6.cloned.1.call-start = ((), (), s32[]{:S(2)}) async-start(), calls=%async_computation.4 | async-start | bytes 3686400 | tf_op jit(solution)/shard_map/all_gather | solution.py:693
  11.2 36.1 %collective-permute-start.2 = (bf16[2,56,768]{2,1,0:T(8,128)(2,1)}, bf16[2,56,768]{2,1,0:T(8,128)(2,1)S(1)}, u32[]{:S(2)}, u32[]{:S(2)}) collective-permute-start(bf16[2,56,768]{2,1,0:T(8,128)(2,1)} %get-tuple-element.79), channel_id=1, source_target_pairs={{0,6},{1,7},{2,4},{3,5},{4,2},{5,3},{6,0},{7,1},{8,14},{9,15},{10,... | collective-permute-start | bytes 516104 | tf_op jit(solution)/shard_map/ppermute | solution.py:28
  55.5 35.8 %collective-permute-start.5 = (bf16[144,1600]{1,0:T(8,128)(2,1)}, bf16[144,1600]{1,0:T(8,128)(2,1)S(1)}, u32[]{:S(2)}, u32[]{:S(2)}) collective-permute-start(bf16[144,1600]{1,0:T(8,128)(2,1)} %get-tuple-element.83), channel_id=1, source_target_pairs={{0,4},{1,5},{2,6},{3,7},{4,0},{5,1},{6,2},{7,3},{8,12},{9,13},{10,... | collective-permute-start | bytes 1382408 | tf_op jit(solution)/shard_map/ppermute | solution.py:28
  59.9 35.4 %collective-permute-start.8 = (bf16[8,56,768]{2,1,0:T(8,128)(2,1)S(1)}, bf16[8,56,768]{2,1,0:T(8,128)(2,1)}, u32[]{:S(2)}, u32[]{:S(2)}) collective-permute-start(bf16[8,56,768]{2,1,0:T(8,128)(2,1)S(1)} %constant_dynamic-update-slice_fusion.refs_0_), channel_id=1, source_target_pairs={{0,8},{8,0},{16,24},{24,16},{1,9},{9,1},{17,25},{25,17},{2,10},{10... | collective-permute-start | bytes 2064392 | tf_op jit(solution)/shard_map/ppermute | solution.py:28
  113.1 138.5 %all-gather.8.cloned.1.call-start = ((), (), s32[]{:S(2)}) async-start(), calls=%async_computation.5 | async-start | bytes 3833856 | tf_op jit(solution)/shard_map/all_gather | solution.py:693
  174.7 37.5 %collective-permute-start.24 = (bf16[8,56,800]{2,1,0:T(8,128)(2,1)}, bf16[8,56,800]{2,1,0:T(8,128)(2,1)}, u32[]{:S(2)}, u32[]{:S(2)}) collective-permute-start(bf16[8,56,800]{2,1,0:T(8,128)(2,1)} %copy-done.35), channel_id=1, source_target_pairs={{0,16},{8,24},{16,0},{24,8},{1,17},{9,25},{17,1},{25,9},{2,18},{10... | collective-permute-start | bytes 2150408 | tf_op jit(solution)/shard_map/ppermute | solution.py:28
  176.2 36.0 %collective-permute-start.25 = (bf16[8,56,800]{2,1,0:T(8,128)(2,1)}, bf16[8,56,800]{2,1,0:T(8,128)(2,1)}, u32[]{:S(2)}, u32[]{:S(2)}) collective-permute-start(bf16[8,56,800]{2,1,0:T(8,128)(2,1)} %copy-done.35), channel_id=1, source_target_pairs={{0,24},{8,16},{16,8},{24,0},{1,25},{9,17},{17,9},{25,1},{2,26},{10... | collective-permute-start | bytes 2150408 | tf_op jit(solution)/shard_map/ppermute | solution.py:28
  212.2 98.9 %reduce-scatter.4.cloned.1.call-start = ((), (), s32[]{:S(2)}) async-start(), calls=%async_computation.6 | async-start | bytes 3833856 | tf_op jit(solution)/shard_map/reduce_scatter | solution.py:697
  269.5 373.0 %reduce-scatter.6.cloned.1.call-start = ((), (), s32[]{:S(2)}) async-start(), calls=%async_computation.7 | async-start | bytes 3833856 | tf_op jit(solution)/shard_map/reduce_scatter | solution.py:697
  346.2 298.4 %reduce-scatter.8.cloned.1.call-start = ((), (), s32[]{:S(2)}) async-start(), calls=%async_computation.8 | async-start | bytes 3833856 | tf_op jit(solution)/shard_map/reduce_scatter | solution.py:697
  346.7 36.0 %collective-permute-start.30 = (bf16[8,56,1600]{2,1,0:T(8,128)(2,1)}, bf16[8,56,1600]{2,1,0:T(8,128)(2,1)S(1)}, u32[]{:S(2)}, u32[]{:S(2)}) collective-permute-start(bf16[8,56,1600]{2,1,0:T(8,128)(2,1)} %get-tuple-element.101), channel_id=1, source_target_pairs={{0,8},{8,0},{16,24},{24,16},{1,9},{9,1},{17,25},{25,17},{2,10},{10... | collective-permute-start | bytes 4300808 | tf_op jit(solution)/shard_map/ppermute | solution.py:28
  349.1 66.7 %collective-permute-start.31 = (bf16[8,56,1600]{2,1,0:T(8,128)(2,1)}, bf16[8,56,1600]{2,1,0:T(8,128)(2,1)S(1)}, u32[]{:S(2)}, u32[]{:S(2)}) collective-permute-start(bf16[8,56,1600]{2,1,0:T(8,128)(2,1)} %get-tuple-element.102), channel_id=1, source_target_pairs={{0,16},{8,24},{16,0},{24,8},{1,17},{9,25},{17,1},{25,9},{2,18},{10... | collective-permute-start | bytes 4300808 | tf_op jit(solution)/shard_map/ppermute | solution.py:28
  350.6 65.2 %collective-permute-start.32 = (bf16[8,56,1600]{2,1,0:T(8,128)(2,1)}, bf16[8,56,1600]{2,1,0:T(8,128)(2,1)S(1)}, u32[]{:S(2)}, u32[]{:S(2)}) collective-permute-start(bf16[8,56,1600]{2,1,0:T(8,128)(2,1)} %get-tuple-element.103), channel_id=1, source_target_pairs={{0,24},{8,16},{16,8},{24,0},{1,25},{9,17},{17,9},{25,1},{2,26},{10... | collective-permute-start | bytes 4300808 | tf_op jit(solution)/shard_map/ppermute | solution.py:28
  363.7 84.2 %collective-permute-start.33 = (bf16[4,4,56,1600]{3,2,1,0:T(8,128)(2,1)}, bf16[4,4,56,1600]{3,2,1,0:T(8,128)(2,1)}, u32[]{:S(2)}, u32[]{:S(2)}) collective-permute-start(bf16[4,4,56,1600]{3,2,1,0:T(8,128)(2,1)} %get-tuple-element.114), channel_id=1, source_target_pairs={{0,1},{1,0},{2,3},{3,2},{4,5},{5,4},{6,7},{7,6},{8,9},{9,8},{10,11... | collective-permute-start | bytes 8601608 | tf_op jit(solution)/shard_map/ppermute | solution.py:28
  455.3 47.5 %collective-permute-start.34 = (bf16[8,56,1600]{2,1,0:T(8,128)(2,1)}, bf16[8,56,1600]{2,1,0:T(8,128)(2,1)S(1)}, u32[]{:S(2)}, u32[]{:S(2)}) collective-permute-start(bf16[8,56,1600]{2,1,0:T(8,128)(2,1)} %get-tuple-element.117), channel_id=1, source_target_pairs={{0,8},{8,0},{16,24},{24,16},{1,9},{9,1},{17,25},{25,17},{2,10},{10... | collective-permute-start | bytes 4300808 | tf_op jit(solution)/shard_map/ppermute | solution.py:28
  456.5 64.3 %collective-permute-start.35 = (bf16[8,56,1600]{2,1,0:T(8,128)(2,1)}, bf16[8,56,1600]{2,1,0:T(8,128)(2,1)S(1)}, u32[]{:S(2)}, u32[]{:S(2)}) collective-permute-start(bf16[8,56,1600]{2,1,0:T(8,128)(2,1)} %get-tuple-element.118), channel_id=1, source_target_pairs={{0,16},{8,24},{16,0},{24,8},{1,17},{9,25},{17,1},{25,9},{2,18},{10... | collective-permute-start | bytes 4300808 | tf_op jit(solution)/shard_map/ppermute | solution.py:28
  457.3 66.7 %collective-permute-start.36 = (bf16[8,56,1600]{2,1,0:T(8,128)(2,1)}, bf16[8,56,1600]{2,1,0:T(8,128)(2,1)S(1)}, u32[]{:S(2)}, u32[]{:S(2)}) collective-permute-start(bf16[8,56,1600]{2,1,0:T(8,128)(2,1)} %get-tuple-element.119), channel_id=1, source_target_pairs={{0,24},{8,16},{16,8},{24,0},{1,25},{9,17},{17,9},{25,1},{2,26},{10... | collective-permute-start | bytes 4300808 | tf_op jit(solution)/shard_map/ppermute | solution.py:28
  501.3 59.5 %collective-permute-start.45 = (bf16[8,56,1600]{2,1,0:T(8,128)(2,1)}, bf16[8,56,1600]{2,1,0:T(8,128)(2,1)}, u32[]{:S(2)}, u32[]{:S(2)}) collective-permute-start(bf16[8,56,1600]{2,1,0:T(8,128)(2,1)} %join_hidden.1.refs_0_), channel_id=1, source_target_pairs={{0,8},{8,0},{16,24},{24,16},{1,9},{9,1},{17,25},{25,17},{2,10},{10... | collective-permute-start | bytes 4300808 | tf_op jit(solution)/shard_map/ppermute | solution.py:28
  533.9 67.6 %collective-permute-start.49 = (bf16[8,56,1600]{2,1,0:T(8,128)(2,1)S(1)}, bf16[8,56,1600]{2,1,0:T(8,128)(2,1)}, u32[]{:S(2)}, u32[]{:S(2)}) collective-permute-start(bf16[8,56,1600]{2,1,0:T(8,128)(2,1)S(1)} %copy-done.16), channel_id=1, source_target_pairs={{0,16},{8,24},{16,0},{24,8},{1,17},{9,25},{17,1},{25,9},{2,18},{10... | collective-permute-start | bytes 4300808 | tf_op jit(solution)/shard_map/ppermute | solution.py:28
  544.3 57.2 %collective-permute-start.50 = (bf16[8,56,1600]{2,1,0:T(8,128)(2,1)S(1)}, bf16[8,56,1600]{2,1,0:T(8,128)(2,1)}, u32[]{:S(2)}, u32[]{:S(2)}) collective-permute-start(bf16[8,56,1600]{2,1,0:T(8,128)(2,1)S(1)} %copy-done.16), channel_id=1, source_target_pairs={{0,24},{8,16},{16,8},{24,0},{1,25},{9,17},{17,9},{25,1},{2,26},{10... | collective-permute-start | bytes 4300808 | tf_op jit(solution)/shard_map/ppermute | solution.py:28
  566.0 46.8 %collective-permute-start.46 = (bf16[5,56,1600]{2,1,0:T(8,128)(2,1)}, bf16[5,56,1600]{2,1,0:T(8,128)(2,1)S(1)}, u32[]{:S(2)}, u32[]{:S(2)}) collective-permute-start(bf16[5,56,1600]{2,1,0:T(8,128)(2,1)} %join_last.1.refs_0_), channel_id=1, source_target_pairs={{0,8},{8,0},{16,24},{24,16},{1,9},{9,1},{17,25},{25,17},{2,10},{10... | collective-permute-start | bytes 2688008 | tf_op jit(solution)/shard_map/ppermute | solution.py:28
  566.7 69.2 %collective-permute-start.47 = (bf16[5,56,1600]{2,1,0:T(8,128)(2,1)}, bf16[5,56,1600]{2,1,0:T(8,128)(2,1)}, u32[]{:S(2)}, u32[]{:S(2)}) collective-permute-start(bf16[5,56,1600]{2,1,0:T(8,128)(2,1)} %join_last.1.refs_0_), channel_id=1, source_target_pairs={{0,16},{8,24},{16,0},{24,8},{1,17},{9,25},{17,1},{25,9},{2,18},{10... | collective-permute-start | bytes 2688008 | tf_op jit(solution)/shard_map/ppermute | solution.py:28
  568.4 67.5 %collective-permute-start.48 = (bf16[5,56,1600]{2,1,0:T(8,128)(2,1)}, bf16[5,56,1600]{2,1,0:T(8,128)(2,1)}, u32[]{:S(2)}, u32[]{:S(2)}) collective-permute-start(bf16[5,56,1600]{2,1,0:T(8,128)(2,1)} %join_last.1.refs_0_), channel_id=1, source_target_pairs={{0,24},{8,16},{16,8},{24,0},{1,25},{9,17},{17,9},{25,1},{2,26},{10... | collective-permute-start | bytes 2688008 | tf_op jit(solution)/shard_map/ppermute | solution.py:28
  (96 other events, 1917.5 us)
Sparse Core Ops, SparseCore 0:
  9.7 52.9 all-gather.3
  113.2 55.2 all-gather.5
  212.3 39.1 all-gather.7
  269.7 41.4 reduce-scatter.3
  346.3 44.2 reduce-scatter.5
  437.5 52.0 reduce-scatter.7

commit v2 on v1

--- a/solution.py
+++ b/solution.py
@@ -345,6 +345,21 @@
     return local_call(kernel, shape, [], "assemble_rows", where, *arrays)
 
 
+def assemble_copies(where, stacks, own_rows):
+    copies, count, span, cols = stacks.shape
+    step, _ = windows(own_rows, copies, 16)
+
+    def kernel(where_ref, stacks_ref, out):
+        for copy in range(copies if step else 1):
+            for rank, bits in enumerate(ranks(count)):
+                out[where_ref[0] ^ bits, copy * step : copy * step + span, :] = stacks_ref[
+                    copy, rank
+                ]
+
+    shape = jax.ShapeDtypeStruct((count, own_rows, cols), low)
+    return local_call(kernel, shape, [], "assemble_copies", where, stacks)
+
+
 def split_heads(where, block, count, width):
     rows, cols = block.shape
 
@@ -405,27 +420,23 @@
     extra = -(-(proj_span + 16) // span)
     after = slot_rows(proj_span) - (extra - 1) * span
 
-    def kernel(where_ref, fc_ref, proj_ref, sums_ref, *outs):
-        for index, out in enumerate(outs):
-            copy = where_ref[1] ^ index
-            start = pl.multiple_of(copy * step, 16)
+    def kernel(where_ref, fc_ref, proj_ref, sums_ref, out_ref):
+        for copy in range(copies):
+            out = out_ref.at[copy]
             for bits in range(count):
                 lane = lane_of(bits, cols)
                 out[bits % SLOTS, :, lane : lane + cols] = fc_ref[
-                    where_ref[0] ^ bits, pl.ds(start, span), :
+                    where_ref[0] ^ bits, copy * step : copy * step + span, :
                 ].astype(low)
-            first = copy * proj_step
             for slot in range(extra):
                 length = min(span, proj_span - slot * span)
                 if length > 0:
-                    at = pl.multiple_of(first + slot * span, 8) if span % 8 == 0 else first
-                    out[SLOTS + slot, :length, :] = proj_ref[pl.ds(at, length), :].astype(low)
+                    at = copy * proj_step + slot * span
+                    out[SLOTS + slot, :length, :] = proj_ref[at : at + length, :].astype(low)
             out[SLOTS + extra - 1, after : after + 16, : sums.shape[2]] = sums_ref[copy].astype(low)
 
-    shape = jax.ShapeDtypeStruct((SLOTS + extra, span, D), low)
-    return local_call(
-        kernel, [shape] * copies, [], "pack_hidden", where, fc_full, proj_full, sums
-    )
+    shape = jax.ShapeDtypeStruct((copies, SLOTS + extra, span, D), low)
+    return local_call(kernel, shape, [], "pack_hidden", where, fc_full, proj_full, sums)
 
 
 def sum_hidden(where, pieces, count, cols):
@@ -748,8 +759,9 @@
     fc_stack = jnp.concatenate(
         [got[:span, :ff_cols][None] for got in fc_got] + [fc_far], 0
     )
-    fc_stacks = from_copies(fc_stack)
-    w_fc = assemble_rows(where, [[stack] for stack in fc_stacks], own_rows).reshape(D, ff_cols)
+    fc_stacks = lax.all_gather(fc_stack.reshape(count * span, ff_cols), "replica")
+    fc_stacks = fc_stacks.reshape(copies, count, span, ff_cols)
+    w_fc = assemble_copies(where, fc_stacks, own_rows).reshape(D, ff_cols)
 
     def own_heads(vector):
         vector = jnp.pad(vector, (0, count * width - D))
@@ -768,15 +780,15 @@
     queries = (projected[:, :width] + own_heads(b_query)).astype(low)
     keys = tie(projected, fc_stack)[:, width : 2 * width].astype(low)
     values = (projected[:, 2 * width :] + own_heads(b_value)).astype(low)
-    cot_all = gather_rows(tie(cotangent, queries))
     attended, log_total = attend_forward(order, queries, keys, values, heads)
 
     attended_own = order_heads(where, *exchange(list(attended.reshape(half, 2, STRETCH, width))))
+    cot_all = gather_rows(tie(cotangent, attended_own, fc_stacks))
     attended_own = attended_own[:, :D]
     in_rows = tokens.astype(full)
     middle = in_rows + mm(attended_own, w_out, 1, 0) + b_out
     second_own = layer_norm(middle, g_second, s_second).astype(low)
-    second_all = gather_rows(tie(second_own, cot_all, *fc_stacks))
+    second_all = gather_rows(tie(second_own, cot_all))
     hidden = mm(second_all, w_fc, 1, 0) + fc_bias.astype(full)
     active, pull_gelu = jax.vjp(gelu_tanh, hidden)
     active_low = active.astype(low)
@@ -793,8 +805,11 @@
     hidden_pieces = pack_hidden(
         where, fc_full.reshape(count, own_rows, ff_cols), proj_full, hidden_sums, copies
     )
-    second_grad = tie(second_grad, hidden_pieces[0])
-    hidden_pieces = to_copies(hidden_pieces)
+    second_grad = tie(second_grad, hidden_pieces)
+    hidden_shape = hidden_pieces.shape[1:]
+    hidden_sum = lax.psum_scatter(
+        hidden_pieces.reshape(-1, D), "replica", scatter_dimension=0, tiled=True
+    ).reshape(hidden_shape)
     grad_rows = cotangent.astype(full)
     _, pull_second = jax.vjp(layer_norm, middle, g_second, s_second)
     middle_part, gsecond_part, ssecond_part = pull_second(second_grad)
@@ -807,7 +822,6 @@
     attended_grad = by_rank(*exchange(attended_pairs)).reshape(count * STRETCH, width)
     outw_far = xor_send(outw_far, "shard", 1)
     output_low = tie(active_low, attended_grad)
-    attended_grad = tie(attended_grad, *hidden_pieces)
     early = jnp.stack(
         [jnp.sum(branch_low.astype(full), axis=0), jnp.sum(grad_rows, axis=0), gsecond_part, ssecond_part]
     )
@@ -848,10 +862,10 @@
     qkv_full = mm(normed_low, projected_grad, 0, 0).reshape(count, own_rows, 3 * width)
     last = pack_last(where, qkv_full, outw_near, outw_far, sums)
     first_grad = tie(first_grad, last[0])
-    hidden_pieces[0] = tie(hidden_pieces[0], last[0])
+    hidden_sum = tie(hidden_sum, last[0])
     last = to_copies(last)
 
-    fc_sums, rest = sum_hidden(where, hidden_pieces, count, ff_cols)
+    fc_sums, rest = sum_hidden(where, [hidden_sum], count, ff_cols)
     hidden_stacks = from_copies(join_hidden(where, *exchange(fc_sums), rest))
     fc_grad, proj_grad, fbias = finish_hidden(
         where, hidden_stacks, count, own_rows, ff_cols, ff_cols, hidden_sums.shape[2]
@@ -862,18 +876,20 @@
     last = [last[0]] + [xor_send(last[j], "shard", evens[j]) for j in range(1, half)]
     far = xor_send(odd_last(where, last, 3 * width), "shard", 1)
     last = from_copies(join_last(where, last, tie(far, hidden_stacks[1])))
-    qkv_grad, outw_grad, sums = finish_last(where, last, count, own_rows, width)
-    sums = sums.reshape(copies, 16 * 64)[:, :share].reshape(8, own_rows)
-
     output_part = mm(output_low, proj_weight, 1, 0).astype(low)
     output = middle + b_proj + scatter_rows(output_part).astype(full)
 
     _, pull_first = jax.vjp(lambda rows: layer_norm(rows, g_first, s_first), in_rows)
     (input_part,) = pull_first(first_grad)
     tokens_grad = (middle_grad + input_part).astype(low)
+    output = output.astype(low)
+    last[0] = tie(last[0], output, tokens_grad)
+
+    qkv_grad, outw_grad, sums = finish_last(where, last, count, own_rows, width)
+    sums = sums.reshape(copies, 16 * 64)[:, :share].reshape(8, own_rows)
     qbias, vbias, obias, pbias, gfirst, sfirst, gsecond, ssecond = sums
     return (
-        output.astype(low),
+        output,
         tokens_grad,
         qkv_grad,
         outw_grad,

time: 665 us -> 637 us (0.958)
  waiting for transfers between devices: 331 us -> 302 us
  starting transfers between devices: 76.3 us -> 65 us
    ppermute x51 -> x45, waiting for transfers between devices: 282 us -> 252 us  [xor_send(): return lax.ppermute(block, axis, [(i, i ^ bits) for i in range(count)])]
    ppermute x51 -> x45, starting transfers between devices: 74.8 us -> 64.1 us  [xor_send(): return lax.ppermute(block, axis, [(i, i ^ bits) for i in range(count)])]
    unnamed x136 -> x162, local copies, waits for them, and re-layouts: 22.8 us -> 25.3 us
  transfers between devices with their start and end apart: 57 -> 53, of which waited for: 30 -> 32; matrix products, arithmetic and copies ran while one was open for 12% -> 18% of each run, Pallas kernels for 15% -> 15%
where the time goes in v2:
time: 637 us; the launch traced here: 625 us
  waiting for transfers between devices  302 us (47%)
  Pallas kernels  96.7 us (15%)
  matrix products  73.2 us (11%)
  starting transfers between devices  65 us (10%)
  local copies, waits for them, and re-layouts  51.2 us (8%)
  other arithmetic  20.9 us (3%)
  between operations  15.4 us (2%)
    ppermute x45, waiting for transfers between devices, xor_send(): return lax.ppermute(block, axis, [(i, i ^ bits) for i in range(count)])  252 us
    pallas_call x18, Pallas kernels, local_call(): pl.pallas_call(kernel, out_shape=tuple(shapes) if many else shapes, in_sp...  77.3 us
    dot_general x12, matrix products, mm(): lax.dot_general(left_side, right_side, (((left_dim,), (right_dim,)), ((),...  72.7 us
    ppermute x45, starting transfers between devices, xor_send(): return lax.ppermute(block, axis, [(i, i ^ bits) for i in range(count)])  64.1 us
    all_gather x3, waiting for transfers between devices, gather_rows(): return lax.all_gather(block, 'shard', axis=0, tiled=True)  34.8 us
    unnamed x162, local copies, waits for them, and re-layouts  25.3 us
    reduce_scatter x3, waiting for transfers between devices, scatter_rows(): return lax.psum_scatter(blocks, 'shard', scatter_dimension=0, tiled=True)  15 us
  transfers between devices with their start and end apart: 53, of which 32 were waited for; matrix products, arithmetic and copies ran while one was open for 18% of the time, Pallas kernels for 15%

profile of v2, /device:TPU:0, one launch (start us, length us, event | category | flops | bytes accessed | tf_op | source)
XLA Modules:
  0.0 624.8 jit_solution(7979088626024184826)
XLA Ops:
  17.8 17.9 %collective-permute-done = bf16[2,56,768]{2,1,0:T(8,128)(2,1)S(1)} collective-permute-done((bf16[2,56,768]{2,1,0:T(8,128)(2,1)}, bf16[2,56,768]{2,1,0:T(8,128)(2,1)S(1)}, u32[]{:S(2)}, u32[]{:S(2)}) %collective-permute-start) | collective-permute-done | bytes 172064 | tf_op jit(solution)/shard_map/ppermute | solution.py:28
  35.7 11.6 %collective-permute-done.1 = bf16[2,56,768]{2,1,0:T(8,128)(2,1)S(1)} collective-permute-done((bf16[2,56,768]{2,1,0:T(8,128)(2,1)}, bf16[2,56,768]{2,1,0:T(8,128)(2,1)S(1)}, u32[]{:S(2)}, u32[]{:S(2)}) %collective-permute-start.1) | collective-permute-done | bytes 172064 | tf_op jit(solution)/shard_map/ppermute | solution.py:28
  61.0 19.7 %collective-permute-done.4.refs_1_ = bf16[144,1600]{1,0:T(8,128)(2,1)S(1)} collective-permute-done((bf16[144,1600]{1,0:T(8,128)(2,1)}, bf16[144,1600]{1,0:T(8,128)(2,1)S(1)}, u32[]{:S(2)}, u32[]{:S(2)}) %collective-permute-start.4) | collective-permute-done | bytes 460832 | tf_op jit(solution)/shard_map/ppermute | solution.py:28
  80.7 10.7 %collective-permute-done.5.refs_2_ = bf16[144,1600]{1,0:T(8,128)(2,1)S(1)} collective-permute-done((bf16[144,1600]{1,0:T(8,128)(2,1)}, bf16[144,1600]{1,0:T(8,128)(2,1)S(1)}, u32[]{:S(2)}, u32[]{:S(2)}) %collective-permute-start.5) | collective-permute-done | bytes 460832 | tf_op jit(solution)/shard_map/ppermute | solution.py:28
  108.6 11.3 %collective-permute-done.8.refs_1_ = bf16[8,56,768]{2,1,0:T(8,128)(2,1)S(1)} collective-permute-done((bf16[8,56,768]{2,1,0:T(8,128)(2,1)}, bf16[8,56,768]{2,1,0:T(8,128)(2,1)S(1)}, u32[]{:S(2)}, u32[]{:S(2)}) %collective-permute-start.8) | collective-permute-done | bytes 688160 | tf_op jit(solution)/shard_map/ppermute | solution.py:28
  124.9 17.7 %collective-permute-done.10.refs_3_ = bf16[8,56,768]{2,1,0:T(8,128)(2,1)} collective-permute-done((bf16[8,56,768]{2,1,0:T(8,128)(2,1)}, bf16[8,56,768]{2,1,0:T(8,128)(2,1)}, u32[]{:S(2)}, u32[]{:S(2)}) %collective-permute-start.10) | collective-permute-done | bytes 688160 | tf_op jit(solution)/shard_map/ppermute | solution.py:28
  154.0 8.5 %attend_forward.1 = (bf16[1024,256]{1,0:T(8,128)(2,1)S(1)}, f32[1,4,1024]{2,1,0:T(4,128)S(1)}) custom-call(s32[3,8]{1,0:T(4,128)S(1)} %pad_add_fusion.order_ref, bf16[1024,256]{1,0:T(8,128)(2,1)S(1)} %get-tuple-element.230.q_ref, bf16[1024,256]{1,0:T(8,128)(2,1)S(1)} %slice.248.k_ref, bf16[1024,256]{1,0:T(8,128)(2,1)S(1)} %get-tuple-element.229.v_ref), custom_call_target="tpu_custom_call" | custom-call | flops 4294967296 | bytes 2097152 | tf_op jit(solution)/shard_map/attend_forward/pallas_call | solution.py:180
  163.3 10.0 %collective-permute-start.12 = (bf16[2,128,256]{2,1,0:T(8,128)(2,1)S(1)}, bf16[2,128,256]{2,1,0:T(8,128)(2,1)S(1)}, u32[]{:S(2)}, u32[]{:S(2)}) collective-permute-start(bf16[2,128,256]{2,1,0:T(8,128)(2,1)S(1)} %bitcast.103), channel_id=1, source_target_pairs={{0,2},{1,3},{2,0},{3,1},{4,6},{5,7},{6,4},{7,5},{8,10},{9,11},{10,... | collective-permute-start | bytes 393224 | tf_op jit(solution)/shard_map/ppermute | solution.py:28
  193.5 16.3 %collective-permute-done.17.refs_2_ = bf16[4,56,1600]{2,1,0:T(8,128)(2,1)} collective-permute-done((bf16[4,56,1600]{2,1,0:T(8,128)(2,1)}, bf16[4,56,1600]{2,1,0:T(8,128)(2,1)}, u32[]{:S(2)}, u32[]{:S(2)}) %collective-permute-start.17) | collective-permute-done | bytes 716832 | tf_op jit(solution)/shard_map/ppermute | solution.py:28
  209.9 16.3 %collective-permute-done.19.refs_4_ = bf16[4,56,1600]{2,1,0:T(8,128)(2,1)} collective-permute-done((bf16[4,56,1600]{2,1,0:T(8,128)(2,1)}, bf16[4,56,1600]{2,1,0:T(8,128)(2,1)}, u32[]{:S(2)}, u32[]{:S(2)}) %collective-permute-start.19) | collective-permute-done | bytes 716832 | tf_op jit(solution)/shard_map/ppermute | solution.py:28
  246.6 34.8 %all-gather.11.cloned.1.call-done = bf16[1024,1600]{1,0:T(8,128)(2,1)} async-done(((bf16[128,1600]{1,0:T(8,128)(2,1)}), bf16[1024,1600]{1,0:T(8,128)(2,1)}) %all-gather.11.cloned.1.call-update) | async-done | bytes 3276816 | tf_op jit(solution)/shard_map/all_gather | solution.py:704
  304.9 8.4 %fusion.61.proj_ref = f32[800,1600]{1,0:T(8,128)} fusion(bf16[1024,800]{0,1:T(8,128)(2,1)} %get-tuple-element.95, bf16[1024,1600]{0,1:T(8,128)(2,1)} %all-gather.9.cloned.1.call-done), kind=kOutput, calls=%fused_computation.145 | convolution fusion | flops 2621440000 | bytes 10035200 | tf_op jit(solution)/shard_map/dot_general | solution.py:49
  318.8 7.8 %pack_hidden.1 = bf16[4,8,56,1600]{3,2,1,0:T(8,128)(2,1)} custom-call(s32[2]{0:T(128)} %pad_add_fusion.1.where_ref, f32[8,200,800]{2,1,0:T(8,128)} %bitcast.90, f32[800,1600]{1,0:T(8,128)} %fusion.61.proj_ref, f32[4,16,256]{2,1,0:T(8,128)} %pad.22.sums_ref), custom_call_target="tpu_custom_call" | custom-call | bytes 30916608 | tf_op jit(solution)/shard_map/pack_hidden/pallas_call | solution.py:240
  328.6 15.0 %reduce-scatter.5.cloned.1.call-done = bf16[128,1600]{1,0:T(8,128)(2,1)} async-done(((bf16[1024,1600]{1,0:T(8,128)(2,1)}), bf16[128,1600]{1,0:T(8,128)(2,1)}) %reduce-scatter.5.cloned.1.call-update) | async-done | bytes 409616 | tf_op jit(solution)/shard_map/reduce_scatter | solution.py:708
  383.2 10.9 %attend_backward.1 = (bf16[1024,256]{1,0:T(8,128)(2,1)S(1)}, bf16[1024,256]{1,0:T(8,128)(2,1)S(1)}, bf16[1024,256]{1,0:T(8,128)(2,1)S(1)}) custom-call(s32[3,8]{1,0:T(4,128)S(1)} %pad_add_fusion.order_ref, bf16[1024,256]{1,0:T(8,128)(2,1)S(1)} %copy-done.7, bf16[1024,256]{1,0:T(8,128)(2,1)S(1)} %copy-done.3, bf16[1024,256]{1,0:T(8,128)(2,1)S(1)} %copy-done.5, ...), custom_call_target="tpu_custom_call" | custom-call | flops 10737418240 | bytes 3670016 | tf_op jit(solution)/shard_map/attend_backward/pallas_call | solution.py:203
  423.4 7.8 %fusion.40 = f32[1600,768]{1,0:T(8,128)} fusion(bf16[1024,768]{1,0:T(8,128)(2,1)} %copy-done.45, bf16[1024,1600]{0,1:T(8,128)(2,1)} %all-gather.5.cloned.1.call-done, f32[1600]{0:T(1024)S(1)} %copy-done.52, f32[1600]{0:T(1024)S(1)} %mul.199, f32[1024]{0:T(1024)S(1)} %copy-done.57, f32[1024]{0:T(1024)S(1)} %broadcast_multiply_fusion), kind=kOutput, calls=%fused_computation.128 | convolution fusion | flops 2526412800 | bytes 9785856 | tf_op jit(solution)/shard_map/dot_general | solution.py:49
  447.8 11.3 %collective-permute-done.37.refs_3_ = bf16[2,56,800]{2,1,0:T(8,128)(2,1)S(1)} collective-permute-done((bf16[2,56,800]{2,1,0:T(8,128)(2,1)}, bf16[2,56,800]{2,1,0:T(8,128)(2,1)S(1)}, u32[]{:S(2)}, u32[]{:S(2)}) %collective-permute-start.37) | collective-permute-done | bytes 179232 | tf_op jit(solution)/shard_map/ppermute | solution.py:28
  459.0 9.6 %collective-permute-start.35 = (bf16[2,56,800]{2,1,0:T(8,128)(2,1)}, bf16[2,56,800]{2,1,0:T(8,128)(2,1)S(1)}, u32[]{:S(2)}, u32[]{:S(2)}) collective-permute-start(bf16[2,56,800]{2,1,0:T(8,128)(2,1)} %get-tuple-element.117), channel_id=1, source_target_pairs={{0,2},{1,3},{2,0},{3,1},{4,6},{5,7},{6,4},{7,5},{8,10},{9,11},{10,... | collective-permute-start | bytes 537608 | tf_op jit(solution)/shard_map/ppermute | solution.py:28
  485.9 21.5 %collective-permute-done.29.refs_2_ = bf16[8,56,1600]{2,1,0:T(8,128)(2,1)} collective-permute-done((bf16[8,56,1600]{2,1,0:T(8,128)(2,1)}, bf16[8,56,1600]{2,1,0:T(8,128)(2,1)}, u32[]{:S(2)}, u32[]{:S(2)}) %collective-permute-start.29) | collective-permute-done | bytes 1433632 | tf_op jit(solution)/shard_map/ppermute | solution.py:28
  515.7 15.8 %collective-permute-done.31.refs_1_ = bf16[2,56,1600]{2,1,0:T(8,128)(2,1)S(1)} collective-permute-done((bf16[2,56,1600]{2,1,0:T(8,128)(2,1)}, bf16[2,56,1600]{2,1,0:T(8,128)(2,1)S(1)}, u32[]{:S(2)}, u32[]{:S(2)}) %collective-permute-start.31) | collective-permute-done | bytes 358432 | tf_op jit(solution)/shard_map/ppermute | solution.py:28
  533.4 10.1 %collective-permute-done.33.refs_3_ = bf16[2,56,1600]{2,1,0:T(8,128)(2,1)S(1)} collective-permute-done((bf16[2,56,1600]{2,1,0:T(8,128)(2,1)}, bf16[2,56,1600]{2,1,0:T(8,128)(2,1)S(1)}, u32[]{:S(2)}, u32[]{:S(2)}) %collective-permute-start.33) | collective-permute-done | bytes 358432 | tf_op jit(solution)/shard_map/ppermute | solution.py:28
  555.1 16.2 %collective-permute-done.43.refs_2_ = bf16[8,56,1600]{2,1,0:T(8,128)(2,1)} collective-permute-done((bf16[8,56,1600]{2,1,0:T(8,128)(2,1)}, bf16[8,56,1600]{2,1,0:T(8,128)(2,1)}, u32[]{:S(2)}, u32[]{:S(2)}) %collective-permute-start.43) | collective-permute-done | bytes 1433632 | tf_op jit(solution)/shard_map/ppermute | solution.py:28
  571.7 9.7 %finish_hidden.1 = (f32[200,6400]{1,0:T(8,128)}, f32[800,1600]{1,0:T(8,128)}, f32[4,16,256]{2,1,0:T(8,128)}) custom-call(s32[2]{0:T(128)} %pad_add_fusion.1.where_ref, bf16[8,56,1600]{2,1,0:T(8,128)(2,1)} %join_hidden.1.refs_0_, bf16[8,56,1600]{2,1,0:T(8,128)(2,1)} %collective-permute-done.39.refs_1_, bf16[8,56,1600]{2,1,0:T(8,128)(2,1)} %collective-permute-done.43.refs_2_, ...), custom_call_target="tpu_custom_call" | custom-call | bytes 17203200 | tf_op jit(solution)/shard_map/finish_hidden/pallas_call | solution.py:240
  592.9 18.3 %collective-permute-done.41.refs_2_ = bf16[5,56,1600]{2,1,0:T(8,128)(2,1)} collective-permute-done((bf16[5,56,1600]{2,1,0:T(8,128)(2,1)}, bf16[5,56,1600]{2,1,0:T(8,128)(2,1)}, u32[]{:S(2)}, u32[]{:S(2)}) %collective-permute-start.41) | collective-permute-done | bytes 896032 | tf_op jit(solution)/shard_map/ppermute | solution.py:28
  (392 shorter events, 272.3 us)
Async XLA Ops:
  7.3 138.7 %all-gather.5.cloned.1.call-start = ((), (), s32[]{:S(2)}) async-start(), calls=%async_computation.4 | async-start | bytes 3686400 | tf_op jit(solution)/shard_map/all_gather | solution.py:704
  8.0 181.9 %all-gather.7.cloned.1.call-start = ((), (), s32[]{:S(2)}) async-start(), calls=%async_computation.5 | async-start | bytes 4014080 | tf_op jit(solution)/shard_map/all_gather | solution.py:762
  11.2 36.1 %collective-permute-start.2 = (bf16[2,56,768]{2,1,0:T(8,128)(2,1)}, bf16[2,56,768]{2,1,0:T(8,128)(2,1)S(1)}, u32[]{:S(2)}, u32[]{:S(2)}) collective-permute-start(bf16[2,56,768]{2,1,0:T(8,128)(2,1)} %get-tuple-element.75), channel_id=1, source_target_pairs={{0,6},{1,7},{2,4},{3,5},{4,2},{5,3},{6,0},{7,1},{8,14},{9,15},{10,... | collective-permute-start | bytes 516104 | tf_op jit(solution)/shard_map/ppermute | solution.py:28
  55.5 35.8 %collective-permute-start.5 = (bf16[144,1600]{1,0:T(8,128)(2,1)}, bf16[144,1600]{1,0:T(8,128)(2,1)S(1)}, u32[]{:S(2)}, u32[]{:S(2)}) collective-permute-start(bf16[144,1600]{1,0:T(8,128)(2,1)} %get-tuple-element.79), channel_id=1, source_target_pairs={{0,4},{1,5},{2,6},{3,7},{4,0},{5,1},{6,2},{7,3},{8,12},{9,13},{10,... | collective-permute-start | bytes 1382408 | tf_op jit(solution)/shard_map/ppermute | solution.py:28
  57.6 33.8 %collective-permute-start.6 = (bf16[144,1600]{1,0:T(8,128)(2,1)}, bf16[144,1600]{1,0:T(8,128)(2,1)S(1)}, u32[]{:S(2)}, u32[]{:S(2)}) collective-permute-start(bf16[144,1600]{1,0:T(8,128)(2,1)} %get-tuple-element.80), channel_id=1, source_target_pairs={{0,6},{1,7},{2,4},{3,5},{4,2},{5,3},{6,0},{7,1},{8,14},{9,15},{10,... | collective-permute-start | bytes 1382408 | tf_op jit(solution)/shard_map/ppermute | solution.py:28
  99.3 142.3 %all-gather.9.cloned.1.call-start = ((), (), s32[]{:S(2)}) async-start(), calls=%async_computation.6 | async-start | bytes 3686400 | tf_op jit(solution)/shard_map/all_gather | solution.py:704
  103.1 39.5 %collective-permute-start.10 = (bf16[8,56,768]{2,1,0:T(8,128)(2,1)}, bf16[8,56,768]{2,1,0:T(8,128)(2,1)}, u32[]{:S(2)}, u32[]{:S(2)}) collective-permute-start(bf16[8,56,768]{2,1,0:T(8,128)(2,1)} %copy-done.31), channel_id=1, source_target_pairs={{0,24},{8,16},{16,8},{24,0},{1,25},{9,17},{17,9},{25,1},{2,26},{10... | collective-permute-start | bytes 2064392 | tf_op jit(solution)/shard_map/ppermute | solution.py:28
  189.9 91.5 %all-gather.11.cloned.1.call-start = ((), (), s32[]{:S(2)}) async-start(), calls=%async_computation.7 | async-start | bytes 3833856 | tf_op jit(solution)/shard_map/all_gather | solution.py:704
  191.4 34.7 %collective-permute-start.19 = (bf16[4,56,1600]{2,1,0:T(8,128)(2,1)}, bf16[4,56,1600]{2,1,0:T(8,128)(2,1)}, u32[]{:S(2)}, u32[]{:S(2)}) collective-permute-start(bf16[4,56,1600]{2,1,0:T(8,128)(2,1)} %get-tuple-element.85.refs_0_), channel_id=1, source_target_pairs={{0,16},{8,24},{16,0},{24,8},{1,17},{9,25},{17,1},{25,9},{2,18},{10... | collective-permute-start | bytes 2150408 | tf_op jit(solution)/shard_map/ppermute | solution.py:28
  192.4 33.8 %collective-permute-start.21 = (bf16[4,56,1600]{2,1,0:T(8,128)(2,1)}, bf16[4,56,1600]{2,1,0:T(8,128)(2,1)}, u32[]{:S(2)}, u32[]{:S(2)}) collective-permute-start(bf16[4,56,1600]{2,1,0:T(8,128)(2,1)} %get-tuple-element.85.refs_0_), channel_id=1, source_target_pairs={{0,24},{8,16},{16,8},{24,0},{1,25},{9,17},{17,9},{25,1},{2,26},{10... | collective-permute-start | bytes 2150408 | tf_op jit(solution)/shard_map/ppermute | solution.py:28
  193.5 35.6 %collective-permute-start.16 = (bf16[4,56,1600]{2,1,0:T(8,128)(2,1)}, bf16[4,56,1600]{2,1,0:T(8,128)(2,1)}, u32[]{:S(2)}, u32[]{:S(2)}) collective-permute-start(bf16[4,56,1600]{2,1,0:T(8,128)(2,1)} %get-tuple-element.85.refs_0_), channel_id=1, source_target_pairs={{0,1},{1,0},{2,3},{3,2},{4,5},{5,4},{6,7},{7,6},{8,9},{9,8},{10,11... | collective-permute-start | bytes 2150408 | tf_op jit(solution)/shard_map/ppermute | solution.py:28
  241.6 102.0 %reduce-scatter.5.cloned.1.call-start = ((), (), s32[]{:S(2)}) async-start(), calls=%async_computation.8 | async-start | bytes 3833856 | tf_op jit(solution)/shard_map/reduce_scatter | solution.py:708
  302.0 140.1 %reduce-scatter.11.cloned.1.call-start = ((), (), s32[]{:S(2)}) async-start(), calls=%async_computation.11 | async-start | bytes 7454720 | tf_op jit(solution)/shard_map/reduce_scatter | solution.py:810
  326.6 256.3 %reduce-scatter.7.cloned.1.call-start = ((), (), s32[]{:S(2)}) async-start(), calls=%async_computation.9 | async-start | bytes 3833856 | tf_op jit(solution)/shard_map/reduce_scatter | solution.py:708
  378.6 208.3 %reduce-scatter.9.cloned.1.call-start = ((), (), s32[]{:S(2)}) async-start(), calls=%async_computation.10 | async-start | bytes 3833856 | tf_op jit(solution)/shard_map/reduce_scatter | solution.py:708
  438.6 46.6 %collective-permute-start.28 = (bf16[8,56,1600]{2,1,0:T(8,128)(2,1)}, bf16[8,56,1600]{2,1,0:T(8,128)(2,1)}, u32[]{:S(2)}, u32[]{:S(2)}) collective-permute-start(bf16[8,56,1600]{2,1,0:T(8,128)(2,1)} %get-tuple-element.108), channel_id=1, source_target_pairs={{0,8},{8,0},{16,24},{24,16},{1,9},{9,1},{17,25},{25,17},{2,10},{10... | collective-permute-start | bytes 4300808 | tf_op jit(solution)/shard_map/ppermute | solution.py:28
  440.6 66.8 %collective-permute-start.29 = (bf16[8,56,1600]{2,1,0:T(8,128)(2,1)}, bf16[8,56,1600]{2,1,0:T(8,128)(2,1)}, u32[]{:S(2)}, u32[]{:S(2)}) collective-permute-start(bf16[8,56,1600]{2,1,0:T(8,128)(2,1)} %get-tuple-element.109), channel_id=1, source_target_pairs={{0,16},{8,24},{16,0},{24,8},{1,17},{9,25},{17,1},{25,9},{2,18},{10... | collective-permute-start | bytes 4300808 | tf_op jit(solution)/shard_map/ppermute | solution.py:28
  442.1 65.7 %collective-permute-start.30 = (bf16[8,56,1600]{2,1,0:T(8,128)(2,1)}, bf16[8,56,1600]{2,1,0:T(8,128)(2,1)}, u32[]{:S(2)}, u32[]{:S(2)}) collective-permute-start(bf16[8,56,1600]{2,1,0:T(8,128)(2,1)} %get-tuple-element.110), channel_id=1, source_target_pairs={{0,24},{8,16},{16,8},{24,0},{1,25},{9,17},{17,9},{25,1},{2,26},{10... | collective-permute-start | bytes 4300808 | tf_op jit(solution)/shard_map/ppermute | solution.py:28
  482.4 66.0 %collective-permute-start.39 = (bf16[8,56,1600]{2,1,0:T(8,128)(2,1)}, bf16[8,56,1600]{2,1,0:T(8,128)(2,1)}, u32[]{:S(2)}, u32[]{:S(2)}) collective-permute-start(bf16[8,56,1600]{2,1,0:T(8,128)(2,1)} %join_hidden.1.refs_0_), channel_id=1, source_target_pairs={{0,8},{8,0},{16,24},{24,16},{1,9},{9,1},{17,25},{25,17},{2,10},{10... | collective-permute-start | bytes 4300808 | tf_op jit(solution)/shard_map/ppermute | solution.py:28
  483.9 87.4 %collective-permute-start.43 = (bf16[8,56,1600]{2,1,0:T(8,128)(2,1)}, bf16[8,56,1600]{2,1,0:T(8,128)(2,1)}, u32[]{:S(2)}, u32[]{:S(2)}) collective-permute-start(bf16[8,56,1600]{2,1,0:T(8,128)(2,1)} %join_hidden.1.refs_0_), channel_id=1, source_target_pairs={{0,16},{8,24},{16,0},{24,8},{1,17},{9,25},{17,1},{25,9},{2,18},{10... | collective-permute-start | bytes 4300808 | tf_op jit(solution)/shard_map/ppermute | solution.py:28
  485.3 86.5 %collective-permute-start.44 = (bf16[8,56,1600]{2,1,0:T(8,128)(2,1)}, bf16[8,56,1600]{2,1,0:T(8,128)(2,1)}, u32[]{:S(2)}, u32[]{:S(2)}) collective-permute-start(bf16[8,56,1600]{2,1,0:T(8,128)(2,1)} %join_hidden.1.refs_0_), channel_id=1, source_target_pairs={{0,24},{8,16},{16,8},{24,0},{1,25},{9,17},{17,9},{25,1},{2,26},{10... | collective-permute-start | bytes 4300808 | tf_op jit(solution)/shard_map/ppermute | solution.py:28
  551.6 41.3 %collective-permute-start.40 = (bf16[5,56,1600]{2,1,0:T(8,128)(2,1)}, bf16[5,56,1600]{2,1,0:T(8,128)(2,1)}, u32[]{:S(2)}, u32[]{:S(2)}) collective-permute-start(bf16[5,56,1600]{2,1,0:T(8,128)(2,1)} %join_last.1.refs_0_), channel_id=1, source_target_pairs={{0,8},{8,0},{16,24},{24,16},{1,9},{9,1},{17,25},{25,17},{2,10},{10... | collective-permute-start | bytes 2688008 | tf_op jit(solution)/shard_map/ppermute | solution.py:28
  553.1 58.1 %collective-permute-start.41 = (bf16[5,56,1600]{2,1,0:T(8,128)(2,1)}, bf16[5,56,1600]{2,1,0:T(8,128)(2,1)}, u32[]{:S(2)}, u32[]{:S(2)}) collective-permute-start(bf16[5,56,1600]{2,1,0:T(8,128)(2,1)} %join_last.1.refs_0_), channel_id=1, source_target_pairs={{0,16},{8,24},{16,0},{24,8},{1,17},{9,25},{17,1},{25,9},{2,18},{10... | collective-permute-start | bytes 2688008 | tf_op jit(solution)/shard_map/ppermute | solution.py:28
  554.9 56.4 %collective-permute-start.42 = (bf16[5,56,1600]{2,1,0:T(8,128)(2,1)}, bf16[5,56,1600]{2,1,0:T(8,128)(2,1)}, u32[]{:S(2)}, u32[]{:S(2)}) collective-permute-start(bf16[5,56,1600]{2,1,0:T(8,128)(2,1)} %join_last.1.refs_0_), channel_id=1, source_target_pairs={{0,24},{8,16},{16,8},{24,0},{1,25},{9,17},{17,9},{25,1},{2,26},{10... | collective-permute-start | bytes 2688008 | tf_op jit(solution)/shard_map/ppermute | solution.py:28
  (105 other events, 1780.2 us)
Sparse Core Ops, SparseCore 0:
  9.7 52.9 all-gather.4
  99.4 74.0 all-gather.6
  190.1 39.6 all-gather.8
  241.7 39.6 all-gather.10
  302.1 41.4 reduce-scatter.4
  346.5 66.1 reduce-scatter.10
  415.5 49.7 reduce-scatter.6
  467.6 50.7 reduce-scatter.8

commit v3 on v2

--- a/solution.py
+++ b/solution.py
@@ -749,11 +749,12 @@
     vectors = lax.dot(chosen, vectors, precision=lax.Precision.HIGHEST)
     vectors = vectors.reshape(count, 8, own_rows).transpose(1, 0, 2).reshape(8, D)
     b_query, b_value, b_out, b_proj, g_first, s_first, g_second, s_second = vectors
-    qkv_stacks = from_copies(qkv_stack)
-    w_qkv = assemble_rows(where, [[stack] for stack in qkv_stacks], own_rows)
+    qkv_stacks = lax.all_gather(qkv_stack.reshape(count * span, 3 * width), "replica")
+    qkv_stacks = qkv_stacks.reshape(copies, count, span, 3 * width)
+    w_qkv = assemble_copies(where, qkv_stacks, own_rows)
     w_qkv = w_qkv.reshape(D, 3 * width)
 
-    out_near = from_copies(tie(out_near, *qkv_stacks))
+    out_near = from_copies(out_near)
     out_far = [xor_send(block, "shard", 1) for block in out_near]
     w_out = assemble_rows(where, list(zip(out_near, out_far)), own_rows).reshape(D, D)
     fc_stack = jnp.concatenate(
@@ -782,6 +783,7 @@
     values = (projected[:, 2 * width :] + own_heads(b_value)).astype(low)
     attended, log_total = attend_forward(order, queries, keys, values, heads)
 
+    attended = tie(attended, *out_near)
     attended_own = order_heads(where, *exchange(list(attended.reshape(half, 2, STRETCH, width))))
     cot_all = gather_rows(tie(cotangent, attended_own, fc_stacks))
     attended_own = attended_own[:, :D]
@@ -821,7 +823,6 @@
     outw_near, outw_far = split_outw(where, outw_full.reshape(count, own_rows, D), copies)
     attended_grad = by_rank(*exchange(attended_pairs)).reshape(count * STRETCH, width)
     outw_far = xor_send(outw_far, "shard", 1)
-    output_low = tie(active_low, attended_grad)
     early = jnp.stack(
         [jnp.sum(branch_low.astype(full), axis=0), jnp.sum(grad_rows, axis=0), gsecond_part, ssecond_part]
     )
@@ -876,7 +877,7 @@
     last = [last[0]] + [xor_send(last[j], "shard", evens[j]) for j in range(1, half)]
     far = xor_send(odd_last(where, last, 3 * width), "shard", 1)
     last = from_copies(join_last(where, last, tie(far, hidden_stacks[1])))
-    output_part = mm(output_low, proj_weight, 1, 0).astype(low)
+    output_part = mm(tie(active_low, fc_sums[0]), proj_weight, 1, 0).astype(low)
     output = middle + b_proj + scatter_rows(output_part).astype(full)
 
     _, pull_first = jax.vjp(lambda rows: layer_norm(rows, g_first, s_first), in_rows)

time: 637 us -> 599 us (0.940); the launches traced: 625 us -> 595 us
  starting transfers between devices: 65 us -> 48.1 us
  waiting for transfers between devices: 302 us -> 288 us
    ppermute x45 -> x42, waiting for transfers between devices: 252 us -> 182 us  [xor_send(): return lax.ppermute(block, axis, [(i, i ^ bits) for i in range(count)])]
    all_gather x3, waiting for transfers between devices: 34.8 us -> 79.2 us  [gather_rows(): return lax.all_gather(block, 'shard', axis=0, tiled=True)]
    ppermute x45 -> x42, starting transfers between devices: 64.1 us -> 47.4 us  [xor_send(): return lax.ppermute(block, axis, [(i, i ^ bits) for i in range(count)])]
    all_gather x1, waiting for transfers between devices: 0.01 us -> 11.3 us  [on_device(): lax.all_gather(fc_stack.reshape(count * span, ff_cols), 'replica')]
  transfers between devices with their start and end apart: 53 -> 51, of which waited for: 32 -> 29; matrix products, arithmetic and copies ran while one was open for 18% -> 18% of each run, Pallas kernels for 15% -> 15%
where the time goes in v3:
time: 599 us; the launch traced here: 595 us
  waiting for transfers between devices  288 us (48%)
  Pallas kernels  97.3 us (16%)
  matrix products  72.9 us (12%)
  local copies, waits for them, and re-layouts  50.5 us (8%)
  starting transfers between devices  48.1 us (8%)
  other arithmetic  22.5 us (4%)
  between operations  15.2 us (3%)
    ppermute x42, waiting for transfers between devices, xor_send(): return lax.ppermute(block, axis, [(i, i ^ bits) for i in range(count)])  182 us
    all_gather x3, waiting for transfers between devices, gather_rows(): return lax.all_gather(block, 'shard', axis=0, tiled=True)  79.2 us
    pallas_call x18, Pallas kernels, local_call(): pl.pallas_call(kernel, out_shape=tuple(shapes) if many else shapes, in_sp...  77.6 us
    dot_general x12, matrix products, mm(): lax.dot_general(left_side, right_side, (((left_dim,), (right_dim,)), ((),...  72.5 us
    ppermute x42, starting transfers between devices, xor_send(): return lax.ppermute(block, axis, [(i, i ^ bits) for i in range(count)])  47.4 us
    unnamed x162, local copies, waits for them, and re-layouts  26.6 us
    reduce_scatter x3, waiting for transfers between devices, scatter_rows(): return lax.psum_scatter(blocks, 'shard', scatter_dimension=0, tiled=True)  15 us
  transfers between devices with their start and end apart: 51, of which 29 were waited for; matrix products, arithmetic and copies ran while one was open for 18% of the time, Pallas kernels for 15%

profile of v3, /device:TPU:0, one launch (start us, length us, event | category | flops | bytes accessed | tf_op | source)
XLA Modules:
  0.0 594.9 jit_solution(1383930308103059957)
XLA Ops:
  20.9 8.5 %collective-permute-done.1 = bf16[2,56,768]{2,1,0:T(8,128)(2,1)S(1)} collective-permute-done((bf16[2,56,768]{2,1,0:T(8,128)(2,1)}, bf16[2,56,768]{2,1,0:T(8,128)(2,1)S(1)}, u32[]{:S(2)}, u32[]{:S(2)}) %collective-permute-start.1) | collective-permute-done | bytes 172064 | tf_op jit(solution)/shard_map/ppermute | solution.py:28
  44.3 17.6 %collective-permute-done.4.refs_1_ = bf16[144,1600]{1,0:T(8,128)(2,1)S(1)} collective-permute-done((bf16[144,1600]{1,0:T(8,128)(2,1)}, bf16[144,1600]{1,0:T(8,128)(2,1)S(1)}, u32[]{:S(2)}, u32[]{:S(2)}) %collective-permute-start.4) | collective-permute-done | bytes 460832 | tf_op jit(solution)/shard_map/ppermute | solution.py:28
  62.0 14.3 %collective-permute-done.5.refs_2_ = bf16[144,1600]{1,0:T(8,128)(2,1)S(1)} collective-permute-done((bf16[144,1600]{1,0:T(8,128)(2,1)}, bf16[144,1600]{1,0:T(8,128)(2,1)S(1)}, u32[]{:S(2)}, u32[]{:S(2)}) %collective-permute-start.5) | collective-permute-done | bytes 460832 | tf_op jit(solution)/shard_map/ppermute | solution.py:28
  96.5 19.8 %all-gather.6.cloned.1.call-done = bf16[1024,1600]{0,1:T(8,128)(2,1)} async-done(((bf16[128,1600]{0,1:T(8,128)(2,1)}), bf16[1024,1600]{0,1:T(8,128)(2,1)}) %all-gather.6.cloned.1.call-update) | async-done | bytes 3276816 | tf_op jit(solution)/shard_map/all_gather | solution.py:704
  124.4 8.6 %attend_forward.1 = (bf16[1024,256]{1,0:T(8,128)(2,1)S(1)}, f32[1,4,1024]{2,1,0:T(4,128)S(1)}) custom-call(s32[3,8]{1,0:T(4,128)S(1)} %pad_add_fusion.order_ref, bf16[1024,256]{1,0:T(8,128)(2,1)S(1)} %get-tuple-element.230.q_ref, bf16[1024,256]{1,0:T(8,128)(2,1)S(1)} %slice.248.k_ref, bf16[1024,256]{1,0:T(8,128)(2,1)S(1)} %get-tuple-element.229.v_ref), custom_call_target="tpu_custom_call" | custom-call | flops 4294967296 | bytes 2097152 | tf_op jit(solution)/shard_map/attend_forward/pallas_call | solution.py:180
  141.0 7.6 %collective-permute-done.13.refs_2_ = bf16[2,128,256]{2,1,0:T(8,128)(2,1)S(1)} collective-permute-done((bf16[2,128,256]{2,1,0:T(8,128)(2,1)S(1)}, bf16[2,128,256]{2,1,0:T(8,128)(2,1)S(1)}, u32[]{:S(2)}, u32[]{:S(2)}) %collective-permute-start.13) | collective-permute-done | bytes 131104 | tf_op jit(solution)/shard_map/ppermute | solution.py:28
  153.3 11.3 %all-gather.10.cloned.1.call-done = bf16[4,448,800]{2,1,0:T(8,128)(2,1)} async-done(((bf16[1,448,800]{2,1,0:T(8,128)(2,1)}), bf16[4,448,800]{2,1,0:T(8,128)(2,1)}) %all-gather.10.cloned.1.call-update) | async-done | bytes 2867216 | tf_op jit(solution)/shard_map/all_gather | solution.py:763
  182.1 24.2 %all-gather.12.cloned.1.call-done = bf16[1024,1600]{0,1:T(8,128)(2,1)} async-done(((bf16[128,1600]{0,1:T(8,128)(2,1)}), bf16[1024,1600]{0,1:T(8,128)(2,1)}) %all-gather.12.cloned.1.call-update) | async-done | bytes 3276816 | tf_op jit(solution)/shard_map/all_gather | solution.py:704
  211.4 35.1 %all-gather.14.cloned.1.call-done = bf16[1024,1600]{1,0:T(8,128)(2,1)} async-done(((bf16[128,1600]{1,0:T(8,128)(2,1)}), bf16[1024,1600]{1,0:T(8,128)(2,1)}) %all-gather.14.cloned.1.call-update) | async-done | bytes 3276816 | tf_op jit(solution)/shard_map/all_gather | solution.py:704
  252.8 7.6 %convert_reduce_fusion.1 = (f32[800]{0:T(1024)}, bf16[1024,800]{0,1:T(8,128)(2,1)S(1)}, bf16[1024,800]{0,1:T(8,128)(2,1)}) fusion(f32[1024,800]{0,1:T(8,128)S(1)} %fusion.59, f32[800]{0:T(1024)S(1)} %copy-done.53, bf16[800,1600]{1,0:T(8,128)(2,1)S(1)} %copy-done, bf16[1024,1600]{0,1:T(8,128)(2,1)S(1)} %copy-done.71), kind=kOutput, calls=%fused_computation.22 | convolution fusion | flops 2645196032 | bytes 12396800 | tf_op jit(solution)/shard_map/dot_general | solution.py:49
  270.0 8.3 %fusion.61.proj_ref = f32[800,1600]{1,0:T(8,128)} fusion(bf16[1024,800]{0,1:T(8,128)(2,1)} %get-tuple-element.108, bf16[1024,1600]{0,1:T(8,128)(2,1)} %all-gather.12.cloned.1.call-done), kind=kOutput, calls=%fused_computation.145 | convolution fusion | flops 2621440000 | bytes 10035200 | tf_op jit(solution)/shard_map/dot_general | solution.py:49
  283.8 7.8 %pack_hidden.1 = bf16[4,8,56,1600]{3,2,1,0:T(8,128)(2,1)} custom-call(s32[2]{0:T(128)} %pad_add_fusion.1.where_ref, f32[8,200,800]{2,1,0:T(8,128)} %bitcast.92, f32[800,1600]{1,0:T(8,128)} %fusion.61.proj_ref, f32[4,16,256]{2,1,0:T(8,128)} %pad.22.sums_ref), custom_call_target="tpu_custom_call" | custom-call | bytes 30916608 | tf_op jit(solution)/shard_map/pack_hidden/pallas_call | solution.py:240
  293.8 15.0 %reduce-scatter.7.cloned.1.call-done = bf16[128,1600]{1,0:T(8,128)(2,1)} async-done(((bf16[1024,1600]{1,0:T(8,128)(2,1)}), bf16[128,1600]{1,0:T(8,128)(2,1)}) %reduce-scatter.7.cloned.1.call-update) | async-done | bytes 409616 | tf_op jit(solution)/shard_map/reduce_scatter | solution.py:708
  340.1 11.1 %attend_backward.1 = (bf16[1024,256]{1,0:T(8,128)(2,1)S(1)}, bf16[1024,256]{1,0:T(8,128)(2,1)S(1)}, bf16[1024,256]{1,0:T(8,128)(2,1)S(1)}) custom-call(s32[3,8]{1,0:T(4,128)S(1)} %pad_add_fusion.order_ref, bf16[1024,256]{1,0:T(8,128)(2,1)S(1)} %copy-done.7, bf16[1024,256]{1,0:T(8,128)(2,1)S(1)} %copy-done.3, bf16[1024,256]{1,0:T(8,128)(2,1)S(1)} %copy-done.5, ...), custom_call_target="tpu_custom_call" | custom-call | flops 10737418240 | bytes 3670016 | tf_op jit(solution)/shard_map/attend_backward/pallas_call | solution.py:203
  368.8 7.4 %split_outw.1 = (bf16[4,56,1600]{2,1,0:T(8,128)(2,1)}, bf16[4,56,1600]{2,1,0:T(8,128)(2,1)}, bf16[4,56,1600]{2,1,0:T(8,128)(2,1)}, bf16[4,56,1600]{2,1,0:T(8,128)(2,1)}, bf16[4,4,56,1600]{3,2,1,0:T(8,128)(2,1)}) custom-call(s32[2]{0:T(128)} %pad_add_fusion.1.where_ref, f32[8,200,1600]{2,1,0:T(8,128)} %bitcast.88), custom_call_target="tpu_custom_call" | custom-call | bytes 30720000 | tf_op jit(solution)/shard_map/split_outw/pallas_call | solution.py:240
  380.3 7.8 %fusion.40 = f32[1600,768]{1,0:T(8,128)} fusion(bf16[1024,768]{1,0:T(8,128)(2,1)} %copy-done.43, bf16[1024,1600]{0,1:T(8,128)(2,1)} %all-gather.6.cloned.1.call-done, f32[1600]{0:T(1024)S(1)} %copy-done.50, f32[1600]{0:T(1024)S(1)} %mul.199, f32[1024]{0:T(1024)S(1)} %copy-done.55, f32[1024]{0:T(1024)S(1)} %broadcast_multiply_fusion), kind=kOutput, calls=%fused_computation.128 | convolution fusion | flops 2526412800 | bytes 9785856 | tf_op jit(solution)/shard_map/dot_general | solution.py:49
  398.2 7.5 %convolution_convert_fusion = bf16[1024,1600]{1,0:T(8,128)(2,1)} fusion(bf16[1024,800]{0,1:T(8,128)(2,1)} %get-tuple-element.108, bf16[800,1600]{1,0:T(8,128)(2,1)S(1)} %copy-done), kind=kOutput, calls=%fused_computation.14 | convolution fusion | flops 2623078400 | bytes 7475200 | tf_op jit(solution)/shard_map/dot_general | solution.py:49
  412.0 15.3 %collective-permute-done.32.refs_1_ = bf16[2,56,800]{2,1,0:T(8,128)(2,1)S(1)} collective-permute-done((bf16[2,56,800]{2,1,0:T(8,128)(2,1)S(1)}, bf16[2,56,800]{2,1,0:T(8,128)(2,1)S(1)}, u32[]{:S(2)}, u32[]{:S(2)}) %collective-permute-start.32) | collective-permute-done | bytes 179232 | tf_op jit(solution)/shard_map/ppermute | solution.py:28
  444.9 29.3 %collective-permute-done.26.refs_2_ = bf16[8,56,1600]{2,1,0:T(8,128)(2,1)S(1)} collective-permute-done((bf16[8,56,1600]{2,1,0:T(8,128)(2,1)}, bf16[8,56,1600]{2,1,0:T(8,128)(2,1)S(1)}, u32[]{:S(2)}, u32[]{:S(2)}) %collective-permute-start.26) | collective-permute-done | bytes 1433632 | tf_op jit(solution)/shard_map/ppermute | solution.py:28
  483.4 14.4 %collective-permute-done.28.refs_1_ = bf16[2,56,1600]{2,1,0:T(8,128)(2,1)S(1)} collective-permute-done((bf16[2,56,1600]{2,1,0:T(8,128)(2,1)}, bf16[2,56,1600]{2,1,0:T(8,128)(2,1)S(1)}, u32[]{:S(2)}, u32[]{:S(2)}) %collective-permute-start.28) | collective-permute-done | bytes 358432 | tf_op jit(solution)/shard_map/ppermute | solution.py:28
  499.1 9.5 %collective-permute-done.29.refs_2_ = bf16[2,56,1600]{2,1,0:T(8,128)(2,1)S(1)} collective-permute-done((bf16[2,56,1600]{2,1,0:T(8,128)(2,1)}, bf16[2,56,1600]{2,1,0:T(8,128)(2,1)S(1)}, u32[]{:S(2)}, u32[]{:S(2)}) %collective-permute-start.29) | collective-permute-done | bytes 358432 | tf_op jit(solution)/shard_map/ppermute | solution.py:28
  521.0 17.5 %collective-permute-done.41.refs_3_ = bf16[8,56,1600]{2,1,0:T(8,128)(2,1)} collective-permute-done((bf16[8,56,1600]{2,1,0:T(8,128)(2,1)}, bf16[8,56,1600]{2,1,0:T(8,128)(2,1)}, u32[]{:S(2)}, u32[]{:S(2)}) %collective-permute-start.41) | collective-permute-done | bytes 1433632 | tf_op jit(solution)/shard_map/ppermute | solution.py:28
  538.5 19.7 %collective-permute-done.40.refs_2_ = bf16[8,56,1600]{2,1,0:T(8,128)(2,1)} collective-permute-done((bf16[8,56,1600]{2,1,0:T(8,128)(2,1)}, bf16[8,56,1600]{2,1,0:T(8,128)(2,1)}, u32[]{:S(2)}, u32[]{:S(2)}) %collective-permute-start.40) | collective-permute-done | bytes 1433632 | tf_op jit(solution)/shard_map/ppermute | solution.py:28
  558.1 9.7 %finish_hidden.1 = (f32[200,6400]{1,0:T(8,128)}, f32[800,1600]{1,0:T(8,128)}, f32[4,16,256]{2,1,0:T(8,128)}) custom-call(s32[2]{0:T(128)} %pad_add_fusion.1.where_ref, bf16[8,56,1600]{2,1,0:T(8,128)(2,1)} %join_hidden.1.refs_0_, bf16[8,56,1600]{2,1,0:T(8,128)(2,1)} %collective-permute-done.36.refs_1_, bf16[8,56,1600]{2,1,0:T(8,128)(2,1)} %collective-permute-done.40.refs_2_, ...), custom_call_target="tpu_custom_call" | custom-call | bytes 17203200 | tf_op jit(solution)/shard_map/finish_hidden/pallas_call | solution.py:240
  (389 shorter events, 244.7 us)
Async XLA Ops:
  7.3 85.8 %all-gather.8.cloned.1.call-start = ((), (), s32[]{:S(2)}) async-start(), calls=%async_computation.5 | async-start | bytes 3440640 | tf_op jit(solution)/shard_map/all_gather | solution.py:752
  32.1 84.3 %all-gather.6.cloned.1.call-start = ((), (), s32[]{:S(2)}) async-start(), calls=%async_computation.4 | async-start | bytes 3686400 | tf_op jit(solution)/shard_map/all_gather | solution.py:704
  32.8 131.8 %all-gather.10.cloned.1.call-start = ((), (), s32[]{:S(2)}) async-start(), calls=%async_computation.6 | async-start | bytes 4014080 | tf_op jit(solution)/shard_map/all_gather | solution.py:763
  40.8 35.5 %collective-permute-start.5 = (bf16[144,1600]{1,0:T(8,128)(2,1)}, bf16[144,1600]{1,0:T(8,128)(2,1)S(1)}, u32[]{:S(2)}, u32[]{:S(2)}) collective-permute-start(bf16[144,1600]{1,0:T(8,128)(2,1)} %get-tuple-element.79), channel_id=1, source_target_pairs={{0,4},{1,5},{2,6},{3,7},{4,0},{5,1},{6,2},{7,3},{8,12},{9,13},{10,... | collective-permute-start | bytes 1382408 | tf_op jit(solution)/shard_map/ppermute | solution.py:28
  41.8 34.5 %collective-permute-start.6 = (bf16[144,1600]{1,0:T(8,128)(2,1)}, bf16[144,1600]{1,0:T(8,128)(2,1)S(1)}, u32[]{:S(2)}, u32[]{:S(2)}) collective-permute-start(bf16[144,1600]{1,0:T(8,128)(2,1)} %get-tuple-element.80), channel_id=1, source_target_pairs={{0,6},{1,7},{2,4},{3,5},{4,2},{5,3},{6,0},{7,1},{8,14},{9,15},{10,... | collective-permute-start | bytes 1382408 | tf_op jit(solution)/shard_map/ppermute | solution.py:28
  84.3 122.1 %all-gather.12.cloned.1.call-start = ((), (), s32[]{:S(2)}) async-start(), calls=%async_computation.7 | async-start | bytes 3686400 | tf_op jit(solution)/shard_map/all_gather | solution.py:704
  88.1 44.9 %collective-permute-start.11 = (bf16[4,56,1600]{2,1,0:T(8,128)(2,1)}, bf16[4,56,1600]{2,1,0:T(8,128)(2,1)}, u32[]{:S(2)}, u32[]{:S(2)}) collective-permute-start(bf16[4,56,1600]{2,1,0:T(8,128)(2,1)} %get-tuple-element.84.refs_0_), channel_id=1, source_target_pairs={{0,24},{8,16},{16,8},{24,0},{1,25},{9,17},{17,9},{25,1},{2,26},{10... | collective-permute-start | bytes 2150408 | tf_op jit(solution)/shard_map/ppermute | solution.py:28
  90.6 42.5 %collective-permute-start.10 = (bf16[4,56,1600]{2,1,0:T(8,128)(2,1)}, bf16[4,56,1600]{2,1,0:T(8,128)(2,1)}, u32[]{:S(2)}, u32[]{:S(2)}) collective-permute-start(bf16[4,56,1600]{2,1,0:T(8,128)(2,1)} %get-tuple-element.84.refs_0_), channel_id=1, source_target_pairs={{0,16},{8,24},{16,0},{24,8},{1,17},{9,25},{17,1},{25,9},{2,18},{10... | collective-permute-start | bytes 2150408 | tf_op jit(solution)/shard_map/ppermute | solution.py:28
  91.1 42.0 %collective-permute-start.9 = (bf16[4,56,1600]{2,1,0:T(8,128)(2,1)}, bf16[4,56,1600]{2,1,0:T(8,128)(2,1)}, u32[]{:S(2)}, u32[]{:S(2)}) collective-permute-start(bf16[4,56,1600]{2,1,0:T(8,128)(2,1)} %get-tuple-element.84.refs_0_), channel_id=1, source_target_pairs={{0,8},{8,0},{16,24},{24,16},{1,9},{9,1},{17,25},{25,17},{2,10},{10... | collective-permute-start | bytes 2150408 | tf_op jit(solution)/shard_map/ppermute | solution.py:28
  164.6 81.9 %all-gather.14.cloned.1.call-start = ((), (), s32[]{:S(2)}) async-start(), calls=%async_computation.8 | async-start | bytes 3833856 | tf_op jit(solution)/shard_map/all_gather | solution.py:704
  206.4 102.4 %reduce-scatter.7.cloned.1.call-start = ((), (), s32[]{:S(2)}) async-start(), calls=%async_computation.10 | async-start | bytes 3833856 | tf_op jit(solution)/shard_map/reduce_scatter | solution.py:708
  267.2 128.3 %reduce-scatter.5.cloned.1.call-start = ((), (), s32[]{:S(2)}) async-start(), calls=%async_computation.9 | async-start | bytes 7454720 | tf_op jit(solution)/shard_map/reduce_scatter | solution.py:812
  291.6 277.8 %reduce-scatter.11.cloned.1.call-start = ((), (), s32[]{:S(2)}) async-start(), calls=%async_computation.12 | async-start | bytes 3833856 | tf_op jit(solution)/shard_map/reduce_scatter | solution.py:708
  361.9 215.8 %reduce-scatter.9.cloned.1.call-start = ((), (), s32[]{:S(2)}) async-start(), calls=%async_computation.11 | async-start | bytes 3833856 | tf_op jit(solution)/shard_map/reduce_scatter | solution.py:708
  405.8 38.7 %collective-permute-start.25 = (bf16[8,56,1600]{2,1,0:T(8,128)(2,1)}, bf16[8,56,1600]{2,1,0:T(8,128)(2,1)S(1)}, u32[]{:S(2)}, u32[]{:S(2)}) collective-permute-start(bf16[8,56,1600]{2,1,0:T(8,128)(2,1)} %get-tuple-element.110), channel_id=1, source_target_pairs={{0,8},{8,0},{16,24},{24,16},{1,9},{9,1},{17,25},{25,17},{2,10},{10... | collective-permute-start | bytes 4300808 | tf_op jit(solution)/shard_map/ppermute | solution.py:28
  407.3 66.9 %collective-permute-start.26 = (bf16[8,56,1600]{2,1,0:T(8,128)(2,1)}, bf16[8,56,1600]{2,1,0:T(8,128)(2,1)S(1)}, u32[]{:S(2)}, u32[]{:S(2)}) collective-permute-start(bf16[8,56,1600]{2,1,0:T(8,128)(2,1)} %get-tuple-element.111), channel_id=1, source_target_pairs={{0,16},{8,24},{16,0},{24,8},{1,17},{9,25},{17,1},{25,9},{2,18},{10... | collective-permute-start | bytes 4300808 | tf_op jit(solution)/shard_map/ppermute | solution.py:28
  408.7 65.6 %collective-permute-start.27 = (bf16[8,56,1600]{2,1,0:T(8,128)(2,1)}, bf16[8,56,1600]{2,1,0:T(8,128)(2,1)S(1)}, u32[]{:S(2)}, u32[]{:S(2)}) collective-permute-start(bf16[8,56,1600]{2,1,0:T(8,128)(2,1)} %get-tuple-element.112), channel_id=1, source_target_pairs={{0,24},{8,16},{16,8},{24,0},{1,25},{9,17},{17,9},{25,1},{2,26},{10... | collective-permute-start | bytes 4300808 | tf_op jit(solution)/shard_map/ppermute | solution.py:28
  441.5 72.0 %collective-permute-start.36 = (bf16[8,56,1600]{2,1,0:T(8,128)(2,1)}, bf16[8,56,1600]{2,1,0:T(8,128)(2,1)}, u32[]{:S(2)}, u32[]{:S(2)}) collective-permute-start(bf16[8,56,1600]{2,1,0:T(8,128)(2,1)} %join_hidden.1.refs_0_), channel_id=1, source_target_pairs={{0,8},{8,0},{16,24},{24,16},{1,9},{9,1},{17,25},{25,17},{2,10},{10... | collective-permute-start | bytes 4300808 | tf_op jit(solution)/shard_map/ppermute | solution.py:28
  443.0 95.4 %collective-permute-start.41 = (bf16[8,56,1600]{2,1,0:T(8,128)(2,1)}, bf16[8,56,1600]{2,1,0:T(8,128)(2,1)}, u32[]{:S(2)}, u32[]{:S(2)}) collective-permute-start(bf16[8,56,1600]{2,1,0:T(8,128)(2,1)} %join_hidden.1.refs_0_), channel_id=1, source_target_pairs={{0,24},{8,16},{16,8},{24,0},{1,25},{9,17},{17,9},{25,1},{2,26},{10... | collective-permute-start | bytes 4300808 | tf_op jit(solution)/shard_map/ppermute | solution.py:28
  444.5 113.7 %collective-permute-start.40 = (bf16[8,56,1600]{2,1,0:T(8,128)(2,1)}, bf16[8,56,1600]{2,1,0:T(8,128)(2,1)}, u32[]{:S(2)}, u32[]{:S(2)}) collective-permute-start(bf16[8,56,1600]{2,1,0:T(8,128)(2,1)} %join_hidden.1.refs_0_), channel_id=1, source_target_pairs={{0,16},{8,24},{16,0},{24,8},{1,17},{9,25},{17,1},{25,9},{2,18},{10... | collective-permute-start | bytes 4300808 | tf_op jit(solution)/shard_map/ppermute | solution.py:28
  482.6 25.9 %collective-permute-start.29 = (bf16[2,56,1600]{2,1,0:T(8,128)(2,1)}, bf16[2,56,1600]{2,1,0:T(8,128)(2,1)S(1)}, u32[]{:S(2)}, u32[]{:S(2)}) collective-permute-start(bf16[2,56,1600]{2,1,0:T(8,128)(2,1)} %get-tuple-element.115), channel_id=1, source_target_pairs={{0,4},{1,5},{2,6},{3,7},{4,0},{5,1},{6,2},{7,3},{8,12},{9,13},{10,... | collective-permute-start | bytes 1075208 | tf_op jit(solution)/shard_map/ppermute | solution.py:28
  516.8 64.9 %collective-permute-start.39 = (bf16[5,56,1600]{2,1,0:T(8,128)(2,1)}, bf16[5,56,1600]{2,1,0:T(8,128)(2,1)}, u32[]{:S(2)}, u32[]{:S(2)}) collective-permute-start(bf16[5,56,1600]{2,1,0:T(8,128)(2,1)} %join_last.1.refs_0_), channel_id=1, source_target_pairs={{0,24},{8,16},{16,8},{24,0},{1,25},{9,17},{17,9},{25,1},{2,26},{10... | collective-permute-start | bytes 2688008 | tf_op jit(solution)/shard_map/ppermute | solution.py:28
  518.2 63.4 %collective-permute-start.38 = (bf16[5,56,1600]{2,1,0:T(8,128)(2,1)}, bf16[5,56,1600]{2,1,0:T(8,128)(2,1)}, u32[]{:S(2)}, u32[]{:S(2)}) collective-permute-start(bf16[5,56,1600]{2,1,0:T(8,128)(2,1)} %join_last.1.refs_0_), channel_id=1, source_target_pairs={{0,16},{8,24},{16,0},{24,8},{1,17},{9,25},{17,1},{25,9},{2,18},{10... | collective-permute-start | bytes 2688008 | tf_op jit(solution)/shard_map/ppermute | solution.py:28
  519.7 61.9 %collective-permute-start.37 = (bf16[5,56,1600]{2,1,0:T(8,128)(2,1)}, bf16[5,56,1600]{2,1,0:T(8,128)(2,1)}, u32[]{:S(2)}, u32[]{:S(2)}) collective-permute-start(bf16[5,56,1600]{2,1,0:T(8,128)(2,1)} %join_last.1.refs_0_), channel_id=1, source_target_pairs={{0,8},{8,0},{16,24},{24,16},{1,9},{9,1},{17,25},{25,17},{2,10},{10... | collective-permute-start | bytes 2688008 | tf_op jit(solution)/shard_map/ppermute | solution.py:28
  (103 other events, 1471.9 us)
Sparse Core Ops, SparseCore 0:
  32.2 42.2 all-gather.7
  76.1 40.2 all-gather.5
  118.8 45.8 all-gather.9
  166.1 40.2 all-gather.11
  207.8 38.6 all-gather.13
  267.3 41.4 reduce-scatter.6
  311.8 66.1 reduce-scatter.4
  380.3 50.1 reduce-scatter.10
  433.4 42.1 reduce-scatter.8

commit v4 on v3

--- a/solution.py
+++ b/solution.py
@@ -275,7 +275,7 @@
 
 
 def slot_rows(span):
-    return -(-span // 16) * 16
+    return -(-span // 8) * 8
 
 
 def pack_columns(where, weight, out_weight, vectors, copies, count):
@@ -296,7 +296,7 @@
             out[slot : slot + span, :] = out_ref[pl.ds(start, span), :]
             out[2 * slot :, :] = vectors_ref[...]
 
-    shape = jax.ShapeDtypeStruct((2 * slot + 16, D), low)
+    shape = jax.ShapeDtypeStruct((2 * slot + 8, D), low)
     scratch = [pltpu.VMEM((count, span, cols), low)]
     return local_call(
         kernel, [shape] * (count // 2), scratch, "pack_columns", where, weight, out_weight, vectors
@@ -736,8 +736,8 @@
     token_all = gather_rows(tokens)
     qkv_got, qkv_far = exchange(pack_heads(where, qkv_weight, copies, count, width))
     qkv_stack = by_rank(qkv_got, qkv_far)
-    vectors = tie(jnp.concatenate(vectors), qkv_stack)
-    vectors = jnp.pad(vectors[None], ((0, 15), (0, D - 8 * own_rows)))
+    vectors = tie(jnp.concatenate(vectors), qkv_stack, token_all)
+    vectors = jnp.pad(vectors[None], ((0, 7), (0, D - 8 * own_rows)))
     fc_pairs = pack_columns(where, fc_weight, out_weight, vectors, copies, count)
     fc_got = [fc_pairs[0]] + [xor_send(fc_pairs[j], "shard", evens[j]) for j in range(1, half)]
     fc_odd, out_near = split_columns(where, fc_got, span, ff_cols)
@@ -751,7 +751,7 @@
     b_query, b_value, b_out, b_proj, g_first, s_first, g_second, s_second = vectors
     qkv_stacks = lax.all_gather(qkv_stack.reshape(count * span, 3 * width), "replica")
     qkv_stacks = qkv_stacks.reshape(copies, count, span, 3 * width)
-    w_qkv = assemble_copies(where, qkv_stacks, own_rows)
+    w_qkv = assemble_copies(where, tie(qkv_stacks, *fc_got), own_rows)
     w_qkv = w_qkv.reshape(D, 3 * width)
 
     out_near = from_copies(out_near)
@@ -760,9 +760,8 @@
     fc_stack = jnp.concatenate(
         [got[:span, :ff_cols][None] for got in fc_got] + [fc_far], 0
     )
-    fc_stacks = lax.all_gather(fc_stack.reshape(count * span, ff_cols), "replica")
-    fc_stacks = fc_stacks.reshape(copies, count, span, ff_cols)
-    w_fc = assemble_copies(where, fc_stacks, own_rows).reshape(D, ff_cols)
+    fc_stacks = from_copies(fc_stack)
+    w_fc = assemble_rows(where, [[stack] for stack in fc_stacks], own_rows).reshape(D, ff_cols)
 
     def own_heads(vector):
         vector = jnp.pad(vector, (0, count * width - D))
@@ -781,16 +780,16 @@
     queries = (projected[:, :width] + own_heads(b_query)).astype(low)
     keys = tie(projected, fc_stack)[:, width : 2 * width].astype(low)
     values = (projected[:, 2 * width :] + own_heads(b_value)).astype(low)
+    cot_all = gather_rows(tie(cotangent, w_qkv))
     attended, log_total = attend_forward(order, queries, keys, values, heads)
 
     attended = tie(attended, *out_near)
     attended_own = order_heads(where, *exchange(list(attended.reshape(half, 2, STRETCH, width))))
-    cot_all = gather_rows(tie(cotangent, attended_own, fc_stacks))
     attended_own = attended_own[:, :D]
     in_rows = tokens.astype(full)
     middle = in_rows + mm(attended_own, w_out, 1, 0) + b_out
     second_own = layer_norm(middle, g_second, s_second).astype(low)
-    second_all = gather_rows(tie(second_own, cot_all))
+    second_all = gather_rows(tie(second_own, cot_all, fc_stacks[1]))
     hidden = mm(second_all, w_fc, 1, 0) + fc_bias.astype(full)
     active, pull_gelu = jax.vjp(gelu_tanh, hidden)
     active_low = active.astype(low)
@@ -867,17 +866,20 @@
     last = to_copies(last)
 
     fc_sums, rest = sum_hidden(where, [hidden_sum], count, ff_cols)
-    hidden_stacks = from_copies(join_hidden(where, *exchange(fc_sums), rest))
+    hidden_joined = join_hidden(where, *exchange(fc_sums), rest)
+    hidden_stacks = from_copies(hidden_joined)
     fc_grad, proj_grad, fbias = finish_hidden(
         where, hidden_stacks, count, own_rows, ff_cols, ff_cols, hidden_sums.shape[2]
     )
     fbias = fbias[:, 0, : ff_cols // copies].reshape(ff_cols)
 
+    last[0] = tie(last[0], hidden_joined)
     last = sum_last(where, last, count, 3 * width)
+    output_low = tie(active_low, last[0])
     last = [last[0]] + [xor_send(last[j], "shard", evens[j]) for j in range(1, half)]
     far = xor_send(odd_last(where, last, 3 * width), "shard", 1)
     last = from_copies(join_last(where, last, tie(far, hidden_stacks[1])))
-    output_part = mm(tie(active_low, fc_sums[0]), proj_weight, 1, 0).astype(low)
+    output_part = mm(output_low, proj_weight, 1, 0).astype(low)
     output = middle + b_proj + scatter_rows(output_part).astype(full)
 
     _, pull_first = jax.vjp(lambda rows: layer_norm(rows, g_first, s_first), in_rows)

time: 599 us -> 602 us (level)
  waiting for transfers between devices: 288 us -> 279 us
  matrix products: 72.9 us -> 79.4 us
    all_gather x3, waiting for transfers between devices: 79.2 us -> 23.7 us  [gather_rows(): return lax.all_gather(block, 'shard', axis=0, tiled=True)]
    all_gather x1, waiting for transfers between devices: 0.01 us -> 31.4 us  [on_device(): lax.all_gather(qkv_stack.reshape(count * span, 3 * width), 'replica')]
    ppermute x42 -> x45, waiting for transfers between devices: 182 us -> 207 us  [xor_send(): return lax.ppermute(block, axis, [(i, i ^ bits) for i in range(count)])]
    all_gather x1 -> x0, waiting for transfers between devices: 11.3 us -> none  [on_device(): lax.all_gather(fc_stack.reshape(count * span, ff_cols), 'replica')]
    unnamed x162 -> x144, local copies, waits for them, and re-layouts: 26.6 us -> 22.6 us
    ppermute x42 -> x45, starting transfers between devices: 47.4 us -> 49.6 us  [xor_send(): return lax.ppermute(block, axis, [(i, i ^ bits) for i in range(count)])]
  transfers between devices with their start and end apart: 51 -> 53, of which waited for: 29 -> 24; matrix products, arithmetic and copies ran while one was open for 18% -> 21% of each run, Pallas kernels for 15% -> 15%
where the time goes in v4:
time: 602 us; the launch traced here: 596 us
  waiting for transfers between devices  279 us (46%)
  Pallas kernels  96.9 us (16%)
  matrix products  79.4 us (13%)
  local copies, waits for them, and re-layouts  52.9 us (9%)
  starting transfers between devices  50.4 us (8%)
  other arithmetic  21.8 us (4%)
  between operations  15.4 us (3%)
    ppermute x45, waiting for transfers between devices, xor_send(): return lax.ppermute(block, axis, [(i, i ^ bits) for i in range(count)])  207 us
    dot_general x12, matrix products, mm(): lax.dot_general(left_side, right_side, (((left_dim,), (right_dim,)), ((),...  77.7 us
    pallas_call x18, Pallas kernels, local_call(): pl.pallas_call(kernel, out_shape=tuple(shapes) if many else shapes, in_sp...  77.5 us
    ppermute x45, starting transfers between devices, xor_send(): return lax.ppermute(block, axis, [(i, i ^ bits) for i in range(count)])  49.6 us
    all_gather x1, waiting for transfers between devices, on_device(): lax.all_gather(qkv_stack.reshape(count * span, 3 * width), 'replica')  31.4 us
    all_gather x3, waiting for transfers between devices, gather_rows(): return lax.all_gather(block, 'shard', axis=0, tiled=True)  23.7 us
    unnamed x144, local copies, waits for them, and re-layouts  22.6 us
    reduce_scatter x3, waiting for transfers between devices, scatter_rows(): return lax.psum_scatter(blocks, 'shard', scatter_dimension=0, tiled=True)  16.7 us
  transfers between devices with their start and end apart: 53, of which 24 were waited for; matrix products, arithmetic and copies ran while one was open for 21% of the time, Pallas kernels for 15%

profile of v4, /device:TPU:0, one launch (start us, length us, event | category | flops | bytes accessed | tf_op | source)
XLA Modules:
  0.0 596.1 jit_solution(12970799492116754372)
XLA Ops:
  21.6 14.3 %collective-permute-done.1 = bf16[2,56,768]{2,1,0:T(8,128)(2,1)S(1)} collective-permute-done((bf16[2,56,768]{2,1,0:T(8,128)(2,1)}, bf16[2,56,768]{2,1,0:T(8,128)(2,1)S(1)}, u32[]{:S(2)}, u32[]{:S(2)}) %collective-permute-start.1) | collective-permute-done | bytes 172064 | tf_op jit(solution)/shard_map/ppermute | solution.py:28
  39.6 23.7 %all-gather.5.cloned.1.call-done = bf16[1024,1600]{0,1:T(8,128)(2,1)} async-done(((bf16[128,1600]{0,1:T(8,128)(2,1)}), bf16[1024,1600]{0,1:T(8,128)(2,1)}) %all-gather.5.cloned.1.call-update) | async-done | bytes 3276816 | tf_op jit(solution)/shard_map/all_gather | solution.py:704
  74.6 31.4 %all-gather.7.cloned.1.call-done = bf16[4,448,768]{2,1,0:T(8,128)(2,1)} async-done(((bf16[1,448,768]{2,1,0:T(8,128)(2,1)}), bf16[4,448,768]{2,1,0:T(8,128)(2,1)}) %all-gather.7.cloned.1.call-update) | async-done | bytes 2752528 | tf_op jit(solution)/shard_map/all_gather | solution.py:752
  138.2 8.2 %attend_forward.1 = (bf16[1024,256]{1,0:T(8,128)(2,1)S(1)}, f32[1,4,1024]{2,1,0:T(4,128)S(1)}) custom-call(s32[3,8]{1,0:T(4,128)S(1)} %pad_add_fusion.order_ref, bf16[1024,256]{1,0:T(8,128)(2,1)S(1)} %get-tuple-element.234.q_ref, bf16[1024,256]{1,0:T(8,128)(2,1)S(1)} %slice.248.k_ref, bf16[1024,256]{1,0:T(8,128)(2,1)S(1)} %get-tuple-element.233.v_ref), custom_call_target="tpu_custom_call" | custom-call | flops 4294967296 | bytes 2097152 | tf_op jit(solution)/shard_map/attend_forward/pallas_call | solution.py:180
  154.4 8.5 %collective-permute-done.13.refs_2_ = bf16[2,128,256]{2,1,0:T(8,128)(2,1)S(1)} collective-permute-done((bf16[2,128,256]{2,1,0:T(8,128)(2,1)S(1)}, bf16[2,128,256]{2,1,0:T(8,128)(2,1)S(1)}, u32[]{:S(2)}, u32[]{:S(2)}) %collective-permute-start.13) | collective-permute-done | bytes 131104 | tf_op jit(solution)/shard_map/ppermute | solution.py:28
  197.6 16.5 %collective-permute-done.22.refs_3_ = bf16[8,56,800]{2,1,0:T(8,128)(2,1)S(1)} collective-permute-done((bf16[8,56,800]{2,1,0:T(8,128)(2,1)}, bf16[8,56,800]{2,1,0:T(8,128)(2,1)S(1)}, u32[]{:S(2)}, u32[]{:S(2)}) %collective-permute-start.22) | collective-permute-done | bytes 716832 | tf_op jit(solution)/shard_map/ppermute | solution.py:28
  214.2 17.1 %collective-permute-done.21.refs_2_ = bf16[8,56,800]{2,1,0:T(8,128)(2,1)S(1)} collective-permute-done((bf16[8,56,800]{2,1,0:T(8,128)(2,1)}, bf16[8,56,800]{2,1,0:T(8,128)(2,1)S(1)}, u32[]{:S(2)}, u32[]{:S(2)}) %collective-permute-start.21) | collective-permute-done | bytes 716832 | tf_op jit(solution)/shard_map/ppermute | solution.py:28
  242.6 11.8 %convert_reduce_fusion.1 = (f32[800]{0:T(1024)}, bf16[1024,800]{0,1:T(8,128)(2,1)S(1)}, bf16[1024,800]{0,1:T(8,128)(2,1)}) fusion(f32[1024,800]{0,1:T(8,128)} %fusion.61, f32[800]{0:T(1024)} %convert_element_type.92, bf16[1024,1600]{1,0:T(8,128)(2,1)} %all-gather.11.cloned.1.call-done, bf16[1600,800]{1,0:T(8,128)(2,1)} %bitcast.92), kind=kOutput, calls=%fused_computation.22 | convolution fusion | flops 2645196032 | bytes 12396800 | tf_op jit(solution)/shard_map/dot_general | solution.py:49
  264.0 8.1 %fusion.60.proj_ref = f32[800,1600]{1,0:T(8,128)} fusion(bf16[1024,800]{0,1:T(8,128)(2,1)} %get-tuple-element.120, bf16[1024,1600]{0,1:T(8,128)(2,1)} %all-gather.9.cloned.1.call-done), kind=kOutput, calls=%fused_computation.144 | convolution fusion | flops 2621440000 | bytes 10035200 | tf_op jit(solution)/shard_map/dot_general | solution.py:49
  277.6 7.8 %pack_hidden.1 = bf16[4,8,56,1600]{3,2,1,0:T(8,128)(2,1)} custom-call(s32[2]{0:T(128)} %pad_add_fusion.1.where_ref, f32[8,200,800]{2,1,0:T(8,128)} %bitcast.90, f32[800,1600]{1,0:T(8,128)} %fusion.60.proj_ref, f32[4,16,256]{2,1,0:T(8,128)} %pad.22.sums_ref), custom_call_target="tpu_custom_call" | custom-call | bytes 30916608 | tf_op jit(solution)/shard_map/pack_hidden/pallas_call | solution.py:240
  287.4 16.7 %reduce-scatter.5.cloned.1.call-done = bf16[128,1600]{1,0:T(8,128)(2,1)} async-done(((bf16[1024,1600]{1,0:T(8,128)(2,1)}), bf16[128,1600]{1,0:T(8,128)(2,1)}) %reduce-scatter.5.cloned.1.call-update) | async-done | bytes 409616 | tf_op jit(solution)/shard_map/reduce_scatter | solution.py:708
  323.6 6.9 %collective-permute-done.24 = bf16[2,128,256]{2,1,0:T(8,128)(2,1)S(1)} collective-permute-done((bf16[2,128,256]{2,1,0:T(8,128)(2,1)}, bf16[2,128,256]{2,1,0:T(8,128)(2,1)S(1)}, u32[]{:S(2)}, u32[]{:S(2)}) %collective-permute-start.24) | collective-permute-done | bytes 131104 | tf_op jit(solution)/shard_map/ppermute | solution.py:28
  335.4 11.3 %attend_backward.1 = (bf16[1024,256]{1,0:T(8,128)(2,1)S(1)}, bf16[1024,256]{1,0:T(8,128)(2,1)S(1)}, bf16[1024,256]{1,0:T(8,128)(2,1)S(1)}) custom-call(s32[3,8]{1,0:T(4,128)S(1)} %pad_add_fusion.order_ref, bf16[1024,256]{1,0:T(8,128)(2,1)S(1)} %copy-done.7, bf16[1024,256]{1,0:T(8,128)(2,1)S(1)} %copy-done.3, bf16[1024,256]{1,0:T(8,128)(2,1)S(1)} %copy-done.5, ...), custom_call_target="tpu_custom_call" | custom-call | flops 10737418240 | bytes 3670016 | tf_op jit(solution)/shard_map/attend_backward/pallas_call | solution.py:203
  357.5 6.8 %fusion.23 = f32[1600,1600]{1,0:T(8,128)} fusion(bf16[128,1600]{1,0:T(8,128)(2,1)} %copy-done.17, bf16[128,2048]{1,0:T(8,128)(2,1)} %order_heads.1), kind=kOutput, calls=%fused_computation.55 | convolution fusion | flops 655360000 | bytes 11091968 | tf_op jit(solution)/shard_map/dot_general | solution.py:49
  364.3 7.4 %split_outw.1 = (bf16[4,56,1600]{2,1,0:T(8,128)(2,1)}, bf16[4,56,1600]{2,1,0:T(8,128)(2,1)}, bf16[4,56,1600]{2,1,0:T(8,128)(2,1)}, bf16[4,56,1600]{2,1,0:T(8,128)(2,1)}, bf16[4,4,56,1600]{3,2,1,0:T(8,128)(2,1)}) custom-call(s32[2]{0:T(128)} %pad_add_fusion.1.where_ref, f32[8,200,1600]{2,1,0:T(8,128)} %bitcast.86), custom_call_target="tpu_custom_call" | custom-call | bytes 30720000 | tf_op jit(solution)/shard_map/split_outw/pallas_call | solution.py:240
  375.8 7.8 %fusion.40 = f32[1600,768]{1,0:T(8,128)} fusion(bf16[1024,768]{1,0:T(8,128)(2,1)} %copy-done.36, bf16[1024,1600]{0,1:T(8,128)(2,1)} %all-gather.5.cloned.1.call-done, f32[1600]{0:T(1024)S(1)} %copy-done.46, f32[1600]{0:T(1024)S(1)} %mul.199, f32[1024]{0:T(1024)S(1)} %copy-done.49, f32[1024]{0:T(1024)S(1)} %broadcast_multiply_fusion), kind=kOutput, calls=%fused_computation.128 | convolution fusion | flops 2526412800 | bytes 9785856 | tf_op jit(solution)/shard_map/dot_general | solution.py:49
  383.7 7.4 %pack_last.1 = (bf16[8,56,1600]{2,1,0:T(8,128)(2,1)}, bf16[8,56,1600]{2,1,0:T(8,128)(2,1)}, bf16[8,56,1600]{2,1,0:T(8,128)(2,1)}, bf16[8,56,1600]{2,1,0:T(8,128)(2,1)}) custom-call(s32[2]{0:T(128)} %pad_add_fusion.1.where_ref, f32[8,200,768]{2,1,0:T(8,128)} %bitcast.91, bf16[4,56,1600]{2,1,0:T(8,128)(2,1)} %get-tuple-element.103.refs_0_, ...), custom_call_target="tpu_custom_call" | custom-call | bytes 32342016 | tf_op jit(solution)/shard_map/pack_last/pallas_call | solution.py:240
  400.0 15.5 %collective-permute-done.28.refs_1_ = bf16[2,56,800]{2,1,0:T(8,128)(2,1)S(1)} collective-permute-done((bf16[2,56,800]{2,1,0:T(8,128)(2,1)}, bf16[2,56,800]{2,1,0:T(8,128)(2,1)S(1)}, u32[]{:S(2)}, u32[]{:S(2)}) %collective-permute-start.28) | collective-permute-done | bytes 179232 | tf_op jit(solution)/shard_map/ppermute | solution.py:28
  418.0 11.4 %collective-permute-done.30.refs_3_ = bf16[2,56,800]{2,1,0:T(8,128)(2,1)S(1)} collective-permute-done((bf16[2,56,800]{2,1,0:T(8,128)(2,1)}, bf16[2,56,800]{2,1,0:T(8,128)(2,1)S(1)}, u32[]{:S(2)}, u32[]{:S(2)}) %collective-permute-start.30) | collective-permute-done | bytes 179232 | tf_op jit(solution)/shard_map/ppermute | solution.py:28
  435.0 24.6 %collective-permute-done.33.refs_2_ = bf16[8,56,1600]{2,1,0:T(8,128)(2,1)} collective-permute-done((bf16[8,56,1600]{2,1,0:T(8,128)(2,1)}, bf16[8,56,1600]{2,1,0:T(8,128)(2,1)}, u32[]{:S(2)}, u32[]{:S(2)}) %collective-permute-start.33) | collective-permute-done | bytes 1433632 | tf_op jit(solution)/shard_map/ppermute | solution.py:28
  475.6 23.9 %collective-permute-done.35.refs_1_ = bf16[2,56,1600]{2,1,0:T(8,128)(2,1)S(1)} collective-permute-done((bf16[2,56,1600]{2,1,0:T(8,128)(2,1)}, bf16[2,56,1600]{2,1,0:T(8,128)(2,1)S(1)}, u32[]{:S(2)}, u32[]{:S(2)}) %collective-permute-start.35) | collective-permute-done | bytes 358432 | tf_op jit(solution)/shard_map/ppermute | solution.py:28
  506.8 15.9 %collective-permute-done.37.refs_3_ = bf16[2,56,1600]{2,1,0:T(8,128)(2,1)S(1)} collective-permute-done((bf16[2,56,1600]{2,1,0:T(8,128)(2,1)}, bf16[2,56,1600]{2,1,0:T(8,128)(2,1)S(1)}, u32[]{:S(2)}, u32[]{:S(2)}) %collective-permute-start.37) | collective-permute-done | bytes 358432 | tf_op jit(solution)/shard_map/ppermute | solution.py:28
  538.0 21.1 %collective-permute-done.43.refs_2_ = bf16[8,56,1600]{2,1,0:T(8,128)(2,1)} collective-permute-done((bf16[8,56,1600]{2,1,0:T(8,128)(2,1)}, bf16[8,56,1600]{2,1,0:T(8,128)(2,1)}, u32[]{:S(2)}, u32[]{:S(2)}) %collective-permute-start.43) | collective-permute-done | bytes 1433632 | tf_op jit(solution)/shard_map/ppermute | solution.py:28
  559.1 9.7 %finish_hidden.1 = (f32[200,6400]{1,0:T(8,128)}, f32[800,1600]{1,0:T(8,128)}, f32[4,16,256]{2,1,0:T(8,128)}) custom-call(s32[2]{0:T(128)} %pad_add_fusion.1.where_ref, bf16[8,56,1600]{2,1,0:T(8,128)(2,1)} %join_hidden.1.refs_0_, bf16[8,56,1600]{2,1,0:T(8,128)(2,1)} %collective-permute-done.39.refs_1_, bf16[8,56,1600]{2,1,0:T(8,128)(2,1)} %collective-permute-done.43.refs_2_, ...), custom_call_target="tpu_custom_call" | custom-call | bytes 17203200 | tf_op jit(solution)/shard_map/finish_hidden/pallas_call | solution.py:240
  (374 shorter events, 247.1 us)
Async XLA Ops:
  7.3 56.0 %all-gather.5.cloned.1.call-start = ((), (), s32[]{:S(2)}) async-start(), calls=%async_computation.4 | async-start | bytes 3686400 | tf_op jit(solution)/shard_map/all_gather | solution.py:704
  8.0 98.0 %all-gather.7.cloned.1.call-start = ((), (), s32[]{:S(2)}) async-start(), calls=%async_computation.5 | async-start | bytes 3440640 | tf_op jit(solution)/shard_map/all_gather | solution.py:752
  38.6 154.7 %all-gather.9.cloned.1.call-start = ((), (), s32[]{:S(2)}) async-start(), calls=%async_computation.6 | async-start | bytes 3686400 | tf_op jit(solution)/shard_map/all_gather | solution.py:704
  67.7 38.2 %collective-permute-start.4 = (bf16[120,1600]{1,0:T(8,128)(2,1)}, bf16[120,1600]{1,0:T(8,128)(2,1)}, u32[]{:S(2)}, u32[]{:S(2)}) collective-permute-start(bf16[120,1600]{1,0:T(8,128)(2,1)} %get-tuple-element.80), channel_id=1, source_target_pairs={{0,2},{1,3},{2,0},{3,1},{4,6},{5,7},{6,4},{7,5},{8,10},{9,11},{10,... | collective-permute-start | bytes 1152008 | tf_op jit(solution)/shard_map/ppermute | solution.py:28
  67.8 38.1 %collective-permute-start.5 = (bf16[120,1600]{1,0:T(8,128)(2,1)}, bf16[120,1600]{1,0:T(8,128)(2,1)}, u32[]{:S(2)}, u32[]{:S(2)}) collective-permute-start(bf16[120,1600]{1,0:T(8,128)(2,1)} %get-tuple-element.81), channel_id=1, source_target_pairs={{0,4},{1,5},{2,6},{3,7},{4,0},{5,1},{6,2},{7,3},{8,12},{9,13},{10,... | collective-permute-start | bytes 1152008 | tf_op jit(solution)/shard_map/ppermute | solution.py:28
  70.2 35.8 %collective-permute-start.6 = (bf16[120,1600]{1,0:T(8,128)(2,1)}, bf16[120,1600]{1,0:T(8,128)(2,1)}, u32[]{:S(2)}, u32[]{:S(2)}) collective-permute-start(bf16[120,1600]{1,0:T(8,128)(2,1)} %get-tuple-element.82), channel_id=1, source_target_pairs={{0,6},{1,7},{2,4},{3,5},{4,2},{5,3},{6,0},{7,1},{8,14},{9,15},{10,... | collective-permute-start | bytes 1152008 | tf_op jit(solution)/shard_map/ppermute | solution.py:28
  109.5 133.2 %all-gather.11.cloned.1.call-start = ((), (), s32[]{:S(2)}) async-start(), calls=%async_computation.7 | async-start | bytes 3833856 | tf_op jit(solution)/shard_map/all_gather | solution.py:704
  113.7 32.7 %collective-permute-start.11 = (bf16[4,56,1600]{2,1,0:T(8,128)(2,1)}, bf16[4,56,1600]{2,1,0:T(8,128)(2,1)}, u32[]{:S(2)}, u32[]{:S(2)}) collective-permute-start(bf16[4,56,1600]{2,1,0:T(8,128)(2,1)} %get-tuple-element.87.refs_0_), channel_id=1, source_target_pairs={{0,24},{8,16},{16,8},{24,0},{1,25},{9,17},{17,9},{25,1},{2,26},{10... | collective-permute-start | bytes 2150408 | tf_op jit(solution)/shard_map/ppermute | solution.py:28
  115.2 34.1 %collective-permute-start.10 = (bf16[4,56,1600]{2,1,0:T(8,128)(2,1)}, bf16[4,56,1600]{2,1,0:T(8,128)(2,1)}, u32[]{:S(2)}, u32[]{:S(2)}) collective-permute-start(bf16[4,56,1600]{2,1,0:T(8,128)(2,1)} %get-tuple-element.87.refs_0_), channel_id=1, source_target_pairs={{0,16},{8,24},{16,0},{24,8},{1,17},{9,25},{17,1},{25,9},{2,18},{10... | collective-permute-start | bytes 2150408 | tf_op jit(solution)/shard_map/ppermute | solution.py:28
  116.6 32.7 %collective-permute-start.9 = (bf16[4,56,1600]{2,1,0:T(8,128)(2,1)}, bf16[4,56,1600]{2,1,0:T(8,128)(2,1)}, u32[]{:S(2)}, u32[]{:S(2)}) collective-permute-start(bf16[4,56,1600]{2,1,0:T(8,128)(2,1)} %get-tuple-element.87.refs_0_), channel_id=1, source_target_pairs={{0,8},{8,0},{16,24},{24,16},{1,9},{9,1},{17,25},{25,17},{2,10},{10... | collective-permute-start | bytes 2150408 | tf_op jit(solution)/shard_map/ppermute | solution.py:28
  193.3 110.8 %reduce-scatter.5.cloned.1.call-start = ((), (), s32[]{:S(2)}) async-start(), calls=%async_computation.8 | async-start | bytes 3833856 | tf_op jit(solution)/shard_map/reduce_scatter | solution.py:708
  194.9 36.4 %collective-permute-start.21 = (bf16[8,56,800]{2,1,0:T(8,128)(2,1)}, bf16[8,56,800]{2,1,0:T(8,128)(2,1)S(1)}, u32[]{:S(2)}, u32[]{:S(2)}) collective-permute-start(bf16[8,56,800]{2,1,0:T(8,128)(2,1)} %copy-done.24), channel_id=1, source_target_pairs={{0,16},{8,24},{16,0},{24,8},{1,17},{9,25},{17,1},{25,9},{2,18},{10... | collective-permute-start | bytes 2150408 | tf_op jit(solution)/shard_map/ppermute | solution.py:28
  261.1 133.5 %reduce-scatter.7.cloned.1.call-start = ((), (), s32[]{:S(2)}) async-start(), calls=%async_computation.9 | async-start | bytes 7454720 | tf_op jit(solution)/shard_map/reduce_scatter | solution.py:811
  285.4 284.9 %reduce-scatter.11.cloned.1.call-start = ((), (), s32[]{:S(2)}) async-start(), calls=%async_computation.11 | async-start | bytes 3833856 | tf_op jit(solution)/shard_map/reduce_scatter | solution.py:708
  357.4 221.3 %reduce-scatter.9.cloned.1.call-start = ((), (), s32[]{:S(2)}) async-start(), calls=%async_computation.10 | async-start | bytes 3833856 | tf_op jit(solution)/shard_map/reduce_scatter | solution.py:708
  391.1 43.9 %collective-permute-start.32 = (bf16[8,56,1600]{2,1,0:T(8,128)(2,1)}, bf16[8,56,1600]{2,1,0:T(8,128)(2,1)}, u32[]{:S(2)}, u32[]{:S(2)}) collective-permute-start(bf16[8,56,1600]{2,1,0:T(8,128)(2,1)} %get-tuple-element.116), channel_id=1, source_target_pairs={{0,8},{8,0},{16,24},{24,16},{1,9},{9,1},{17,25},{25,17},{2,10},{10... | collective-permute-start | bytes 4300808 | tf_op jit(solution)/shard_map/ppermute | solution.py:28
  392.5 67.1 %collective-permute-start.33 = (bf16[8,56,1600]{2,1,0:T(8,128)(2,1)}, bf16[8,56,1600]{2,1,0:T(8,128)(2,1)}, u32[]{:S(2)}, u32[]{:S(2)}) collective-permute-start(bf16[8,56,1600]{2,1,0:T(8,128)(2,1)} %get-tuple-element.117), channel_id=1, source_target_pairs={{0,16},{8,24},{16,0},{24,8},{1,17},{9,25},{17,1},{25,9},{2,18},{10... | collective-permute-start | bytes 4300808 | tf_op jit(solution)/shard_map/ppermute | solution.py:28
  394.1 65.5 %collective-permute-start.34 = (bf16[8,56,1600]{2,1,0:T(8,128)(2,1)}, bf16[8,56,1600]{2,1,0:T(8,128)(2,1)}, u32[]{:S(2)}, u32[]{:S(2)}) collective-permute-start(bf16[8,56,1600]{2,1,0:T(8,128)(2,1)} %get-tuple-element.118), channel_id=1, source_target_pairs={{0,24},{8,16},{16,8},{24,0},{1,25},{9,17},{17,9},{25,1},{2,26},{10... | collective-permute-start | bytes 4300808 | tf_op jit(solution)/shard_map/ppermute | solution.py:28
  469.5 58.1 %collective-permute-start.39 = (bf16[8,56,1600]{2,1,0:T(8,128)(2,1)}, bf16[8,56,1600]{2,1,0:T(8,128)(2,1)}, u32[]{:S(2)}, u32[]{:S(2)}) collective-permute-start(bf16[8,56,1600]{2,1,0:T(8,128)(2,1)} %join_hidden.1.refs_0_), channel_id=1, source_target_pairs={{0,8},{8,0},{16,24},{24,16},{1,9},{9,1},{17,25},{25,17},{2,10},{10... | collective-permute-start | bytes 4300808 | tf_op jit(solution)/shard_map/ppermute | solution.py:28
  470.6 67.4 %collective-permute-start.44 = (bf16[8,56,1600]{2,1,0:T(8,128)(2,1)}, bf16[8,56,1600]{2,1,0:T(8,128)(2,1)}, u32[]{:S(2)}, u32[]{:S(2)}) collective-permute-start(bf16[8,56,1600]{2,1,0:T(8,128)(2,1)} %join_hidden.1.refs_0_), channel_id=1, source_target_pairs={{0,24},{8,16},{16,8},{24,0},{1,25},{9,17},{17,9},{25,1},{2,26},{10... | collective-permute-start | bytes 4300808 | tf_op jit(solution)/shard_map/ppermute | solution.py:28
  472.3 86.8 %collective-permute-start.43 = (bf16[8,56,1600]{2,1,0:T(8,128)(2,1)}, bf16[8,56,1600]{2,1,0:T(8,128)(2,1)}, u32[]{:S(2)}, u32[]{:S(2)}) collective-permute-start(bf16[8,56,1600]{2,1,0:T(8,128)(2,1)} %join_hidden.1.refs_0_), channel_id=1, source_target_pairs={{0,16},{8,24},{16,0},{24,8},{1,17},{9,25},{17,1},{25,9},{2,18},{10... | collective-permute-start | bytes 4300808 | tf_op jit(solution)/shard_map/ppermute | solution.py:28
  530.8 51.7 %collective-permute-start.42 = (bf16[5,56,1600]{2,1,0:T(8,128)(2,1)}, bf16[5,56,1600]{2,1,0:T(8,128)(2,1)}, u32[]{:S(2)}, u32[]{:S(2)}) collective-permute-start(bf16[5,56,1600]{2,1,0:T(8,128)(2,1)} %join_last.1.refs_0_), channel_id=1, source_target_pairs={{0,24},{8,16},{16,8},{24,0},{1,25},{9,17},{17,9},{25,1},{2,26},{10... | collective-permute-start | bytes 2688008 | tf_op jit(solution)/shard_map/ppermute | solution.py:28
  532.1 50.5 %collective-permute-start.41 = (bf16[5,56,1600]{2,1,0:T(8,128)(2,1)}, bf16[5,56,1600]{2,1,0:T(8,128)(2,1)}, u32[]{:S(2)}, u32[]{:S(2)}) collective-permute-start(bf16[5,56,1600]{2,1,0:T(8,128)(2,1)} %join_last.1.refs_0_), channel_id=1, source_target_pairs={{0,16},{8,24},{16,0},{24,8},{1,17},{9,25},{17,1},{25,9},{2,18},{10... | collective-permute-start | bytes 2688008 | tf_op jit(solution)/shard_map/ppermute | solution.py:28
  533.6 48.9 %collective-permute-start.40 = (bf16[5,56,1600]{2,1,0:T(8,128)(2,1)}, bf16[5,56,1600]{2,1,0:T(8,128)(2,1)}, u32[]{:S(2)}, u32[]{:S(2)}) collective-permute-start(bf16[5,56,1600]{2,1,0:T(8,128)(2,1)} %join_last.1.refs_0_), channel_id=1, source_target_pairs={{0,8},{8,0},{16,24},{24,16},{1,9},{9,1},{17,25},{25,17},{2,10},{10... | collective-permute-start | bytes 2688008 | tf_op jit(solution)/shard_map/ppermute | solution.py:28
  (96 other events, 1696.1 us)
Sparse Core Ops, SparseCore 0:
  9.7 53.5 all-gather.4
  65.7 40.2 all-gather.6
  109.6 40.2 all-gather.8
  193.4 40.7 all-gather.10
  261.2 42.8 reduce-scatter.4
  307.0 66.0 reduce-scatter.6
  375.5 55.4 reduce-scatter.10
  469.6 69.5 reduce-scatter.8

commit v5 on v4

--- a/solution.py
+++ b/solution.py
@@ -831,6 +831,7 @@
     )
     projected_grad = jnp.concatenate([query_grads, key_grads, value_grads], 1)
     first_part = mm(projected_grad, w_qkv, 1, 1)
+    first_part = with_layout_constraint(first_part, Layout((0, 1)))
 
     def head_sums(block):
         sums = jnp.sum(block.astype(full), axis=0)
@@ -866,7 +867,9 @@
     last = to_copies(last)
 
     fc_sums, rest = sum_hidden(where, [hidden_sum], count, ff_cols)
-    hidden_joined = join_hidden(where, *exchange(fc_sums), rest)
+    fc_sums, fc_sums_far = exchange(fc_sums)
+    output_low = tie(active_low, fc_sums[1])
+    hidden_joined = join_hidden(where, fc_sums, fc_sums_far, tie(rest, *last[1:]))
     hidden_stacks = from_copies(hidden_joined)
     fc_grad, proj_grad, fbias = finish_hidden(
         where, hidden_stacks, count, own_rows, ff_cols, ff_cols, hidden_sums.shape[2]
@@ -875,18 +878,18 @@
 
     last[0] = tie(last[0], hidden_joined)
     last = sum_last(where, last, count, 3 * width)
-    output_low = tie(active_low, last[0])
     last = [last[0]] + [xor_send(last[j], "shard", evens[j]) for j in range(1, half)]
+    _, pull_first = jax.vjp(lambda rows: layer_norm(rows, g_first, s_first), in_rows)
+    (input_part,) = pull_first(first_grad)
+    tokens_grad = (middle_grad + input_part).astype(low)
+    last[1] = tie(last[1], tokens_grad)
     far = xor_send(odd_last(where, last, 3 * width), "shard", 1)
     last = from_copies(join_last(where, last, tie(far, hidden_stacks[1])))
     output_part = mm(output_low, proj_weight, 1, 0).astype(low)
     output = middle + b_proj + scatter_rows(output_part).astype(full)
 
-    _, pull_first = jax.vjp(lambda rows: layer_norm(rows, g_first, s_first), in_rows)
-    (input_part,) = pull_first(first_grad)
-    tokens_grad = (middle_grad + input_part).astype(low)
     output = output.astype(low)
-    last[0] = tie(last[0], output, tokens_grad)
+    last[0] = tie(last[0], output)
 
     qkv_grad, outw_grad, sums = finish_last(where, last, count, own_rows, width)
     sums = sums.reshape(copies, 16 * 64)[:, :share].reshape(8, own_rows)

time: 602 us -> 610 us (1.013)
  waiting for transfers between devices: 279 us -> 299 us
  local copies, waits for them, and re-layouts: 52.9 us -> 46.2 us
    ppermute x45, waiting for transfers between devices: 207 us -> 228 us  [xor_send(): return lax.ppermute(block, axis, [(i, i ^ bits) for i in range(count)])]
    unnamed x144 -> x152, local copies, waits for them, and re-layouts: 22.6 us -> 27 us
  transfers between devices with their start and end apart: 53 -> 53, of which waited for: 24 -> 25; matrix products, arithmetic and copies ran while one was open for 21% -> 18% of each run, Pallas kernels for 15% -> 15%
where the time goes in v5:
time: 610 us; the launch traced here: 605 us
  waiting for transfers between devices  299 us (49%)
  Pallas kernels  97.2 us (16%)
  matrix products  80.1 us (13%)
  starting transfers between devices  49 us (8%)
  local copies, waits for them, and re-layouts  46.2 us (8%)
  other arithmetic  17.9 us (3%)
  between operations  15.7 us (3%)
    ppermute x45, waiting for transfers between devices, xor_send(): return lax.ppermute(block, axis, [(i, i ^ bits) for i in range(count)])  228 us
    dot_general x12, matrix products, mm(): lax.dot_general(left_side, right_side, (((left_dim,), (right_dim,)), ((),...  79.7 us
    pallas_call x18, Pallas kernels, local_call(): pl.pallas_call(kernel, out_shape=tuple(shapes) if many else shapes, in_sp...  77.9 us
    ppermute x45, starting transfers between devices, xor_send(): return lax.ppermute(block, axis, [(i, i ^ bits) for i in range(count)])  48.3 us
    all_gather x1, waiting for transfers between devices, on_device(): lax.all_gather(qkv_stack.reshape(count * span, 3 * width), 'replica')  31.2 us
    unnamed x152, local copies, waits for them, and re-layouts  27 us
    all_gather x3, waiting for transfers between devices, gather_rows(): return lax.all_gather(block, 'shard', axis=0, tiled=True)  22.6 us
    reduce_scatter x3, waiting for transfers between devices, scatter_rows(): return lax.psum_scatter(blocks, 'shard', scatter_dimension=0, tiled=True)  16.9 us
  transfers between devices with their start and end apart: 53, of which 25 were waited for; matrix products, arithmetic and copies ran while one was open for 18% of the time, Pallas kernels for 15%

profile of v5, /device:TPU:0, one launch (start us, length us, event | category | flops | bytes accessed | tf_op | source)
XLA Modules:
  0.0 605.0 jit_solution(228066561270654208)
XLA Ops:
  23.1 13.2 %collective-permute-done.1 = bf16[2,56,768]{2,1,0:T(8,128)(2,1)S(1)} collective-permute-done((bf16[2,56,768]{2,1,0:T(8,128)(2,1)}, bf16[2,56,768]{2,1,0:T(8,128)(2,1)S(1)}, u32[]{:S(2)}, u32[]{:S(2)}) %collective-permute-start.1) | collective-permute-done | bytes 172064 | tf_op jit(solution)/shard_map/ppermute | solution.py:28
  40.1 22.6 %all-gather.5.cloned.1.call-done = bf16[1024,1600]{1,0:T(8,128)(2,1)} async-done(((bf16[128,1600]{1,0:T(8,128)(2,1)}), bf16[1024,1600]{1,0:T(8,128)(2,1)}) %all-gather.5.cloned.1.call-update) | async-done | bytes 3276816 | tf_op jit(solution)/shard_map/all_gather | solution.py:704
  74.8 31.2 %all-gather.7.cloned.1.call-done = bf16[4,448,768]{2,1,0:T(8,128)(2,1)} async-done(((bf16[1,448,768]{2,1,0:T(8,128)(2,1)}), bf16[4,448,768]{2,1,0:T(8,128)(2,1)}) %all-gather.7.cloned.1.call-update) | async-done | bytes 2752528 | tf_op jit(solution)/shard_map/all_gather | solution.py:752
  133.3 8.2 %attend_forward.1 = (bf16[1024,256]{1,0:T(8,128)(2,1)S(1)}, f32[1,4,1024]{2,1,0:T(4,128)S(1)}) custom-call(s32[3,8]{1,0:T(4,128)S(1)} %pad_add_fusion.order_ref, bf16[1024,256]{1,0:T(8,128)(2,1)S(1)} %get-tuple-element.238.q_ref, bf16[1024,256]{1,0:T(8,128)(2,1)S(1)} %slice.248.k_ref, bf16[1024,256]{1,0:T(8,128)(2,1)S(1)} %get-tuple-element.237.v_ref), custom_call_target="tpu_custom_call" | custom-call | flops 4294967296 | bytes 2097152 | tf_op jit(solution)/shard_map/attend_forward/pallas_call | solution.py:180
  141.6 7.5 %collective-permute-done.10.refs_4_ = bf16[4,56,1600]{2,1,0:T(8,128)(2,1)} collective-permute-done((bf16[4,56,1600]{2,1,0:T(8,128)(2,1)}, bf16[4,56,1600]{2,1,0:T(8,128)(2,1)}, u32[]{:S(2)}, u32[]{:S(2)}) %collective-permute-start.10) | collective-permute-done | bytes 716832 | tf_op jit(solution)/shard_map/ppermute | solution.py:28
  154.1 8.5 %collective-permute-done.13.refs_2_ = bf16[2,128,256]{2,1,0:T(8,128)(2,1)S(1)} collective-permute-done((bf16[2,128,256]{2,1,0:T(8,128)(2,1)S(1)}, bf16[2,128,256]{2,1,0:T(8,128)(2,1)S(1)}, u32[]{:S(2)}, u32[]{:S(2)}) %collective-permute-start.13) | collective-permute-done | bytes 131104 | tf_op jit(solution)/shard_map/ppermute | solution.py:28
  196.5 16.1 %collective-permute-done.22.refs_3_ = bf16[8,56,800]{2,1,0:T(8,128)(2,1)S(1)} collective-permute-done((bf16[8,56,800]{2,1,0:T(8,128)(2,1)}, bf16[8,56,800]{2,1,0:T(8,128)(2,1)S(1)}, u32[]{:S(2)}, u32[]{:S(2)}) %collective-permute-start.22) | collective-permute-done | bytes 716832 | tf_op jit(solution)/shard_map/ppermute | solution.py:28
  212.6 17.1 %collective-permute-done.21.refs_2_ = bf16[8,56,800]{2,1,0:T(8,128)(2,1)S(1)} collective-permute-done((bf16[8,56,800]{2,1,0:T(8,128)(2,1)}, bf16[8,56,800]{2,1,0:T(8,128)(2,1)S(1)}, u32[]{:S(2)}, u32[]{:S(2)}) %collective-permute-start.21) | collective-permute-done | bytes 716832 | tf_op jit(solution)/shard_map/ppermute | solution.py:28
  241.1 11.8 %convert_reduce_fusion.1 = (f32[800]{0:T(1024)}, bf16[1024,800]{0,1:T(8,128)(2,1)S(1)}, bf16[1024,800]{0,1:T(8,128)(2,1)}) fusion(f32[1024,800]{0,1:T(8,128)} %fusion.61, f32[800]{0:T(1024)} %convert_element_type.92, bf16[1024,1600]{1,0:T(8,128)(2,1)} %all-gather.11.cloned.1.call-done, bf16[1600,800]{1,0:T(8,128)(2,1)} %bitcast.92), kind=kOutput, calls=%fused_computation.22 | convolution fusion | flops 2645196032 | bytes 12396800 | tf_op jit(solution)/shard_map/dot_general | solution.py:49
  262.4 8.0 %fusion.60.proj_ref = f32[800,1600]{1,0:T(8,128)} fusion(bf16[1024,800]{0,1:T(8,128)(2,1)} %get-tuple-element.113, bf16[1024,1600]{0,1:T(8,128)(2,1)} %all-gather.9.cloned.1.call-done), kind=kOutput, calls=%fused_computation.144 | convolution fusion | flops 2621440000 | bytes 10035200 | tf_op jit(solution)/shard_map/dot_general | solution.py:49
  276.0 7.7 %pack_hidden.1 = bf16[4,8,56,1600]{3,2,1,0:T(8,128)(2,1)} custom-call(s32[2]{0:T(128)} %pad_add_fusion.1.where_ref, f32[8,200,800]{2,1,0:T(8,128)} %bitcast.90, f32[800,1600]{1,0:T(8,128)} %fusion.60.proj_ref, f32[4,16,256]{2,1,0:T(8,128)} %pad.22.sums_ref), custom_call_target="tpu_custom_call" | custom-call | bytes 30916608 | tf_op jit(solution)/shard_map/pack_hidden/pallas_call | solution.py:240
  285.9 16.9 %reduce-scatter.7.cloned.1.call-done = bf16[128,1600]{1,0:T(8,128)(2,1)} async-done(((bf16[1024,1600]{1,0:T(8,128)(2,1)}), bf16[128,1600]{1,0:T(8,128)(2,1)}) %reduce-scatter.7.cloned.1.call-update) | async-done | bytes 409616 | tf_op jit(solution)/shard_map/reduce_scatter | solution.py:708
  334.0 11.1 %attend_backward.1 = (bf16[1024,256]{1,0:T(8,128)(2,1)S(1)}, bf16[1024,256]{1,0:T(8,128)(2,1)S(1)}, bf16[1024,256]{1,0:T(8,128)(2,1)S(1)}) custom-call(s32[3,8]{1,0:T(4,128)S(1)} %pad_add_fusion.order_ref, bf16[1024,256]{1,0:T(8,128)(2,1)S(1)} %copy-done.7, bf16[1024,256]{1,0:T(8,128)(2,1)S(1)} %copy-done.3, bf16[1024,256]{1,0:T(8,128)(2,1)S(1)} %copy-done.5, ...), custom_call_target="tpu_custom_call" | custom-call | flops 10737418240 | bytes 3670016 | tf_op jit(solution)/shard_map/attend_backward/pallas_call | solution.py:203
  368.3 7.9 %fusion.40 = f32[1600,768]{1,0:T(8,128)} fusion(bf16[1024,768]{1,0:T(8,128)(2,1)} %copy-done.41, bf16[1024,1600]{1,0:T(8,128)(2,1)} %all-gather.5.cloned.1.call-done, f32[1600]{0:T(1024)S(1)} %copy-done.48, f32[1600]{0:T(1024)S(1)} %mul.199, f32[1024]{0:T(1024)S(1)} %copy-done.52, f32[1024]{0:T(1024)S(1)} %broadcast_multiply_fusion), kind=kOutput, calls=%fused_computation.128 | convolution fusion | flops 2526412800 | bytes 9785856 | tf_op jit(solution)/shard_map/dot_general | solution.py:49
  388.1 10.9 %collective-permute-done.28.refs_1_ = bf16[2,56,800]{2,1,0:T(8,128)(2,1)S(1)} collective-permute-done((bf16[2,56,800]{2,1,0:T(8,128)(2,1)}, bf16[2,56,800]{2,1,0:T(8,128)(2,1)S(1)}, u32[]{:S(2)}, u32[]{:S(2)}) %collective-permute-start.28) | collective-permute-done | bytes 179232 | tf_op jit(solution)/shard_map/ppermute | solution.py:28
  399.1 7.6 %convolution_convert_fusion = bf16[1024,1600]{1,0:T(8,128)(2,1)} fusion(bf16[1024,800]{0,1:T(8,128)(2,1)} %get-tuple-element.113, bf16[800,1600]{1,0:T(8,128)(2,1)S(1)} %copy-done), kind=kOutput, calls=%fused_computation.14 | convolution fusion | flops 2623078400 | bytes 7475200 | tf_op jit(solution)/shard_map/dot_general | solution.py:49
  413.7 18.0 %collective-permute-done.29.refs_2_ = bf16[2,56,800]{2,1,0:T(8,128)(2,1)S(1)} collective-permute-done((bf16[2,56,800]{2,1,0:T(8,128)(2,1)}, bf16[2,56,800]{2,1,0:T(8,128)(2,1)S(1)}, u32[]{:S(2)}, u32[]{:S(2)}) %collective-permute-start.29) | collective-permute-done | bytes 179232 | tf_op jit(solution)/shard_map/ppermute | solution.py:28
  432.7 9.7 %collective-permute-done.32.refs_1_ = bf16[8,56,1600]{2,1,0:T(8,128)(2,1)S(1)} collective-permute-done((bf16[8,56,1600]{2,1,0:T(8,128)(2,1)}, bf16[8,56,1600]{2,1,0:T(8,128)(2,1)S(1)}, u32[]{:S(2)}, u32[]{:S(2)}) %collective-permute-start.32) | collective-permute-done | bytes 1433632 | tf_op jit(solution)/shard_map/ppermute | solution.py:28
  442.5 32.4 %collective-permute-done.33.refs_2_ = bf16[8,56,1600]{2,1,0:T(8,128)(2,1)S(1)} collective-permute-done((bf16[8,56,1600]{2,1,0:T(8,128)(2,1)}, bf16[8,56,1600]{2,1,0:T(8,128)(2,1)S(1)}, u32[]{:S(2)}, u32[]{:S(2)}) %collective-permute-start.33) | collective-permute-done | bytes 1433632 | tf_op jit(solution)/shard_map/ppermute | solution.py:28
  490.7 12.6 %collective-permute-done.35.refs_1_ = bf16[2,56,1600]{2,1,0:T(8,128)(2,1)} collective-permute-done((bf16[2,56,1600]{2,1,0:T(8,128)(2,1)}, bf16[2,56,1600]{2,1,0:T(8,128)(2,1)}, u32[]{:S(2)}, u32[]{:S(2)}) %collective-permute-start.35) | collective-permute-done | bytes 358432 | tf_op jit(solution)/shard_map/ppermute | solution.py:28
  505.3 9.4 %collective-permute-done.37.refs_3_ = bf16[2,56,1600]{2,1,0:T(8,128)(2,1)S(1)} collective-permute-done((bf16[2,56,1600]{2,1,0:T(8,128)(2,1)S(1)}, bf16[2,56,1600]{2,1,0:T(8,128)(2,1)S(1)}, u32[]{:S(2)}, u32[]{:S(2)}) %collective-permute-start.37) | collective-permute-done | bytes 358432 | tf_op jit(solution)/shard_map/ppermute | solution.py:28
  517.5 28.4 %collective-permute-done.39.refs_1_ = bf16[8,56,1600]{2,1,0:T(8,128)(2,1)} collective-permute-done((bf16[8,56,1600]{2,1,0:T(8,128)(2,1)}, bf16[8,56,1600]{2,1,0:T(8,128)(2,1)}, u32[]{:S(2)}, u32[]{:S(2)}) %collective-permute-start.39) | collective-permute-done | bytes 1433632 | tf_op jit(solution)/shard_map/ppermute | solution.py:28
  552.9 9.8 %finish_hidden.1 = (f32[200,6400]{1,0:T(8,128)}, f32[800,1600]{1,0:T(8,128)}, f32[4,16,256]{2,1,0:T(8,128)}) custom-call(s32[2]{0:T(128)} %pad_add_fusion.1.where_ref, bf16[8,56,1600]{2,1,0:T(8,128)(2,1)} %join_hidden.1.refs_0_, bf16[8,56,1600]{2,1,0:T(8,128)(2,1)} %collective-permute-done.39.refs_1_, bf16[8,56,1600]{2,1,0:T(8,128)(2,1)} %collective-permute-done.43.refs_2_, ...), custom_call_target="tpu_custom_call" | custom-call | bytes 17203200 | tf_op jit(solution)/shard_map/finish_hidden/pallas_call | solution.py:240
  574.1 17.1 %collective-permute-done.41.refs_2_ = bf16[5,56,1600]{2,1,0:T(8,128)(2,1)} collective-permute-done((bf16[5,56,1600]{2,1,0:T(8,128)(2,1)}, bf16[5,56,1600]{2,1,0:T(8,128)(2,1)}, u32[]{:S(2)}, u32[]{:S(2)}) %collective-permute-start.41) | collective-permute-done | bytes 896032 | tf_op jit(solution)/shard_map/ppermute | solution.py:28
  (381 shorter events, 245.5 us)
Async XLA Ops:
  7.3 55.5 %all-gather.5.cloned.1.call-start = ((), (), s32[]{:S(2)}) async-start(), calls=%async_computation.4 | async-start | bytes 3833856 | tf_op jit(solution)/shard_map/all_gather | solution.py:704
  9.5 96.5 %all-gather.7.cloned.1.call-start = ((), (), s32[]{:S(2)}) async-start(), calls=%async_computation.5 | async-start | bytes 3440640 | tf_op jit(solution)/shard_map/all_gather | solution.py:752
  39.0 153.1 %all-gather.9.cloned.1.call-start = ((), (), s32[]{:S(2)}) async-start(), calls=%async_computation.6 | async-start | bytes 3686400 | tf_op jit(solution)/shard_map/all_gather | solution.py:704
  67.2 38.8 %collective-permute-start.4 = (bf16[120,1600]{1,0:T(8,128)(2,1)}, bf16[120,1600]{1,0:T(8,128)(2,1)S(1)}, u32[]{:S(2)}, u32[]{:S(2)}) collective-permute-start(bf16[120,1600]{1,0:T(8,128)(2,1)} %get-tuple-element.82), channel_id=1, source_target_pairs={{0,2},{1,3},{2,0},{3,1},{4,6},{5,7},{6,4},{7,5},{8,10},{9,11},{10,... | collective-permute-start | bytes 1152008 | tf_op jit(solution)/shard_map/ppermute | solution.py:28
  67.2 38.8 %collective-permute-start.5 = (bf16[120,1600]{1,0:T(8,128)(2,1)}, bf16[120,1600]{1,0:T(8,128)(2,1)S(1)}, u32[]{:S(2)}, u32[]{:S(2)}) collective-permute-start(bf16[120,1600]{1,0:T(8,128)(2,1)} %get-tuple-element.83), channel_id=1, source_target_pairs={{0,4},{1,5},{2,6},{3,7},{4,0},{5,1},{6,2},{7,3},{8,12},{9,13},{10,... | collective-permute-start | bytes 1152008 | tf_op jit(solution)/shard_map/ppermute | solution.py:28
  70.2 35.8 %collective-permute-start.6 = (bf16[120,1600]{1,0:T(8,128)(2,1)}, bf16[120,1600]{1,0:T(8,128)(2,1)}, u32[]{:S(2)}, u32[]{:S(2)}) collective-permute-start(bf16[120,1600]{1,0:T(8,128)(2,1)} %get-tuple-element.84), channel_id=1, source_target_pairs={{0,6},{1,7},{2,4},{3,5},{4,2},{5,3},{6,0},{7,1},{8,14},{9,15},{10,... | collective-permute-start | bytes 1152008 | tf_op jit(solution)/shard_map/ppermute | solution.py:28
  109.8 131.3 %all-gather.11.cloned.1.call-start = ((), (), s32[]{:S(2)}) async-start(), calls=%async_computation.7 | async-start | bytes 3833856 | tf_op jit(solution)/shard_map/all_gather | solution.py:704
  114.9 34.1 %collective-permute-start.10 = (bf16[4,56,1600]{2,1,0:T(8,128)(2,1)}, bf16[4,56,1600]{2,1,0:T(8,128)(2,1)}, u32[]{:S(2)}, u32[]{:S(2)}) collective-permute-start(bf16[4,56,1600]{2,1,0:T(8,128)(2,1)} %get-tuple-element.89.refs_0_), channel_id=1, source_target_pairs={{0,16},{8,24},{16,0},{24,8},{1,17},{9,25},{17,1},{25,9},{2,18},{10... | collective-permute-start | bytes 2150408 | tf_op jit(solution)/shard_map/ppermute | solution.py:28
  116.4 32.7 %collective-permute-start.9 = (bf16[4,56,1600]{2,1,0:T(8,128)(2,1)}, bf16[4,56,1600]{2,1,0:T(8,128)(2,1)}, u32[]{:S(2)}, u32[]{:S(2)}) collective-permute-start(bf16[4,56,1600]{2,1,0:T(8,128)(2,1)} %get-tuple-element.89.refs_0_), channel_id=1, source_target_pairs={{0,8},{8,0},{16,24},{24,16},{1,9},{9,1},{17,25},{25,17},{2,10},{10... | collective-permute-start | bytes 2150408 | tf_op jit(solution)/shard_map/ppermute | solution.py:28
  192.2 110.6 %reduce-scatter.7.cloned.1.call-start = ((), (), s32[]{:S(2)}) async-start(), calls=%async_computation.9 | async-start | bytes 3833856 | tf_op jit(solution)/shard_map/reduce_scatter | solution.py:708
  193.8 36.0 %collective-permute-start.21 = (bf16[8,56,800]{2,1,0:T(8,128)(2,1)}, bf16[8,56,800]{2,1,0:T(8,128)(2,1)S(1)}, u32[]{:S(2)}, u32[]{:S(2)}) collective-permute-start(bf16[8,56,800]{2,1,0:T(8,128)(2,1)} %constant_dynamic-update-slice_fusion.1.refs_0_), channel_id=1, source_target_pairs={{0,16},{8,24},{16,0},{24,8},{1,17},{9,25},{17,1},{25,9},{2,18},{10... | collective-permute-start | bytes 2150408 | tf_op jit(solution)/shard_map/ppermute | solution.py:28
  259.7 123.8 %reduce-scatter.5.cloned.1.call-start = ((), (), s32[]{:S(2)}) async-start(), calls=%async_computation.8 | async-start | bytes 7454720 | tf_op jit(solution)/shard_map/reduce_scatter | solution.py:811
  283.7 205.0 %reduce-scatter.11.cloned.1.call-start = ((), (), s32[]{:S(2)}) async-start(), calls=%async_computation.11 | async-start | bytes 3833856 | tf_op jit(solution)/shard_map/reduce_scatter | solution.py:708
  350.0 216.0 %reduce-scatter.9.cloned.1.call-start = ((), (), s32[]{:S(2)}) async-start(), calls=%async_computation.10 | async-start | bytes 3833856 | tf_op jit(solution)/shard_map/reduce_scatter | solution.py:708
  406.7 35.8 %collective-permute-start.32 = (bf16[8,56,1600]{2,1,0:T(8,128)(2,1)}, bf16[8,56,1600]{2,1,0:T(8,128)(2,1)S(1)}, u32[]{:S(2)}, u32[]{:S(2)}) collective-permute-start(bf16[8,56,1600]{2,1,0:T(8,128)(2,1)} %get-tuple-element.119), channel_id=1, source_target_pairs={{0,8},{8,0},{16,24},{24,16},{1,9},{9,1},{17,25},{25,17},{2,10},{10... | collective-permute-start | bytes 4300808 | tf_op jit(solution)/shard_map/ppermute | solution.py:28
  408.2 66.6 %collective-permute-start.33 = (bf16[8,56,1600]{2,1,0:T(8,128)(2,1)}, bf16[8,56,1600]{2,1,0:T(8,128)(2,1)S(1)}, u32[]{:S(2)}, u32[]{:S(2)}) collective-permute-start(bf16[8,56,1600]{2,1,0:T(8,128)(2,1)} %get-tuple-element.120), channel_id=1, source_target_pairs={{0,16},{8,24},{16,0},{24,8},{1,17},{9,25},{17,1},{25,9},{2,18},{10... | collective-permute-start | bytes 4300808 | tf_op jit(solution)/shard_map/ppermute | solution.py:28
  409.8 65.0 %collective-permute-start.34 = (bf16[8,56,1600]{2,1,0:T(8,128)(2,1)}, bf16[8,56,1600]{2,1,0:T(8,128)(2,1)S(1)}, u32[]{:S(2)}, u32[]{:S(2)}) collective-permute-start(bf16[8,56,1600]{2,1,0:T(8,128)(2,1)} %get-tuple-element.121), channel_id=1, source_target_pairs={{0,24},{8,16},{16,8},{24,0},{1,25},{9,17},{17,9},{25,1},{2,26},{10... | collective-permute-start | bytes 4300808 | tf_op jit(solution)/shard_map/ppermute | solution.py:28
  432.5 42.3 %collective-permute-start.31 = (bf16[4,56,800]{2,1,0:T(8,128)(2,1)S(1)}, bf16[4,56,800]{2,1,0:T(8,128)(2,1)S(1)}, u32[]{:S(2)}, u32[]{:S(2)}) collective-permute-start(bf16[4,56,800]{2,1,0:T(8,128)(2,1)S(1)} %pad_maximum_fusion), channel_id=1, source_target_pairs={{0,1},{1,0},{2,3},{3,2},{4,5},{5,4},{6,7},{7,6},{8,9},{9,8},{10,11... | collective-permute-start | bytes 1075208 | tf_op jit(solution)/shard_map/ppermute | solution.py:28
  478.9 74.0 %collective-permute-start.44 = (bf16[8,56,1600]{2,1,0:T(8,128)(2,1)}, bf16[8,56,1600]{2,1,0:T(8,128)(2,1)}, u32[]{:S(2)}, u32[]{:S(2)}) collective-permute-start(bf16[8,56,1600]{2,1,0:T(8,128)(2,1)} %join_hidden.1.refs_0_), channel_id=1, source_target_pairs={{0,24},{8,16},{16,8},{24,0},{1,25},{9,17},{17,9},{25,1},{2,26},{10... | collective-permute-start | bytes 4300808 | tf_op jit(solution)/shard_map/ppermute | solution.py:28
  480.4 72.5 %collective-permute-start.43 = (bf16[8,56,1600]{2,1,0:T(8,128)(2,1)}, bf16[8,56,1600]{2,1,0:T(8,128)(2,1)}, u32[]{:S(2)}, u32[]{:S(2)}) collective-permute-start(bf16[8,56,1600]{2,1,0:T(8,128)(2,1)} %join_hidden.1.refs_0_), channel_id=1, source_target_pairs={{0,16},{8,24},{16,0},{24,8},{1,17},{9,25},{17,1},{25,9},{2,18},{10... | collective-permute-start | bytes 4300808 | tf_op jit(solution)/shard_map/ppermute | solution.py:28
  481.4 64.6 %collective-permute-start.39 = (bf16[8,56,1600]{2,1,0:T(8,128)(2,1)}, bf16[8,56,1600]{2,1,0:T(8,128)(2,1)}, u32[]{:S(2)}, u32[]{:S(2)}) collective-permute-start(bf16[8,56,1600]{2,1,0:T(8,128)(2,1)} %join_hidden.1.refs_0_), channel_id=1, source_target_pairs={{0,8},{8,0},{16,24},{24,16},{1,9},{9,1},{17,25},{25,17},{2,10},{10... | collective-permute-start | bytes 4300808 | tf_op jit(solution)/shard_map/ppermute | solution.py:28
  517.5 28.4 %collective-permute-start.38 = (bf16[4,56,832]{2,1,0:T(8,128)(2,1)}, bf16[4,56,832]{2,1,0:T(8,128)(2,1)S(1)}, u32[]{:S(2)}, u32[]{:S(2)}) collective-permute-start(bf16[4,56,832]{2,1,0:T(8,128)(2,1)} %odd_last.1), channel_id=1, source_target_pairs={{0,1},{1,0},{2,3},{3,2},{4,5},{5,4},{6,7},{7,6},{8,9},{9,8},{10,11... | collective-permute-start | bytes 1118216 | tf_op jit(solution)/shard_map/ppermute | solution.py:28
  550.4 40.8 %collective-permute-start.41 = (bf16[5,56,1600]{2,1,0:T(8,128)(2,1)}, bf16[5,56,1600]{2,1,0:T(8,128)(2,1)}, u32[]{:S(2)}, u32[]{:S(2)}) collective-permute-start(bf16[5,56,1600]{2,1,0:T(8,128)(2,1)} %join_last.1.refs_0_), channel_id=1, source_target_pairs={{0,16},{8,24},{16,0},{24,8},{1,17},{9,25},{17,1},{25,9},{2,18},{10... | collective-permute-start | bytes 2688008 | tf_op jit(solution)/shard_map/ppermute | solution.py:28
  550.8 40.4 %collective-permute-start.40 = (bf16[5,56,1600]{2,1,0:T(8,128)(2,1)}, bf16[5,56,1600]{2,1,0:T(8,128)(2,1)}, u32[]{:S(2)}, u32[]{:S(2)}) collective-permute-start(bf16[5,56,1600]{2,1,0:T(8,128)(2,1)} %join_last.1.refs_0_), channel_id=1, source_target_pairs={{0,8},{8,0},{16,24},{24,16},{1,9},{9,1},{17,25},{25,17},{2,10},{10... | collective-permute-start | bytes 2688008 | tf_op jit(solution)/shard_map/ppermute | solution.py:28
  (100 other events, 1668.9 us)
Sparse Core Ops, SparseCore 0:
  9.8 52.9 all-gather.4
  65.2 40.7 all-gather.6
  109.9 40.2 all-gather.8
  192.3 40.7 all-gather.10
  259.8 42.9 reduce-scatter.6
  305.7 66.0 reduce-scatter.4
  374.7 53.2 reduce-scatter.10
  430.9 43.1 reduce-scatter.8

commit v6 on v5

--- a/solution.py
+++ b/solution.py
@@ -867,9 +867,7 @@
     last = to_copies(last)
 
     fc_sums, rest = sum_hidden(where, [hidden_sum], count, ff_cols)
-    fc_sums, fc_sums_far = exchange(fc_sums)
-    output_low = tie(active_low, fc_sums[1])
-    hidden_joined = join_hidden(where, fc_sums, fc_sums_far, tie(rest, *last[1:]))
+    hidden_joined = join_hidden(where, *exchange(fc_sums), rest)
     hidden_stacks = from_copies(hidden_joined)
     fc_grad, proj_grad, fbias = finish_hidden(
         where, hidden_stacks, count, own_rows, ff_cols, ff_cols, hidden_sums.shape[2]
@@ -878,6 +876,7 @@
 
     last[0] = tie(last[0], hidden_joined)
     last = sum_last(where, last, count, 3 * width)
+    output_low = tie(active_low, last[0])
     last = [last[0]] + [xor_send(last[j], "shard", evens[j]) for j in range(1, half)]
     _, pull_first = jax.vjp(lambda rows: layer_norm(rows, g_first, s_first), in_rows)
     (input_part,) = pull_first(first_grad)

time: 610 us -> 596 us (0.977)
  waiting for transfers between devices: 299 us -> 282 us
    ppermute x45, waiting for transfers between devices: 228 us -> 211 us  [xor_send(): return lax.ppermute(block, axis, [(i, i ^ bits) for i in range(count)])]
    unnamed x152 -> x146, local copies, waits for them, and re-layouts: 27 us -> 27.1 us
  transfers between devices with their start and end apart: 53 -> 53, of which waited for: 25 -> 25; matrix products, arithmetic and copies ran while one was open for 18% -> 19% of each run, Pallas kernels for 15% -> 15%
where the time goes in v6:
time: 596 us; the launch traced here: 590 us
  waiting for transfers between devices  282 us (47%)
  Pallas kernels  96.9 us (16%)
  matrix products  78.1 us (13%)
  starting transfers between devices  52 us (9%)
  local copies, waits for them, and re-layouts  47.2 us (8%)
  other arithmetic  17.9 us (3%)
  between operations  15.7 us (3%)
    ppermute x45, waiting for transfers between devices, xor_send(): return lax.ppermute(block, axis, [(i, i ^ bits) for i in range(count)])  211 us
    dot_general x12, matrix products, mm(): lax.dot_general(left_side, right_side, (((left_dim,), (right_dim,)), ((),...  77.7 us
    pallas_call x18, Pallas kernels, local_call(): pl.pallas_call(kernel, out_shape=tuple(shapes) if many else shapes, in_sp...  77.7 us
    ppermute x45, starting transfers between devices, xor_send(): return lax.ppermute(block, axis, [(i, i ^ bits) for i in range(count)])  51.3 us
    all_gather x1, waiting for transfers between devices, on_device(): lax.all_gather(qkv_stack.reshape(count * span, 3 * width), 'replica')  31.2 us
    unnamed x146, local copies, waits for them, and re-layouts  27.1 us
    all_gather x3, waiting for transfers between devices, gather_rows(): return lax.all_gather(block, 'shard', axis=0, tiled=True)  22.6 us
    reduce_scatter x3, waiting for transfers between devices, scatter_rows(): return lax.psum_scatter(blocks, 'shard', scatter_dimension=0, tiled=True)  16.8 us
  transfers between devices with their start and end apart: 53, of which 25 were waited for; matrix products, arithmetic and copies ran while one was open for 19% of the time, Pallas kernels for 15%

profile of v6, /device:TPU:0, one launch (start us, length us, event | category | flops | bytes accessed | tf_op | source)
XLA Modules:
  0.0 589.6 jit_solution(17179299444074534208)
XLA Ops:
  23.1 13.2 %collective-permute-done.1 = bf16[2,56,768]{2,1,0:T(8,128)(2,1)S(1)} collective-permute-done((bf16[2,56,768]{2,1,0:T(8,128)(2,1)}, bf16[2,56,768]{2,1,0:T(8,128)(2,1)S(1)}, u32[]{:S(2)}, u32[]{:S(2)}) %collective-permute-start.1) | collective-permute-done | bytes 172064 | tf_op jit(solution)/shard_map/ppermute | solution.py:28
  40.1 22.6 %all-gather.5.cloned.1.call-done = bf16[1024,1600]{1,0:T(8,128)(2,1)} async-done(((bf16[128,1600]{1,0:T(8,128)(2,1)}), bf16[1024,1600]{1,0:T(8,128)(2,1)}) %all-gather.5.cloned.1.call-update) | async-done | bytes 3276816 | tf_op jit(solution)/shard_map/all_gather | solution.py:704
  74.8 31.2 %all-gather.7.cloned.1.call-done = bf16[4,448,768]{2,1,0:T(8,128)(2,1)} async-done(((bf16[1,448,768]{2,1,0:T(8,128)(2,1)}), bf16[4,448,768]{2,1,0:T(8,128)(2,1)}) %all-gather.7.cloned.1.call-update) | async-done | bytes 2752528 | tf_op jit(solution)/shard_map/all_gather | solution.py:752
  133.4 8.2 %attend_forward.1 = (bf16[1024,256]{1,0:T(8,128)(2,1)S(1)}, f32[1,4,1024]{2,1,0:T(4,128)S(1)}) custom-call(s32[3,8]{1,0:T(4,128)S(1)} %pad_add_fusion.order_ref, bf16[1024,256]{1,0:T(8,128)(2,1)S(1)} %get-tuple-element.236.q_ref, bf16[1024,256]{1,0:T(8,128)(2,1)S(1)} %slice.248.k_ref, bf16[1024,256]{1,0:T(8,128)(2,1)S(1)} %get-tuple-element.235.v_ref), custom_call_target="tpu_custom_call" | custom-call | flops 4294967296 | bytes 2097152 | tf_op jit(solution)/shard_map/attend_forward/pallas_call | solution.py:180
  141.6 7.5 %collective-permute-done.10.refs_4_ = bf16[4,56,1600]{2,1,0:T(8,128)(2,1)} collective-permute-done((bf16[4,56,1600]{2,1,0:T(8,128)(2,1)}, bf16[4,56,1600]{2,1,0:T(8,128)(2,1)}, u32[]{:S(2)}, u32[]{:S(2)}) %collective-permute-start.10) | collective-permute-done | bytes 716832 | tf_op jit(solution)/shard_map/ppermute | solution.py:28
  154.1 8.5 %collective-permute-done.13.refs_2_ = bf16[2,128,256]{2,1,0:T(8,128)(2,1)S(1)} collective-permute-done((bf16[2,128,256]{2,1,0:T(8,128)(2,1)S(1)}, bf16[2,128,256]{2,1,0:T(8,128)(2,1)S(1)}, u32[]{:S(2)}, u32[]{:S(2)}) %collective-permute-start.13) | collective-permute-done | bytes 131104 | tf_op jit(solution)/shard_map/ppermute | solution.py:28
  196.5 16.1 %collective-permute-done.22.refs_3_ = bf16[8,56,800]{2,1,0:T(8,128)(2,1)S(1)} collective-permute-done((bf16[8,56,800]{2,1,0:T(8,128)(2,1)}, bf16[8,56,800]{2,1,0:T(8,128)(2,1)S(1)}, u32[]{:S(2)}, u32[]{:S(2)}) %collective-permute-start.22) | collective-permute-done | bytes 716832 | tf_op jit(solution)/shard_map/ppermute | solution.py:28
  212.6 17.1 %collective-permute-done.21.refs_2_ = bf16[8,56,800]{2,1,0:T(8,128)(2,1)S(1)} collective-permute-done((bf16[8,56,800]{2,1,0:T(8,128)(2,1)}, bf16[8,56,800]{2,1,0:T(8,128)(2,1)S(1)}, u32[]{:S(2)}, u32[]{:S(2)}) %collective-permute-start.21) | collective-permute-done | bytes 716832 | tf_op jit(solution)/shard_map/ppermute | solution.py:28
  241.1 11.8 %convert_reduce_fusion.1 = (f32[800]{0:T(1024)}, bf16[1024,800]{0,1:T(8,128)(2,1)S(1)}, bf16[1024,800]{0,1:T(8,128)(2,1)}) fusion(f32[1024,800]{0,1:T(8,128)} %fusion.61, f32[800]{0:T(1024)} %convert_element_type.92, bf16[1024,1600]{1,0:T(8,128)(2,1)} %all-gather.11.cloned.1.call-done, bf16[1600,800]{1,0:T(8,128)(2,1)} %bitcast.92), kind=kOutput, calls=%fused_computation.22 | convolution fusion | flops 2645196032 | bytes 12396800 | tf_op jit(solution)/shard_map/dot_general | solution.py:49
  262.4 8.0 %fusion.60.proj_ref = f32[800,1600]{1,0:T(8,128)} fusion(bf16[1024,800]{0,1:T(8,128)(2,1)} %get-tuple-element.121, bf16[1024,1600]{0,1:T(8,128)(2,1)} %all-gather.9.cloned.1.call-done), kind=kOutput, calls=%fused_computation.144 | convolution fusion | flops 2621440000 | bytes 10035200 | tf_op jit(solution)/shard_map/dot_general | solution.py:49
  276.0 7.7 %pack_hidden.1 = bf16[4,8,56,1600]{3,2,1,0:T(8,128)(2,1)} custom-call(s32[2]{0:T(128)} %pad_add_fusion.1.where_ref, f32[8,200,800]{2,1,0:T(8,128)} %bitcast.90, f32[800,1600]{1,0:T(8,128)} %fusion.60.proj_ref, f32[4,16,256]{2,1,0:T(8,128)} %pad.22.sums_ref), custom_call_target="tpu_custom_call" | custom-call | bytes 30916608 | tf_op jit(solution)/shard_map/pack_hidden/pallas_call | solution.py:240
  285.9 16.8 %reduce-scatter.5.cloned.1.call-done = bf16[128,1600]{1,0:T(8,128)(2,1)} async-done(((bf16[1024,1600]{1,0:T(8,128)(2,1)}), bf16[128,1600]{1,0:T(8,128)(2,1)}) %reduce-scatter.5.cloned.1.call-update) | async-done | bytes 409616 | tf_op jit(solution)/shard_map/reduce_scatter | solution.py:708
  334.0 11.1 %attend_backward.1 = (bf16[1024,256]{1,0:T(8,128)(2,1)S(1)}, bf16[1024,256]{1,0:T(8,128)(2,1)S(1)}, bf16[1024,256]{1,0:T(8,128)(2,1)S(1)}) custom-call(s32[3,8]{1,0:T(4,128)S(1)} %pad_add_fusion.order_ref, bf16[1024,256]{1,0:T(8,128)(2,1)S(1)} %copy-done.7, bf16[1024,256]{1,0:T(8,128)(2,1)S(1)} %copy-done.3, bf16[1024,256]{1,0:T(8,128)(2,1)S(1)} %copy-done.5, ...), custom_call_target="tpu_custom_call" | custom-call | flops 10737418240 | bytes 3670016 | tf_op jit(solution)/shard_map/attend_backward/pallas_call | solution.py:203
  356.7 7.4 %split_outw.1 = (bf16[4,56,1600]{2,1,0:T(8,128)(2,1)}, bf16[4,56,1600]{2,1,0:T(8,128)(2,1)}, bf16[4,56,1600]{2,1,0:T(8,128)(2,1)}, bf16[4,56,1600]{2,1,0:T(8,128)(2,1)}, bf16[4,4,56,1600]{3,2,1,0:T(8,128)(2,1)}) custom-call(s32[2]{0:T(128)} %pad_add_fusion.1.where_ref, f32[8,200,1600]{2,1,0:T(8,128)} %bitcast.86), custom_call_target="tpu_custom_call" | custom-call | bytes 30720000 | tf_op jit(solution)/shard_map/split_outw/pallas_call | solution.py:240
  368.3 7.9 %fusion.40 = f32[1600,768]{1,0:T(8,128)} fusion(bf16[1024,768]{1,0:T(8,128)(2,1)} %copy-done.37, bf16[1024,1600]{1,0:T(8,128)(2,1)} %all-gather.5.cloned.1.call-done, f32[1600]{0:T(1024)S(1)} %copy-done.44, f32[1600]{0:T(1024)S(1)} %mul.199, f32[1024]{0:T(1024)S(1)} %copy-done.48, f32[1024]{0:T(1024)S(1)} %broadcast_multiply_fusion), kind=kOutput, calls=%fused_computation.128 | convolution fusion | flops 2526412800 | bytes 9785856 | tf_op jit(solution)/shard_map/dot_general | solution.py:49
  376.2 7.3 %pack_last.1 = (bf16[8,56,1600]{2,1,0:T(8,128)(2,1)}, bf16[8,56,1600]{2,1,0:T(8,128)(2,1)}, bf16[8,56,1600]{2,1,0:T(8,128)(2,1)}, bf16[8,56,1600]{2,1,0:T(8,128)(2,1)}) custom-call(s32[2]{0:T(128)} %pad_add_fusion.1.where_ref, f32[8,200,768]{2,1,0:T(8,128)} %bitcast.91, bf16[4,56,1600]{2,1,0:T(8,128)(2,1)} %get-tuple-element.104.refs_0_, ...), custom_call_target="tpu_custom_call" | custom-call | bytes 32342016 | tf_op jit(solution)/shard_map/pack_last/pallas_call | solution.py:240
  392.7 15.1 %collective-permute-done.28.refs_1_ = bf16[2,56,800]{2,1,0:T(8,128)(2,1)S(1)} collective-permute-done((bf16[2,56,800]{2,1,0:T(8,128)(2,1)}, bf16[2,56,800]{2,1,0:T(8,128)(2,1)S(1)}, u32[]{:S(2)}, u32[]{:S(2)}) %collective-permute-start.28) | collective-permute-done | bytes 179232 | tf_op jit(solution)/shard_map/ppermute | solution.py:28
  410.7 11.1 %collective-permute-done.30.refs_3_ = bf16[2,56,800]{2,1,0:T(8,128)(2,1)S(1)} collective-permute-done((bf16[2,56,800]{2,1,0:T(8,128)(2,1)}, bf16[2,56,800]{2,1,0:T(8,128)(2,1)S(1)}, u32[]{:S(2)}, u32[]{:S(2)}) %collective-permute-start.30) | collective-permute-done | bytes 179232 | tf_op jit(solution)/shard_map/ppermute | solution.py:28
  427.4 24.5 %collective-permute-done.33.refs_2_ = bf16[8,56,1600]{2,1,0:T(8,128)(2,1)} collective-permute-done((bf16[8,56,1600]{2,1,0:T(8,128)(2,1)}, bf16[8,56,1600]{2,1,0:T(8,128)(2,1)}, u32[]{:S(2)}, u32[]{:S(2)}) %collective-permute-start.33) | collective-permute-done | bytes 1433632 | tf_op jit(solution)/shard_map/ppermute | solution.py:28
  471.2 22.2 %collective-permute-done.35.refs_1_ = bf16[2,56,1600]{2,1,0:T(8,128)(2,1)} collective-permute-done((bf16[2,56,1600]{2,1,0:T(8,128)(2,1)}, bf16[2,56,1600]{2,1,0:T(8,128)(2,1)}, u32[]{:S(2)}, u32[]{:S(2)}) %collective-permute-start.35) | collective-permute-done | bytes 358432 | tf_op jit(solution)/shard_map/ppermute | solution.py:28
  503.6 12.5 %collective-permute-done.37.refs_3_ = bf16[2,56,1600]{2,1,0:T(8,128)(2,1)S(1)} collective-permute-done((bf16[2,56,1600]{2,1,0:T(8,128)(2,1)S(1)}, bf16[2,56,1600]{2,1,0:T(8,128)(2,1)S(1)}, u32[]{:S(2)}, u32[]{:S(2)}) %collective-permute-start.37) | collective-permute-done | bytes 358432 | tf_op jit(solution)/shard_map/ppermute | solution.py:28
  519.0 11.2 %collective-permute-done.39.refs_1_ = bf16[8,56,1600]{2,1,0:T(8,128)(2,1)} collective-permute-done((bf16[8,56,1600]{2,1,0:T(8,128)(2,1)}, bf16[8,56,1600]{2,1,0:T(8,128)(2,1)}, u32[]{:S(2)}, u32[]{:S(2)}) %collective-permute-start.39) | collective-permute-done | bytes 1433632 | tf_op jit(solution)/shard_map/ppermute | solution.py:28
  537.2 9.8 %finish_hidden.1 = (f32[200,6400]{1,0:T(8,128)}, f32[800,1600]{1,0:T(8,128)}, f32[4,16,256]{2,1,0:T(8,128)}) custom-call(s32[2]{0:T(128)} %pad_add_fusion.1.where_ref, bf16[8,56,1600]{2,1,0:T(8,128)(2,1)} %join_hidden.1.refs_0_, bf16[8,56,1600]{2,1,0:T(8,128)(2,1)} %collective-permute-done.39.refs_1_, bf16[8,56,1600]{2,1,0:T(8,128)(2,1)} %collective-permute-done.43.refs_2_, ...), custom_call_target="tpu_custom_call" | custom-call | bytes 17203200 | tf_op jit(solution)/shard_map/finish_hidden/pallas_call | solution.py:240
  558.4 17.4 %collective-permute-done.41.refs_2_ = bf16[5,56,1600]{2,1,0:T(8,128)(2,1)} collective-permute-done((bf16[5,56,1600]{2,1,0:T(8,128)(2,1)}, bf16[5,56,1600]{2,1,0:T(8,128)(2,1)}, u32[]{:S(2)}, u32[]{:S(2)}) %collective-permute-start.41) | collective-permute-done | bytes 896032 | tf_op jit(solution)/shard_map/ppermute | solution.py:28
  (375 shorter events, 247.6 us)
Async XLA Ops:
  7.3 55.5 %all-gather.5.cloned.1.call-start = ((), (), s32[]{:S(2)}) async-start(), calls=%async_computation.4 | async-start | bytes 3833856 | tf_op jit(solution)/shard_map/all_gather | solution.py:704
  9.5 96.5 %all-gather.7.cloned.1.call-start = ((), (), s32[]{:S(2)}) async-start(), calls=%async_computation.5 | async-start | bytes 3440640 | tf_op jit(solution)/shard_map/all_gather | solution.py:752
  39.1 153.1 %all-gather.9.cloned.1.call-start = ((), (), s32[]{:S(2)}) async-start(), calls=%async_computation.6 | async-start | bytes 3686400 | tf_op jit(solution)/shard_map/all_gather | solution.py:704
  67.2 38.8 %collective-permute-start.4 = (bf16[120,1600]{1,0:T(8,128)(2,1)}, bf16[120,1600]{1,0:T(8,128)(2,1)S(1)}, u32[]{:S(2)}, u32[]{:S(2)}) collective-permute-start(bf16[120,1600]{1,0:T(8,128)(2,1)} %get-tuple-element.81), channel_id=1, source_target_pairs={{0,2},{1,3},{2,0},{3,1},{4,6},{5,7},{6,4},{7,5},{8,10},{9,11},{10,... | collective-permute-start | bytes 1152008 | tf_op jit(solution)/shard_map/ppermute | solution.py:28
  67.2 38.8 %collective-permute-start.5 = (bf16[120,1600]{1,0:T(8,128)(2,1)}, bf16[120,1600]{1,0:T(8,128)(2,1)S(1)}, u32[]{:S(2)}, u32[]{:S(2)}) collective-permute-start(bf16[120,1600]{1,0:T(8,128)(2,1)} %get-tuple-element.82), channel_id=1, source_target_pairs={{0,4},{1,5},{2,6},{3,7},{4,0},{5,1},{6,2},{7,3},{8,12},{9,13},{10,... | collective-permute-start | bytes 1152008 | tf_op jit(solution)/shard_map/ppermute | solution.py:28
  70.2 35.8 %collective-permute-start.6 = (bf16[120,1600]{1,0:T(8,128)(2,1)}, bf16[120,1600]{1,0:T(8,128)(2,1)}, u32[]{:S(2)}, u32[]{:S(2)}) collective-permute-start(bf16[120,1600]{1,0:T(8,128)(2,1)} %get-tuple-element.83), channel_id=1, source_target_pairs={{0,6},{1,7},{2,4},{3,5},{4,2},{5,3},{6,0},{7,1},{8,14},{9,15},{10,... | collective-permute-start | bytes 1152008 | tf_op jit(solution)/shard_map/ppermute | solution.py:28
  109.9 131.2 %all-gather.11.cloned.1.call-start = ((), (), s32[]{:S(2)}) async-start(), calls=%async_computation.7 | async-start | bytes 3833856 | tf_op jit(solution)/shard_map/all_gather | solution.py:704
  113.4 28.1 %collective-permute-start.11 = (bf16[4,56,1600]{2,1,0:T(8,128)(2,1)}, bf16[4,56,1600]{2,1,0:T(8,128)(2,1)}, u32[]{:S(2)}, u32[]{:S(2)}) collective-permute-start(bf16[4,56,1600]{2,1,0:T(8,128)(2,1)} %get-tuple-element.88.refs_0_), channel_id=1, source_target_pairs={{0,24},{8,16},{16,8},{24,0},{1,25},{9,17},{17,9},{25,1},{2,26},{10... | collective-permute-start | bytes 2150408 | tf_op jit(solution)/shard_map/ppermute | solution.py:28
  114.9 34.1 %collective-permute-start.10 = (bf16[4,56,1600]{2,1,0:T(8,128)(2,1)}, bf16[4,56,1600]{2,1,0:T(8,128)(2,1)}, u32[]{:S(2)}, u32[]{:S(2)}) collective-permute-start(bf16[4,56,1600]{2,1,0:T(8,128)(2,1)} %get-tuple-element.88.refs_0_), channel_id=1, source_target_pairs={{0,16},{8,24},{16,0},{24,8},{1,17},{9,25},{17,1},{25,9},{2,18},{10... | collective-permute-start | bytes 2150408 | tf_op jit(solution)/shard_map/ppermute | solution.py:28
  116.4 32.7 %collective-permute-start.9 = (bf16[4,56,1600]{2,1,0:T(8,128)(2,1)}, bf16[4,56,1600]{2,1,0:T(8,128)(2,1)}, u32[]{:S(2)}, u32[]{:S(2)}) collective-permute-start(bf16[4,56,1600]{2,1,0:T(8,128)(2,1)} %get-tuple-element.88.refs_0_), channel_id=1, source_target_pairs={{0,8},{8,0},{16,24},{24,16},{1,9},{9,1},{17,25},{25,17},{2,10},{10... | collective-permute-start | bytes 2150408 | tf_op jit(solution)/shard_map/ppermute | solution.py:28
  192.2 110.5 %reduce-scatter.5.cloned.1.call-start = ((), (), s32[]{:S(2)}) async-start(), calls=%async_computation.8 | async-start | bytes 3833856 | tf_op jit(solution)/shard_map/reduce_scatter | solution.py:708
  193.8 36.0 %collective-permute-start.21 = (bf16[8,56,800]{2,1,0:T(8,128)(2,1)}, bf16[8,56,800]{2,1,0:T(8,128)(2,1)S(1)}, u32[]{:S(2)}, u32[]{:S(2)}) collective-permute-start(bf16[8,56,800]{2,1,0:T(8,128)(2,1)} %constant_dynamic-update-slice_fusion.1.refs_0_), channel_id=1, source_target_pairs={{0,16},{8,24},{16,0},{24,8},{1,17},{9,25},{17,1},{25,9},{2,18},{10... | collective-permute-start | bytes 2150408 | tf_op jit(solution)/shard_map/ppermute | solution.py:28
  259.6 127.3 %reduce-scatter.7.cloned.1.call-start = ((), (), s32[]{:S(2)}) async-start(), calls=%async_computation.9 | async-start | bytes 7454720 | tf_op jit(solution)/shard_map/reduce_scatter | solution.py:811
  283.7 185.6 %reduce-scatter.11.cloned.1.call-start = ((), (), s32[]{:S(2)}) async-start(), calls=%async_computation.11 | async-start | bytes 3833856 | tf_op jit(solution)/shard_map/reduce_scatter | solution.py:708
  350.0 200.4 %reduce-scatter.9.cloned.1.call-start = ((), (), s32[]{:S(2)}) async-start(), calls=%async_computation.10 | async-start | bytes 3833856 | tf_op jit(solution)/shard_map/reduce_scatter | solution.py:708
  383.5 43.9 %collective-permute-start.32 = (bf16[8,56,1600]{2,1,0:T(8,128)(2,1)}, bf16[8,56,1600]{2,1,0:T(8,128)(2,1)}, u32[]{:S(2)}, u32[]{:S(2)}) collective-permute-start(bf16[8,56,1600]{2,1,0:T(8,128)(2,1)} %get-tuple-element.117), channel_id=1, source_target_pairs={{0,8},{8,0},{16,24},{24,16},{1,9},{9,1},{17,25},{25,17},{2,10},{10... | collective-permute-start | bytes 4300808 | tf_op jit(solution)/shard_map/ppermute | solution.py:28
  384.9 67.0 %collective-permute-start.33 = (bf16[8,56,1600]{2,1,0:T(8,128)(2,1)}, bf16[8,56,1600]{2,1,0:T(8,128)(2,1)}, u32[]{:S(2)}, u32[]{:S(2)}) collective-permute-start(bf16[8,56,1600]{2,1,0:T(8,128)(2,1)} %get-tuple-element.118), channel_id=1, source_target_pairs={{0,16},{8,24},{16,0},{24,8},{1,17},{9,25},{17,1},{25,9},{2,18},{10... | collective-permute-start | bytes 4300808 | tf_op jit(solution)/shard_map/ppermute | solution.py:28
  386.4 65.5 %collective-permute-start.34 = (bf16[8,56,1600]{2,1,0:T(8,128)(2,1)}, bf16[8,56,1600]{2,1,0:T(8,128)(2,1)}, u32[]{:S(2)}, u32[]{:S(2)}) collective-permute-start(bf16[8,56,1600]{2,1,0:T(8,128)(2,1)} %get-tuple-element.119), channel_id=1, source_target_pairs={{0,24},{8,16},{16,8},{24,0},{1,25},{9,17},{17,9},{25,1},{2,26},{10... | collective-permute-start | bytes 4300808 | tf_op jit(solution)/shard_map/ppermute | solution.py:28
  462.9 74.2 %collective-permute-start.44 = (bf16[8,56,1600]{2,1,0:T(8,128)(2,1)}, bf16[8,56,1600]{2,1,0:T(8,128)(2,1)}, u32[]{:S(2)}, u32[]{:S(2)}) collective-permute-start(bf16[8,56,1600]{2,1,0:T(8,128)(2,1)} %join_hidden.1.refs_0_), channel_id=1, source_target_pairs={{0,24},{8,16},{16,8},{24,0},{1,25},{9,17},{17,9},{25,1},{2,26},{10... | collective-permute-start | bytes 4300808 | tf_op jit(solution)/shard_map/ppermute | solution.py:28
  464.4 72.7 %collective-permute-start.43 = (bf16[8,56,1600]{2,1,0:T(8,128)(2,1)}, bf16[8,56,1600]{2,1,0:T(8,128)(2,1)}, u32[]{:S(2)}, u32[]{:S(2)}) collective-permute-start(bf16[8,56,1600]{2,1,0:T(8,128)(2,1)} %join_hidden.1.refs_0_), channel_id=1, source_target_pairs={{0,16},{8,24},{16,0},{24,8},{1,17},{9,25},{17,1},{25,9},{2,18},{10... | collective-permute-start | bytes 4300808 | tf_op jit(solution)/shard_map/ppermute | solution.py:28
  465.7 64.5 %collective-permute-start.39 = (bf16[8,56,1600]{2,1,0:T(8,128)(2,1)}, bf16[8,56,1600]{2,1,0:T(8,128)(2,1)}, u32[]{:S(2)}, u32[]{:S(2)}) collective-permute-start(bf16[8,56,1600]{2,1,0:T(8,128)(2,1)} %join_hidden.1.refs_0_), channel_id=1, source_target_pairs={{0,8},{8,0},{16,24},{24,16},{1,9},{9,1},{17,25},{25,17},{2,10},{10... | collective-permute-start | bytes 4300808 | tf_op jit(solution)/shard_map/ppermute | solution.py:28
  468.5 35.1 %collective-permute-start.36 = (bf16[2,56,1600]{2,1,0:T(8,128)(2,1)}, bf16[2,56,1600]{2,1,0:T(8,128)(2,1)}, u32[]{:S(2)}, u32[]{:S(2)}) collective-permute-start(bf16[2,56,1600]{2,1,0:T(8,128)(2,1)} %get-tuple-element.125), channel_id=1, source_target_pairs={{0,4},{1,5},{2,6},{3,7},{4,0},{5,1},{6,2},{7,3},{8,12},{9,13},{10,... | collective-permute-start | bytes 1075208 | tf_op jit(solution)/shard_map/ppermute | solution.py:28
  535.0 40.7 %collective-permute-start.41 = (bf16[5,56,1600]{2,1,0:T(8,128)(2,1)}, bf16[5,56,1600]{2,1,0:T(8,128)(2,1)}, u32[]{:S(2)}, u32[]{:S(2)}) collective-permute-start(bf16[5,56,1600]{2,1,0:T(8,128)(2,1)} %join_last.1.refs_0_), channel_id=1, source_target_pairs={{0,16},{8,24},{16,0},{24,8},{1,17},{9,25},{17,1},{25,9},{2,18},{10... | collective-permute-start | bytes 2688008 | tf_op jit(solution)/shard_map/ppermute | solution.py:28
  535.5 40.3 %collective-permute-start.40 = (bf16[5,56,1600]{2,1,0:T(8,128)(2,1)}, bf16[5,56,1600]{2,1,0:T(8,128)(2,1)}, u32[]{:S(2)}, u32[]{:S(2)}) collective-permute-start(bf16[5,56,1600]{2,1,0:T(8,128)(2,1)} %join_last.1.refs_0_), channel_id=1, source_target_pairs={{0,8},{8,0},{16,24},{24,16},{1,9},{9,1},{17,25},{25,17},{2,10},{10... | collective-permute-start | bytes 2688008 | tf_op jit(solution)/shard_map/ppermute | solution.py:28
  (97 other events, 1620.0 us)
Sparse Core Ops, SparseCore 0:
  9.8 52.9 all-gather.4
  65.2 40.7 all-gather.6
  110.0 40.2 all-gather.8
  192.3 40.7 all-gather.10
  259.8 42.8 reduce-scatter.4
  305.6 66.0 reduce-scatter.6
  374.6 55.4 reduce-scatter.10
  461.9 71.2 reduce-scatter.8

commit v7 on v6

--- a/solution.py
+++ b/solution.py
@@ -876,8 +876,8 @@
 
     last[0] = tie(last[0], hidden_joined)
     last = sum_last(where, last, count, 3 * width)
-    output_low = tie(active_low, last[0])
     last = [last[0]] + [xor_send(last[j], "shard", evens[j]) for j in range(1, half)]
+    output_low = tie(active_low, last[1])
     _, pull_first = jax.vjp(lambda rows: layer_norm(rows, g_first, s_first), in_rows)
     (input_part,) = pull_first(first_grad)
     tokens_grad = (middle_grad + input_part).astype(low)

time: 596 us -> 604 us (1.013)
  waiting for transfers between devices: 282 us -> 292 us
    ppermute x45, waiting for transfers between devices: 211 us -> 221 us  [xor_send(): return lax.ppermute(block, axis, [(i, i ^ bits) for i in range(count)])]
    unnamed x146 -> x142, local copies, waits for them, and re-layouts: 27.1 us -> 26.3 us
  transfers between devices with their start and end apart: 53 -> 53, of which waited for: 25 -> 24; matrix products, arithmetic and copies ran while one was open for 19% -> 18% of each run, Pallas kernels for 15% -> 15%
where the time goes in v7:
time: 604 us; the launch traced here: 599 us
  waiting for transfers between devices  292 us (48%)
  Pallas kernels  96.9 us (16%)
  matrix products  78 us (13%)
  starting transfers between devices  52.3 us (9%)
  local copies, waits for them, and re-layouts  46.4 us (8%)
  other arithmetic  17.9 us (3%)
  between operations  15.7 us (3%)
    ppermute x45, waiting for transfers between devices, xor_send(): return lax.ppermute(block, axis, [(i, i ^ bits) for i in range(count)])  221 us
    dot_general x12, matrix products, mm(): lax.dot_general(left_side, right_side, (((left_dim,), (right_dim,)), ((),...  77.6 us
    pallas_call x18, Pallas kernels, local_call(): pl.pallas_call(kernel, out_shape=tuple(shapes) if many else shapes, in_sp...  77.6 us
    ppermute x45, starting transfers between devices, xor_send(): return lax.ppermute(block, axis, [(i, i ^ bits) for i in range(count)])  51.6 us
    all_gather x1, waiting for transfers between devices, on_device(): lax.all_gather(qkv_stack.reshape(count * span, 3 * width), 'replica')  31.2 us
    unnamed x142, local copies, waits for them, and re-layouts  26.3 us
    all_gather x3, waiting for transfers between devices, gather_rows(): return lax.all_gather(block, 'shard', axis=0, tiled=True)  22.6 us
    reduce_scatter x3, waiting for transfers between devices, scatter_rows(): return lax.psum_scatter(blocks, 'shard', scatter_dimension=0, tiled=True)  16.9 us
  transfers between devices with their start and end apart: 53, of which 24 were waited for; matrix products, arithmetic and copies ran while one was open for 18% of the time, Pallas kernels for 15%

profile of v7, /device:TPU:0, one launch (start us, length us, event | category | flops | bytes accessed | tf_op | source)
XLA Modules:
  0.0 599.2 jit_solution(883602524341993986)
XLA Ops:
  23.1 13.2 %collective-permute-done.1 = bf16[2,56,768]{2,1,0:T(8,128)(2,1)S(1)} collective-permute-done((bf16[2,56,768]{2,1,0:T(8,128)(2,1)}, bf16[2,56,768]{2,1,0:T(8,128)(2,1)S(1)}, u32[]{:S(2)}, u32[]{:S(2)}) %collective-permute-start.1) | collective-permute-done | bytes 172064 | tf_op jit(solution)/shard_map/ppermute | solution.py:28
  40.1 22.6 %all-gather.5.cloned.1.call-done = bf16[1024,1600]{1,0:T(8,128)(2,1)} async-done(((bf16[128,1600]{1,0:T(8,128)(2,1)}), bf16[1024,1600]{1,0:T(8,128)(2,1)}) %all-gather.5.cloned.1.call-update) | async-done | bytes 3276816 | tf_op jit(solution)/shard_map/all_gather | solution.py:704
  74.8 31.2 %all-gather.7.cloned.1.call-done = bf16[4,448,768]{2,1,0:T(8,128)(2,1)} async-done(((bf16[1,448,768]{2,1,0:T(8,128)(2,1)}), bf16[4,448,768]{2,1,0:T(8,128)(2,1)}) %all-gather.7.cloned.1.call-update) | async-done | bytes 2752528 | tf_op jit(solution)/shard_map/all_gather | solution.py:752
  133.3 8.2 %attend_forward.1 = (bf16[1024,256]{1,0:T(8,128)(2,1)S(1)}, f32[1,4,1024]{2,1,0:T(4,128)S(1)}) custom-call(s32[3,8]{1,0:T(4,128)S(1)} %pad_add_fusion.order_ref, bf16[1024,256]{1,0:T(8,128)(2,1)S(1)} %get-tuple-element.236.q_ref, bf16[1024,256]{1,0:T(8,128)(2,1)S(1)} %slice.248.k_ref, bf16[1024,256]{1,0:T(8,128)(2,1)S(1)} %get-tuple-element.235.v_ref), custom_call_target="tpu_custom_call" | custom-call | flops 4294967296 | bytes 2097152 | tf_op jit(solution)/shard_map/attend_forward/pallas_call | solution.py:180
  141.6 7.5 %collective-permute-done.10.refs_4_ = bf16[4,56,1600]{2,1,0:T(8,128)(2,1)} collective-permute-done((bf16[4,56,1600]{2,1,0:T(8,128)(2,1)}, bf16[4,56,1600]{2,1,0:T(8,128)(2,1)}, u32[]{:S(2)}, u32[]{:S(2)}) %collective-permute-start.10) | collective-permute-done | bytes 716832 | tf_op jit(solution)/shard_map/ppermute | solution.py:28
  154.1 8.5 %collective-permute-done.13.refs_2_ = bf16[2,128,256]{2,1,0:T(8,128)(2,1)S(1)} collective-permute-done((bf16[2,128,256]{2,1,0:T(8,128)(2,1)S(1)}, bf16[2,128,256]{2,1,0:T(8,128)(2,1)S(1)}, u32[]{:S(2)}, u32[]{:S(2)}) %collective-permute-start.13) | collective-permute-done | bytes 131104 | tf_op jit(solution)/shard_map/ppermute | solution.py:28
  196.5 16.1 %collective-permute-done.22.refs_3_ = bf16[8,56,800]{2,1,0:T(8,128)(2,1)S(1)} collective-permute-done((bf16[8,56,800]{2,1,0:T(8,128)(2,1)}, bf16[8,56,800]{2,1,0:T(8,128)(2,1)S(1)}, u32[]{:S(2)}, u32[]{:S(2)}) %collective-permute-start.22) | collective-permute-done | bytes 716832 | tf_op jit(solution)/shard_map/ppermute | solution.py:28
  212.6 17.1 %collective-permute-done.21.refs_2_ = bf16[8,56,800]{2,1,0:T(8,128)(2,1)S(1)} collective-permute-done((bf16[8,56,800]{2,1,0:T(8,128)(2,1)}, bf16[8,56,800]{2,1,0:T(8,128)(2,1)S(1)}, u32[]{:S(2)}, u32[]{:S(2)}) %collective-permute-start.21) | collective-permute-done | bytes 716832 | tf_op jit(solution)/shard_map/ppermute | solution.py:28
  241.1 11.8 %convert_reduce_fusion.1 = (f32[800]{0:T(1024)}, bf16[1024,800]{0,1:T(8,128)(2,1)S(1)}, bf16[1024,800]{0,1:T(8,128)(2,1)}) fusion(f32[1024,800]{0,1:T(8,128)} %fusion.61, f32[800]{0:T(1024)} %convert_element_type.92, bf16[1024,1600]{1,0:T(8,128)(2,1)} %all-gather.11.cloned.1.call-done, bf16[1600,800]{1,0:T(8,128)(2,1)} %bitcast.92), kind=kOutput, calls=%fused_computation.22 | convolution fusion | flops 2645196032 | bytes 12396800 | tf_op jit(solution)/shard_map/dot_general | solution.py:49
  262.3 8.0 %fusion.60.proj_ref = f32[800,1600]{1,0:T(8,128)} fusion(bf16[1024,800]{0,1:T(8,128)(2,1)} %get-tuple-element.121, bf16[1024,1600]{0,1:T(8,128)(2,1)} %all-gather.9.cloned.1.call-done), kind=kOutput, calls=%fused_computation.144 | convolution fusion | flops 2621440000 | bytes 10035200 | tf_op jit(solution)/shard_map/dot_general | solution.py:49
  275.8 7.7 %pack_hidden.1 = bf16[4,8,56,1600]{3,2,1,0:T(8,128)(2,1)} custom-call(s32[2]{0:T(128)} %pad_add_fusion.1.where_ref, f32[8,200,800]{2,1,0:T(8,128)} %bitcast.90, f32[800,1600]{1,0:T(8,128)} %fusion.60.proj_ref, f32[4,16,256]{2,1,0:T(8,128)} %pad.22.sums_ref), custom_call_target="tpu_custom_call" | custom-call | bytes 30916608 | tf_op jit(solution)/shard_map/pack_hidden/pallas_call | solution.py:240
  285.8 16.9 %reduce-scatter.5.cloned.1.call-done = bf16[128,1600]{1,0:T(8,128)(2,1)} async-done(((bf16[1024,1600]{1,0:T(8,128)(2,1)}), bf16[128,1600]{1,0:T(8,128)(2,1)}) %reduce-scatter.5.cloned.1.call-update) | async-done | bytes 409616 | tf_op jit(solution)/shard_map/reduce_scatter | solution.py:708
  333.9 11.1 %attend_backward.1 = (bf16[1024,256]{1,0:T(8,128)(2,1)S(1)}, bf16[1024,256]{1,0:T(8,128)(2,1)S(1)}, bf16[1024,256]{1,0:T(8,128)(2,1)S(1)}) custom-call(s32[3,8]{1,0:T(4,128)S(1)} %pad_add_fusion.order_ref, bf16[1024,256]{1,0:T(8,128)(2,1)S(1)} %copy-done.7, bf16[1024,256]{1,0:T(8,128)(2,1)S(1)} %copy-done.3, bf16[1024,256]{1,0:T(8,128)(2,1)S(1)} %copy-done.5, ...), custom_call_target="tpu_custom_call" | custom-call | flops 10737418240 | bytes 3670016 | tf_op jit(solution)/shard_map/attend_backward/pallas_call | solution.py:203
  356.6 7.4 %split_outw.1 = (bf16[4,56,1600]{2,1,0:T(8,128)(2,1)}, bf16[4,56,1600]{2,1,0:T(8,128)(2,1)}, bf16[4,56,1600]{2,1,0:T(8,128)(2,1)}, bf16[4,56,1600]{2,1,0:T(8,128)(2,1)}, bf16[4,4,56,1600]{3,2,1,0:T(8,128)(2,1)}) custom-call(s32[2]{0:T(128)} %pad_add_fusion.1.where_ref, f32[8,200,1600]{2,1,0:T(8,128)} %bitcast.86), custom_call_target="tpu_custom_call" | custom-call | bytes 30720000 | tf_op jit(solution)/shard_map/split_outw/pallas_call | solution.py:240
  368.2 7.9 %fusion.40 = f32[1600,768]{1,0:T(8,128)} fusion(bf16[1024,768]{1,0:T(8,128)(2,1)} %copy-done.36, bf16[1024,1600]{1,0:T(8,128)(2,1)} %all-gather.5.cloned.1.call-done, f32[1600]{0:T(1024)S(1)} %copy-done.43, f32[1600]{0:T(1024)S(1)} %mul.199, f32[1024]{0:T(1024)S(1)} %copy-done.47, f32[1024]{0:T(1024)S(1)} %broadcast_multiply_fusion), kind=kOutput, calls=%fused_computation.128 | convolution fusion | flops 2526412800 | bytes 9785856 | tf_op jit(solution)/shard_map/dot_general | solution.py:49
  376.1 7.3 %pack_last.1 = (bf16[8,56,1600]{2,1,0:T(8,128)(2,1)}, bf16[8,56,1600]{2,1,0:T(8,128)(2,1)}, bf16[8,56,1600]{2,1,0:T(8,128)(2,1)}, bf16[8,56,1600]{2,1,0:T(8,128)(2,1)}) custom-call(s32[2]{0:T(128)} %pad_add_fusion.1.where_ref, f32[8,200,768]{2,1,0:T(8,128)} %bitcast.91, bf16[4,56,1600]{2,1,0:T(8,128)(2,1)} %get-tuple-element.104.refs_0_, ...), custom_call_target="tpu_custom_call" | custom-call | bytes 32342016 | tf_op jit(solution)/shard_map/pack_last/pallas_call | solution.py:240
  392.7 15.1 %collective-permute-done.28.refs_1_ = bf16[2,56,800]{2,1,0:T(8,128)(2,1)S(1)} collective-permute-done((bf16[2,56,800]{2,1,0:T(8,128)(2,1)}, bf16[2,56,800]{2,1,0:T(8,128)(2,1)S(1)}, u32[]{:S(2)}, u32[]{:S(2)}) %collective-permute-start.28) | collective-permute-done | bytes 179232 | tf_op jit(solution)/shard_map/ppermute | solution.py:28
  410.6 11.1 %collective-permute-done.30.refs_3_ = bf16[2,56,800]{2,1,0:T(8,128)(2,1)S(1)} collective-permute-done((bf16[2,56,800]{2,1,0:T(8,128)(2,1)}, bf16[2,56,800]{2,1,0:T(8,128)(2,1)S(1)}, u32[]{:S(2)}, u32[]{:S(2)}) %collective-permute-start.30) | collective-permute-done | bytes 179232 | tf_op jit(solution)/shard_map/ppermute | solution.py:28
  427.3 24.5 %collective-permute-done.33.refs_2_ = bf16[8,56,1600]{2,1,0:T(8,128)(2,1)} collective-permute-done((bf16[8,56,1600]{2,1,0:T(8,128)(2,1)}, bf16[8,56,1600]{2,1,0:T(8,128)(2,1)}, u32[]{:S(2)}, u32[]{:S(2)}) %collective-permute-start.33) | collective-permute-done | bytes 1433632 | tf_op jit(solution)/shard_map/ppermute | solution.py:28
  458.1 8.5 %collective-permute-done.35.refs_1_ = bf16[2,56,1600]{2,1,0:T(8,128)(2,1)} collective-permute-done((bf16[2,56,1600]{2,1,0:T(8,128)(2,1)}, bf16[2,56,1600]{2,1,0:T(8,128)(2,1)}, u32[]{:S(2)}, u32[]{:S(2)}) %collective-permute-start.35) | collective-permute-done | bytes 358432 | tf_op jit(solution)/shard_map/ppermute | solution.py:28
  484.2 35.4 %collective-permute-done.36.refs_2_ = bf16[2,56,1600]{2,1,0:T(8,128)(2,1)} collective-permute-done((bf16[2,56,1600]{2,1,0:T(8,128)(2,1)}, bf16[2,56,1600]{2,1,0:T(8,128)(2,1)}, u32[]{:S(2)}, u32[]{:S(2)}) %collective-permute-start.36) | collective-permute-done | bytes 358432 | tf_op jit(solution)/shard_map/ppermute | solution.py:28
  521.7 18.7 %collective-permute-done.39.refs_1_ = bf16[8,56,1600]{2,1,0:T(8,128)(2,1)} collective-permute-done((bf16[8,56,1600]{2,1,0:T(8,128)(2,1)}, bf16[8,56,1600]{2,1,0:T(8,128)(2,1)}, u32[]{:S(2)}, u32[]{:S(2)}) %collective-permute-start.39) | collective-permute-done | bytes 1433632 | tf_op jit(solution)/shard_map/ppermute | solution.py:28
  547.3 9.8 %finish_hidden.1 = (f32[200,6400]{1,0:T(8,128)}, f32[800,1600]{1,0:T(8,128)}, f32[4,16,256]{2,1,0:T(8,128)}) custom-call(s32[2]{0:T(128)} %pad_add_fusion.1.where_ref, bf16[8,56,1600]{2,1,0:T(8,128)(2,1)} %join_hidden.1.refs_0_, bf16[8,56,1600]{2,1,0:T(8,128)(2,1)} %collective-permute-done.39.refs_1_, bf16[8,56,1600]{2,1,0:T(8,128)(2,1)} %collective-permute-done.43.refs_2_, ...), custom_call_target="tpu_custom_call" | custom-call | bytes 17203200 | tf_op jit(solution)/shard_map/finish_hidden/pallas_call | solution.py:240
  568.5 16.9 %collective-permute-done.41.refs_2_ = bf16[5,56,1600]{2,1,0:T(8,128)(2,1)} collective-permute-done((bf16[5,56,1600]{2,1,0:T(8,128)(2,1)}, bf16[5,56,1600]{2,1,0:T(8,128)(2,1)}, u32[]{:S(2)}, u32[]{:S(2)}) %collective-permute-start.41) | collective-permute-done | bytes 896032 | tf_op jit(solution)/shard_map/ppermute | solution.py:28
  (371 shorter events, 241.0 us)
Async XLA Ops:
  7.3 55.5 %all-gather.5.cloned.1.call-start = ((), (), s32[]{:S(2)}) async-start(), calls=%async_computation.4 | async-start | bytes 3833856 | tf_op jit(solution)/shard_map/all_gather | solution.py:704
  9.5 96.5 %all-gather.7.cloned.1.call-start = ((), (), s32[]{:S(2)}) async-start(), calls=%async_computation.5 | async-start | bytes 3440640 | tf_op jit(solution)/shard_map/all_gather | solution.py:752
  39.1 153.1 %all-gather.9.cloned.1.call-start = ((), (), s32[]{:S(2)}) async-start(), calls=%async_computation.6 | async-start | bytes 3686400 | tf_op jit(solution)/shard_map/all_gather | solution.py:704
  67.2 38.8 %collective-permute-start.4 = (bf16[120,1600]{1,0:T(8,128)(2,1)}, bf16[120,1600]{1,0:T(8,128)(2,1)S(1)}, u32[]{:S(2)}, u32[]{:S(2)}) collective-permute-start(bf16[120,1600]{1,0:T(8,128)(2,1)} %get-tuple-element.81), channel_id=1, source_target_pairs={{0,2},{1,3},{2,0},{3,1},{4,6},{5,7},{6,4},{7,5},{8,10},{9,11},{10,... | collective-permute-start | bytes 1152008 | tf_op jit(solution)/shard_map/ppermute | solution.py:28
  67.2 38.8 %collective-permute-start.5 = (bf16[120,1600]{1,0:T(8,128)(2,1)}, bf16[120,1600]{1,0:T(8,128)(2,1)S(1)}, u32[]{:S(2)}, u32[]{:S(2)}) collective-permute-start(bf16[120,1600]{1,0:T(8,128)(2,1)} %get-tuple-element.82), channel_id=1, source_target_pairs={{0,4},{1,5},{2,6},{3,7},{4,0},{5,1},{6,2},{7,3},{8,12},{9,13},{10,... | collective-permute-start | bytes 1152008 | tf_op jit(solution)/shard_map/ppermute | solution.py:28
  70.2 35.8 %collective-permute-start.6 = (bf16[120,1600]{1,0:T(8,128)(2,1)}, bf16[120,1600]{1,0:T(8,128)(2,1)}, u32[]{:S(2)}, u32[]{:S(2)}) collective-permute-start(bf16[120,1600]{1,0:T(8,128)(2,1)} %get-tuple-element.83), channel_id=1, source_target_pairs={{0,6},{1,7},{2,4},{3,5},{4,2},{5,3},{6,0},{7,1},{8,14},{9,15},{10,... | collective-permute-start | bytes 1152008 | tf_op jit(solution)/shard_map/ppermute | solution.py:28
  109.8 131.2 %all-gather.11.cloned.1.call-start = ((), (), s32[]{:S(2)}) async-start(), calls=%async_computation.7 | async-start | bytes 3833856 | tf_op jit(solution)/shard_map/all_gather | solution.py:704
  114.9 34.1 %collective-permute-start.10 = (bf16[4,56,1600]{2,1,0:T(8,128)(2,1)}, bf16[4,56,1600]{2,1,0:T(8,128)(2,1)}, u32[]{:S(2)}, u32[]{:S(2)}) collective-permute-start(bf16[4,56,1600]{2,1,0:T(8,128)(2,1)} %get-tuple-element.88.refs_0_), channel_id=1, source_target_pairs={{0,16},{8,24},{16,0},{24,8},{1,17},{9,25},{17,1},{25,9},{2,18},{10... | collective-permute-start | bytes 2150408 | tf_op jit(solution)/shard_map/ppermute | solution.py:28
  116.4 32.7 %collective-permute-start.9 = (bf16[4,56,1600]{2,1,0:T(8,128)(2,1)}, bf16[4,56,1600]{2,1,0:T(8,128)(2,1)}, u32[]{:S(2)}, u32[]{:S(2)}) collective-permute-start(bf16[4,56,1600]{2,1,0:T(8,128)(2,1)} %get-tuple-element.88.refs_0_), channel_id=1, source_target_pairs={{0,8},{8,0},{16,24},{24,16},{1,9},{9,1},{17,25},{25,17},{2,10},{10... | collective-permute-start | bytes 2150408 | tf_op jit(solution)/shard_map/ppermute | solution.py:28
  192.2 110.5 %reduce-scatter.5.cloned.1.call-start = ((), (), s32[]{:S(2)}) async-start(), calls=%async_computation.8 | async-start | bytes 3833856 | tf_op jit(solution)/shard_map/reduce_scatter | solution.py:708
  193.8 36.0 %collective-permute-start.21 = (bf16[8,56,800]{2,1,0:T(8,128)(2,1)}, bf16[8,56,800]{2,1,0:T(8,128)(2,1)S(1)}, u32[]{:S(2)}, u32[]{:S(2)}) collective-permute-start(bf16[8,56,800]{2,1,0:T(8,128)(2,1)} %constant_dynamic-update-slice_fusion.1.refs_0_), channel_id=1, source_target_pairs={{0,16},{8,24},{16,0},{24,8},{1,17},{9,25},{17,1},{25,9},{2,18},{10... | collective-permute-start | bytes 2150408 | tf_op jit(solution)/shard_map/ppermute | solution.py:28
  259.6 127.3 %reduce-scatter.7.cloned.1.call-start = ((), (), s32[]{:S(2)}) async-start(), calls=%async_computation.9 | async-start | bytes 7454720 | tf_op jit(solution)/shard_map/reduce_scatter | solution.py:811
  283.6 197.5 %reduce-scatter.11.cloned.1.call-start = ((), (), s32[]{:S(2)}) async-start(), calls=%async_computation.11 | async-start | bytes 3833856 | tf_op jit(solution)/shard_map/reduce_scatter | solution.py:708
  349.9 210.6 %reduce-scatter.9.cloned.1.call-start = ((), (), s32[]{:S(2)}) async-start(), calls=%async_computation.10 | async-start | bytes 3833856 | tf_op jit(solution)/shard_map/reduce_scatter | solution.py:708
  383.4 43.9 %collective-permute-start.32 = (bf16[8,56,1600]{2,1,0:T(8,128)(2,1)}, bf16[8,56,1600]{2,1,0:T(8,128)(2,1)}, u32[]{:S(2)}, u32[]{:S(2)}) collective-permute-start(bf16[8,56,1600]{2,1,0:T(8,128)(2,1)} %get-tuple-element.117), channel_id=1, source_target_pairs={{0,8},{8,0},{16,24},{24,16},{1,9},{9,1},{17,25},{25,17},{2,10},{10... | collective-permute-start | bytes 4300808 | tf_op jit(solution)/shard_map/ppermute | solution.py:28
  384.8 67.0 %collective-permute-start.33 = (bf16[8,56,1600]{2,1,0:T(8,128)(2,1)}, bf16[8,56,1600]{2,1,0:T(8,128)(2,1)}, u32[]{:S(2)}, u32[]{:S(2)}) collective-permute-start(bf16[8,56,1600]{2,1,0:T(8,128)(2,1)} %get-tuple-element.118), channel_id=1, source_target_pairs={{0,16},{8,24},{16,0},{24,8},{1,17},{9,25},{17,1},{25,9},{2,18},{10... | collective-permute-start | bytes 4300808 | tf_op jit(solution)/shard_map/ppermute | solution.py:28
  386.4 65.4 %collective-permute-start.34 = (bf16[8,56,1600]{2,1,0:T(8,128)(2,1)}, bf16[8,56,1600]{2,1,0:T(8,128)(2,1)}, u32[]{:S(2)}, u32[]{:S(2)}) collective-permute-start(bf16[8,56,1600]{2,1,0:T(8,128)(2,1)} %get-tuple-element.119), channel_id=1, source_target_pairs={{0,24},{8,16},{16,8},{24,0},{1,25},{9,17},{17,9},{25,1},{2,26},{10... | collective-permute-start | bytes 4300808 | tf_op jit(solution)/shard_map/ppermute | solution.py:28
  473.4 73.9 %collective-permute-start.44 = (bf16[8,56,1600]{2,1,0:T(8,128)(2,1)}, bf16[8,56,1600]{2,1,0:T(8,128)(2,1)}, u32[]{:S(2)}, u32[]{:S(2)}) collective-permute-start(bf16[8,56,1600]{2,1,0:T(8,128)(2,1)} %join_hidden.1.refs_0_), channel_id=1, source_target_pairs={{0,24},{8,16},{16,8},{24,0},{1,25},{9,17},{17,9},{25,1},{2,26},{10... | collective-permute-start | bytes 4300808 | tf_op jit(solution)/shard_map/ppermute | solution.py:28
  474.9 72.4 %collective-permute-start.43 = (bf16[8,56,1600]{2,1,0:T(8,128)(2,1)}, bf16[8,56,1600]{2,1,0:T(8,128)(2,1)}, u32[]{:S(2)}, u32[]{:S(2)}) collective-permute-start(bf16[8,56,1600]{2,1,0:T(8,128)(2,1)} %join_hidden.1.refs_0_), channel_id=1, source_target_pairs={{0,16},{8,24},{16,0},{24,8},{1,17},{9,25},{17,1},{25,9},{2,18},{10... | collective-permute-start | bytes 4300808 | tf_op jit(solution)/shard_map/ppermute | solution.py:28
  476.7 63.7 %collective-permute-start.39 = (bf16[8,56,1600]{2,1,0:T(8,128)(2,1)}, bf16[8,56,1600]{2,1,0:T(8,128)(2,1)}, u32[]{:S(2)}, u32[]{:S(2)}) collective-permute-start(bf16[8,56,1600]{2,1,0:T(8,128)(2,1)} %join_hidden.1.refs_0_), channel_id=1, source_target_pairs={{0,8},{8,0},{16,24},{24,16},{1,9},{9,1},{17,25},{25,17},{2,10},{10... | collective-permute-start | bytes 4300808 | tf_op jit(solution)/shard_map/ppermute | solution.py:28
  476.9 42.7 %collective-permute-start.36 = (bf16[2,56,1600]{2,1,0:T(8,128)(2,1)}, bf16[2,56,1600]{2,1,0:T(8,128)(2,1)}, u32[]{:S(2)}, u32[]{:S(2)}) collective-permute-start(bf16[2,56,1600]{2,1,0:T(8,128)(2,1)} %get-tuple-element.125), channel_id=1, source_target_pairs={{0,4},{1,5},{2,6},{3,7},{4,0},{5,1},{6,2},{7,3},{8,12},{9,13},{10,... | collective-permute-start | bytes 1075208 | tf_op jit(solution)/shard_map/ppermute | solution.py:28
  479.2 40.4 %collective-permute-start.37 = (bf16[2,56,1600]{2,1,0:T(8,128)(2,1)}, bf16[2,56,1600]{2,1,0:T(8,128)(2,1)}, u32[]{:S(2)}, u32[]{:S(2)}) collective-permute-start(bf16[2,56,1600]{2,1,0:T(8,128)(2,1)} %get-tuple-element.126), channel_id=1, source_target_pairs={{0,6},{1,7},{2,4},{3,5},{4,2},{5,3},{6,0},{7,1},{8,14},{9,15},{10,... | collective-permute-start | bytes 1075208 | tf_op jit(solution)/shard_map/ppermute | solution.py:28
  545.6 39.8 %collective-permute-start.41 = (bf16[5,56,1600]{2,1,0:T(8,128)(2,1)}, bf16[5,56,1600]{2,1,0:T(8,128)(2,1)}, u32[]{:S(2)}, u32[]{:S(2)}) collective-permute-start(bf16[5,56,1600]{2,1,0:T(8,128)(2,1)} %join_last.1.refs_0_), channel_id=1, source_target_pairs={{0,16},{8,24},{16,0},{24,8},{1,17},{9,25},{17,1},{25,9},{2,18},{10... | collective-permute-start | bytes 2688008 | tf_op jit(solution)/shard_map/ppermute | solution.py:28
  545.6 39.8 %collective-permute-start.40 = (bf16[5,56,1600]{2,1,0:T(8,128)(2,1)}, bf16[5,56,1600]{2,1,0:T(8,128)(2,1)}, u32[]{:S(2)}, u32[]{:S(2)}) collective-permute-start(bf16[5,56,1600]{2,1,0:T(8,128)(2,1)} %join_last.1.refs_0_), channel_id=1, source_target_pairs={{0,8},{8,0},{16,24},{24,16},{1,9},{9,1},{17,25},{25,17},{2,10},{10... | collective-permute-start | bytes 2688008 | tf_op jit(solution)/shard_map/ppermute | solution.py:28
  (95 other events, 1549.6 us)
Sparse Core Ops, SparseCore 0:
  9.8 52.9 all-gather.4
  65.2 40.7 all-gather.6
  110.0 40.2 all-gather.8
  192.3 40.7 all-gather.10
  259.7 42.8 reduce-scatter.4
  305.6 66.0 reduce-scatter.6
  374.6 55.4 reduce-scatter.10
  472.4 69.1 reduce-scatter.8
